TPU v7x, 512 devices: a whole 4x8x8 slice. The times are simulated.
512 devices in a mesh: row: 8 (over z), col: 16 (over y, core), depth: 4 (over x).
Axes of the slice: x: 4, y: 8, z: 8, core: 2. Of those that a mesh axis runs over, the one named last changes fastest.
Arguments:
- tokens: bfloat16 [4096, 8192], P(('row', 'col'), 'depth'), may hold values from -6 to 6
- gate_weight: bfloat16 [8192, 14336], P(('depth', 'row'), 'col'), may hold values from -0.0625 to 0.0625
- up_weight: bfloat16 [8192, 14336], P(('depth', 'row'), 'col'), may hold values from -0.0625 to 0.0625
- down_weight: bfloat16 [14336, 8192], P(('col', 'row'), 'depth'), may hold values from -0.125 to 0.125
- gate_keep: int32 [64, 112], replicated, may hold values from 0 to 1, as said below
- up_keep: int32 [64, 112], replicated, may hold values from 0 to 1, as said below
- down_keep: int32 [112, 64], replicated, may hold values from 0 to 1, as said below
Outputs:
- mixed: bfloat16 [4096, 8192], P(('row', 'col'), 'depth')
Inputs may be any that keep to these rules, and one draw needn't show every extreme that they name: `gate_keep`: 1 marks a kept block of the gate projection, 0 a dropped one. `up_keep`: 1 marks a kept block of the up projection, 0 a dropped one. `down_keep`: 1 marks a kept block of the down projection, 0 a dropped one.
All inputs are finite; a program needn't handle non-finite values.
Results may differ from a plain program's by a relative error of at most 0.005.
Values may be sent and summed in bfloat16 or wider, within the bound.
No kernel may reach another device: no remote copies, remote signals or barrier semaphores. Data moves between devices by JAX's collectives and lax.ppermute only.
A program may use at most 64 MiB of HBM per device.

v0:
```python
import jax
import jax.numpy as jnp
from jax import lax
from jax.sharding import PartitionSpec as P

BLOCK = 128


def keep_table(keep, row_start, col_start, row_count, col_count):
    keep_bits = keep.astype(jnp.bfloat16)
    row_ids = (row_start + jnp.arange(row_count, dtype=jnp.int32)) // BLOCK
    col_ids = (col_start + jnp.arange(col_count, dtype=jnp.int32)) // BLOCK
    pick_rows = (row_ids[:, None] == jnp.arange(keep.shape[0], dtype=jnp.int32)[None, :]).astype(
        jnp.bfloat16
    )
    pick_cols = (jnp.arange(keep.shape[1], dtype=jnp.int32)[:, None] == col_ids[None, :]).astype(
        jnp.bfloat16
    )
    inner = jnp.dot(keep_bits, pick_cols, preferred_element_type=jnp.float32).astype(jnp.bfloat16)
    return jnp.dot(pick_rows, inner, preferred_element_type=jnp.float32).astype(jnp.bfloat16)


def add_panel(token_block, piece):
    return jnp.dot(token_block, piece, preferred_element_type=jnp.float32)


def on_device(tokens, gate_weight, up_weight, down_weight, gate_keep, up_keep, down_keep):
    depth_pos = lax.axis_index("depth")
    row_pos = lax.axis_index("row")
    column_pos = lax.axis_index("col")
    row_total = lax.axis_size("row")
    feature_rows = gate_weight.shape[0]
    hidden_cols = gate_weight.shape[1]
    feature_start = (depth_pos * row_total + row_pos) * feature_rows
    hidden_start = column_pos * hidden_cols
    gate_masked = gate_weight * keep_table(
        gate_keep, feature_start, hidden_start, feature_rows, hidden_cols
    )
    up_masked = up_weight * keep_table(
        up_keep, feature_start, hidden_start, feature_rows, hidden_cols
    )
    down_rows_count = down_weight.shape[0]
    down_features = down_weight.shape[1]
    down_start = (column_pos * row_total + row_pos) * down_rows_count
    down_masked = down_weight * keep_table(
        down_keep, down_start, depth_pos * down_features, down_rows_count, down_features
    )
    token_block = lax.all_gather(tokens, "col", axis=0, tiled=True)

    def add_one(piece):
        return add_panel(token_block, piece)

    gate = add_one(lax.all_gather(gate_masked, "row", axis=0, tiled=True))
    up = add_one(lax.all_gather(up_masked, "row", axis=0, tiled=True))
    both = jnp.stack((gate, up), 0)
    total = lax.psum(both, "depth")
    hidden = (jax.nn.silu(total[0]) * total[1]).astype(jnp.bfloat16)
    down_block = lax.all_gather(down_masked, "row", axis=0, tiled=True)
    mixed = lax.psum_scatter(
        jnp.dot(hidden, down_block, preferred_element_type=jnp.float32),
        "col",
        scatter_dimension=0,
        tiled=True,
    )
    return mixed.astype(jnp.bfloat16)


def solution(mesh):
    placed = (
        P(("row", "col"), "depth"),
        P(("depth", "row"), "col"),
        P(("depth", "row"), "col"),
        P(("col", "row"), "depth"),
        P(),
        P(),
        P(),
    )
    return jax.shard_map(
        on_device, mesh=mesh, in_specs=placed, out_specs=P(("row", "col"), "depth"), check_vma=False
    )
```

profile of v0, /device:TPU:1, one launch (start us, length us, event | category | flops | bytes accessed | tf_op | source)
XLA Modules:
  0.0 392.8 jit_solution(8674119538249657588)
XLA Ops:
  6.5 0.0 copy-start
  6.5 0.0 copy-start.1
  6.5 0.0 all-gather.7.cloned.1.call-start
  6.5 0.7 all-gather.7.cloned.1.call-update
  7.3 0.0 all-gather.9.cloned.1.call-start
  7.4 2.3 fusion.4
  9.7 0.0 all-gather.9.cloned.1.call-update
  9.7 0.0 all-gather.5.cloned.1.call-start
  9.8 2.3 fusion.3
  12.1 0.0 all-gather.5.cloned.1.call-update
  12.1 0.0 all-gather.11.cloned.1.call-start
  12.2 0.0 copy-done
  12.2 0.0 copy-done.1
  12.2 1.4 fusion
  13.7 0.0 all-gather.11.cloned.1.call-update
  13.7 0.0 all-reduce.2.cloned.1.call-start
  13.7 43.6 %all-gather.7.cloned.1.call-done = bf16[512,2048]{1,0:T(8,128)(2,1)} async-done(((bf16[32,2048]{1,0:T(8,128)(2,1)}), bf16[512,2048]{1,0:T(8,128)(2,1)}) %all-gather.7.cloned.1.call-update) | async-done | bytes 2097168 | tf_op jit(solution)/shard_map/all_gather | solution.py:48
  57.3 53.9 %all-gather.9.cloned.1.call-done = bf16[2048,896]{1,0:T(8,128)(2,1)} async-done(((bf16[256,896]{1,0:T(8,128)(2,1)}), bf16[2048,896]{1,0:T(8,128)(2,1)}) %all-gather.9.cloned.1.call-update) | async-done | bytes 3670032 | tf_op jit(solution)/shard_map/all_gather | solution.py:54
  111.3 4.8 %convolution_bitcast_fusion = f32[1,512,896]{1,2,0:T(8,128)S(1)} fusion(bf16[2048,896]{1,0:T(8,128)(2,1)} %all-gather.9.cloned.1.call-done, bf16[512,2048]{1,0:T(8,128)(2,1)} %all-gather.7.cloned.1.call-done), kind=kOutput, calls=%fused_computation.8 | convolution fusion | flops 1879048192 | bytes 7602176 | tf_op jit(solution)/shard_map/dot_general | solution.py:24
  116.1 48.7 %all-gather.5.cloned.1.call-done = bf16[2048,896]{1,0:T(8,128)(2,1)} async-done(((bf16[256,896]{1,0:T(8,128)(2,1)}), bf16[2048,896]{1,0:T(8,128)(2,1)}) %all-gather.5.cloned.1.call-update) | async-done | bytes 3670032 | tf_op jit(solution)/shard_map/all_gather | solution.py:53
  164.8 4.8 %convolution_bitcast_fusion.1 = f32[1,512,896]{1,2,0:T(8,128)S(1)} fusion(bf16[2048,896]{1,0:T(8,128)(2,1)} %all-gather.5.cloned.1.call-done, bf16[512,2048]{1,0:T(8,128)(2,1)} %all-gather.7.cloned.1.call-done), kind=kOutput, calls=%fused_computation.9 | convolution fusion | flops 1879048192 | bytes 7602176 | tf_op jit(solution)/shard_map/dot_general | solution.py:24
  169.6 2.3 pad_maximum_fusion
  171.9 0.0 all-reduce.2.cloned.1.call-update
  172.0 0.0 reduce-scatter.2.cloned.1.call-start
  172.0 46.2 %all-gather.11.cloned.1.call-done = bf16[896,2048]{1,0:T(8,128)(2,1)} async-done(((bf16[112,2048]{1,0:T(8,128)(2,1)}), bf16[896,2048]{1,0:T(8,128)(2,1)}) %all-gather.11.cloned.1.call-update) | async-done | bytes 3670032 | tf_op jit(solution)/shard_map/all_gather | solution.py:58
  218.2 95.3 %all-reduce.2.cloned.1.call-done = f32[2,512,896]{1,2,0:T(8,128)} async-done(((f32[2,512,896]{1,2,0:T(8,128)}), f32[2,512,896]{1,2,0:T(8,128)}) %all-reduce.2.cloned.1.call-update) | async-done | bytes 3670032 | tf_op jit(solution)/shard_map/psum | solution.py:56
  313.5 7.7 %fusion.5 = f32[512,2048]{1,0:T(8,128)} fusion(bf16[896,2048]{1,0:T(8,128)(2,1)} %all-gather.11.cloned.1.call-done, f32[2,512,896]{1,2,0:T(8,128)} %all-reduce.2.cloned.1.call-done), kind=kOutput, calls=%fused_computation.16 | convolution fusion | flops 1881800704 | bytes 11534336 | tf_op jit(solution)/shard_map/dot_general | solution.py:60
  321.1 0.0 reduce-scatter.2.cloned.1.call-update
  321.2 63.1 %reduce-scatter.2.cloned.1.call-done = f32[32,2048]{1,0:T(8,128)} async-done(((f32[512,2048]{1,0:T(8,128)}), f32[32,2048]{1,0:T(8,128)}) %reduce-scatter.2.cloned.1.call-update) | async-done | bytes 262160 | tf_op jit(solution)/shard_map/reduce_scatter | solution.py:59
  384.3 1.6 convert_element_type.52
  (4 shorter events, 0.0 us)
Async XLA Ops:
  6.5 5.7 %copy-start = (bf16[112,2048]{1,0:T(8,128)(2,1)S(1)}, bf16[112,2048]{1,0:T(8,128)(2,1)}, u32[]{:S(2)}) copy-start(bf16[112,2048]{1,0:T(8,128)(2,1)} %param.10) | copy-start | bytes 1376260
  6.5 5.7 %copy-start.1 = (s32[112,64]{0,1:T(8,128)S(1)}, s32[112,64]{0,1:T(8,128)}, u32[]{:S(2)}) copy-start(s32[112,64]{0,1:T(8,128)} %param.13) | copy-start | bytes 86020
  6.5 50.8 %all-gather.7.cloned.1.call-start = ((), (), s32[]{:S(2)}) async-start(), calls=%async_computation.2 | async-start | bytes 2228224 | tf_op jit(solution)/shard_map/all_gather | solution.py:48
  7.3 104.0 %all-gather.9.cloned.1.call-start = ((), (), s32[]{:S(2)}) async-start(), calls=%async_computation.3 | async-start | bytes 4128768 | tf_op jit(solution)/shard_map/all_gather | solution.py:54
  9.7 155.1 %all-gather.5.cloned.1.call-start = ((), (), s32[]{:S(2)}) async-start(), calls=%async_computation.1 | async-start | bytes 4128768 | tf_op jit(solution)/shard_map/all_gather | solution.py:53
  12.1 206.1 %all-gather.11.cloned.1.call-start = ((), (), s32[]{:S(2)}) async-start(), calls=%async_computation.5 | async-start | bytes 4128768 | tf_op jit(solution)/shard_map/all_gather | solution.py:58
  13.7 299.8 %all-reduce.2.cloned.1.call-start = ((), (), s32[]{:S(2)}) async-start(), calls=%async_computation.4 | async-start | bytes 7340032 | tf_op jit(solution)/shard_map/psum | solution.py:56
  172.0 212.3 %reduce-scatter.2.cloned.1.call-start = ((), (), s32[]{:S(2)}) async-start(), calls=%async_computation.6 | async-start | bytes 4456448 | tf_op jit(solution)/shard_map/reduce_scatter | solution.py:59
Sparse Core Ops, SparseCore 0:
  9.5 47.7 all-gather.6
  59.4 51.8 all-gather.8
  113.3 51.4 all-gather.4
  166.7 51.3 all-gather.10
  220.4 93.0 all-reduce.1
  321.3 62.9 reduce-scatter.1
where the time goes:
time: 394 us; the launch traced here: 393 us
  waiting for transfers between devices  352 us (89%)
  matrix products  23.4 us (6%)
  between operations  13.5 us (3%)
  other arithmetic  4 us (1%)
    psum x1, waiting for transfers between devices, on_device(): total = lax.psum(both, 'depth')  95.3 us
    reduce_scatter x1, waiting for transfers between devices, on_device(): lax.psum_scatter(jnp.dot(hidden, down_block, preferred_element_type=jnp.f...  63.1 us
    all_gather x1, waiting for transfers between devices, on_device(): up = add_one(lax.all_gather(up_masked, 'row', axis=0, tiled=True))  53.9 us
    all_gather x1, waiting for transfers between devices, on_device(): gate = add_one(lax.all_gather(gate_masked, 'row', axis=0, tiled=True))  48.7 us
    all_gather x1, waiting for transfers between devices, on_device(): down_block = lax.all_gather(down_masked, 'row', axis=0, tiled=True)  46.2 us
    all_gather x1, waiting for transfers between devices, on_device(): token_block = lax.all_gather(tokens, 'col', axis=0, tiled=True)  43.6 us
    dot_general x2, matrix products, add_panel(): return jnp.dot(token_block, piece, preferred_element_type=jnp.float32)  9.62 us
  transfers between devices with their start and end apart: 6, of which 6 were waited for; matrix products, arithmetic and copies ran while one was open for 5% of the time, Pallas kernels for 0%

commit v1 on v0

v1 whole, which is shorter than its diff:
```python
import jax
import jax.numpy as jnp
from jax import lax
from jax.experimental import pallas as pl
from jax.experimental.pallas import tpu as pltpu
from jax.sharding import PartitionSpec as P

BLOCK = 128
VMEM = 56 * 1024 * 1024


def ring(size, step):
    return [(i, (i + step) % size) for i in range(size)]


def gather_ring(piece, axis):
    size = lax.axis_size(axis)
    rows = piece.shape[0]
    found = [(0, 0, piece)]
    ahead = behind = piece
    for step in range(1, size // 2):
        ahead = lax.ppermute(ahead, axis, ring(size, 1))
        behind = lax.ppermute(behind, axis, ring(size, -1))
        found += [(-step, 0, ahead), (step, 0, behind)]
    half = rows // 2
    found.append((size // 2, 0, lax.ppermute(ahead[:half], axis, ring(size, 1))))
    found.append((size // 2, half, lax.ppermute(behind[half:], axis, ring(size, -1))))
    return found


def first_kernel(offsets, up_rows, place, gate_keep, up_keep, tokens, gate, *refs):
    up_refs, out = refs[:-1], refs[-1]
    j = pl.program_id(0)
    column = place[1] + j
    gate_parts = []
    for i in range(gate.shape[0] // BLOCK):
        keep = gate_keep[place[0] + i, column].astype(jnp.bfloat16)
        gate_parts.append(gate[pl.ds(i * BLOCK, BLOCK), :] * keep)
    gate_sum = jnp.dot(tokens[...], jnp.concatenate(gate_parts, 0), preferred_element_type=jnp.float32)
    up_sum = None
    for k, ref in enumerate(up_refs):
        first = place[2 + k]
        parts = []
        for i in range(ref.shape[0] // BLOCK):
            keep = up_keep[place[0] + first + i, column].astype(jnp.bfloat16)
            parts.append(ref[pl.ds(i * BLOCK, BLOCK), :] * keep)
        masked = jnp.concatenate(parts, 0) if len(parts) > 1 else parts[0]
        left = tokens[:, pl.ds(pl.multiple_of(first * BLOCK, BLOCK), ref.shape[0])]
        term = jnp.dot(left, masked, preferred_element_type=jnp.float32)
        up_sum = term if up_sum is None else up_sum + term
    shape = out.shape[:1] + out.shape[2:]
    out[:, 0] = gate_sum.reshape(shape).astype(out.dtype)
    out[:, 1] = up_sum.reshape(shape).astype(out.dtype)


def first_product(tokens, gate, up_pieces, gate_keep, up_keep, parts, row, depth, col):
    count, features = tokens.shape
    units = gate.shape[1]
    size = lax.axis_size("row")
    rows = features // size
    place = [depth * (features // BLOCK), col * (units // BLOCK)]
    place += [((row + off) % size) * (rows // BLOCK) + start // BLOCK for off, start, _ in up_pieces]
    place = jnp.stack([jnp.asarray(p, jnp.int32) for p in place])
    arrays = [a for _, _, a in up_pieces]

    def kernel(*refs):
        first_kernel(None, None, *refs)

    return pl.pallas_call(
        kernel,
        out_shape=jax.ShapeDtypeStruct((parts, 2, count // parts, units), jnp.bfloat16),
        grid_spec=pltpu.PrefetchScalarGridSpec(
            num_scalar_prefetch=3,
            grid=(units // BLOCK,),
            in_specs=[
                pl.BlockSpec((count, features), lambda j, *_: (0, 0)),
                pl.BlockSpec((features, BLOCK), lambda j, *_: (0, j)),
            ]
            + [pl.BlockSpec((a.shape[0], BLOCK), lambda j, *_: (0, j)) for a in arrays],
            out_specs=pl.BlockSpec((parts, 2, count // parts, BLOCK), lambda j, *_: (0, 0, 0, j)),
        ),
        compiler_params=pltpu.CompilerParams(vmem_limit_bytes=VMEM),
        cost_estimate=pl.CostEstimate(
            flops=4 * count * features * units, bytes_accessed=12 * 1024 * 1024, transcendentals=0
        ),
        name="first",
    )(place, gate_keep, up_keep, tokens, gate, *arrays)


def second_kernel(place, down_keep, down, *refs):
    hidden_refs, (out_own, out_other, held) = refs[:-3], refs[-3:]
    j = pl.program_id(0)

    @pl.when(j == 0)
    def _():
        for k, ref in enumerate(hidden_refs):
            rows = ref.shape[0]
            held[pl.ds(pl.multiple_of(place[2 + k] * rows, rows), rows), :] = ref[...]

    width = down.shape[1]
    columns = []
    for n in range(width // BLOCK):
        column = place[1] + j * (width // BLOCK) + n
        parts = []
        for i in range(down.shape[0] // BLOCK):
            keep = down_keep[place[0] + i, column].astype(jnp.bfloat16)
            parts.append(down[pl.ds(i * BLOCK, BLOCK), pl.ds(n * BLOCK, BLOCK)] * keep)
        columns.append(jnp.concatenate(parts, 0))
    total = jnp.dot(held[...], jnp.concatenate(columns, 1), preferred_element_type=jnp.float32)
    half = out_own.shape[0]
    out_own[...] = total[:half].astype(out_own.dtype)
    out_other[...] = total[half:].astype(out_other.dtype)


def second_product(hidden_pieces, down, down_keep, depth, col):
    units, features = down.shape
    size = lax.axis_size("depth")
    arrays = [a for _, a in hidden_pieces]
    count = sum(a.shape[0] for a in arrays)
    width = 2 * BLOCK
    place = [col * (units // BLOCK), depth * (features // BLOCK)]
    place += [(depth + off) % size for off, _ in hidden_pieces]
    place = jnp.stack([jnp.asarray(p, jnp.int32) for p in place])
    half = jax.ShapeDtypeStruct((count // 2, features), jnp.float32)
    return pl.pallas_call(
        second_kernel,
        out_shape=(half, half),
        grid_spec=pltpu.PrefetchScalarGridSpec(
            num_scalar_prefetch=2,
            grid=(features // width,),
            in_specs=[pl.BlockSpec((units, width), lambda j, *_: (0, j))]
            + [pl.BlockSpec(a.shape, lambda j, *_: (0, 0)) for a in arrays],
            out_specs=(pl.BlockSpec((count // 2, width), lambda j, *_: (0, j)),) * 2,
            scratch_shapes=[pltpu.VMEM((count, units), jnp.bfloat16)],
        ),
        compiler_params=pltpu.CompilerParams(vmem_limit_bytes=VMEM),
        cost_estimate=pl.CostEstimate(
            flops=2 * count * features * units, bytes_accessed=9 * 1024 * 1024, transcendentals=0
        ),
        name="second",
    )(place, down_keep, down, *arrays)


def on_device(tokens, gate_weight, up_weight, down_weight, gate_keep, up_keep, down_keep):
    depth = lax.axis_index("depth")
    row = lax.axis_index("row")
    col = lax.axis_index("col")
    depth_size, col_size = lax.axis_size("depth"), lax.axis_size("col")
    ways = col_size // 2
    same_core = [list(range(c, col_size, 2)) for c in range(2)]
    swap = [(i, i ^ 1) for i in range(col_size)]

    gate = lax.all_gather(gate_weight, "row", axis=0, tiled=True)
    up_pieces = gather_ring(up_weight, "row")
    down = lax.all_gather(down_weight, "row", axis=0, tiled=True)

    spread = jnp.broadcast_to(tokens[None], (ways,) + tokens.shape)
    own = lax.all_to_all(spread, "col", 0, 0, axis_index_groups=same_core, tiled=True)
    own = own.reshape(-1, tokens.shape[1])
    other = lax.ppermute(own, "col", swap)
    token_block = jnp.concatenate([own, other], 0)

    both = first_product(
        token_block, gate, up_pieces, gate_keep, up_keep, depth_size, row, depth, col
    )
    both = lax.all_to_all(both, "depth", 0, 0, tiled=True)
    total = jnp.sum(both.astype(jnp.float32), 0)
    hidden = (jax.nn.silu(total[0]) * total[1]).astype(jnp.bfloat16)
    pieces = [(0, hidden)] + [
        (k, lax.ppermute(hidden, "depth", ring(depth_size, -k))) for k in range(1, depth_size)
    ]
    mine, theirs = second_product(pieces, down, down_keep, depth, col)
    mine = mine + lax.ppermute(theirs, "col", swap)
    mine = mine.astype(jnp.bfloat16).reshape((ways, -1, mine.shape[1]))
    mixed = lax.all_to_all(mine, "col", 0, 0, axis_index_groups=same_core, tiled=True)
    return jnp.sum(mixed.astype(jnp.float32), 0).astype(jnp.bfloat16)


def solution(mesh):
    placed = (
        P(("row", "col"), "depth"),
        P(("depth", "row"), "col"),
        P(("depth", "row"), "col"),
        P(("col", "row"), "depth"),
        P(),
        P(),
        P(),
    )
    return jax.shard_map(
        on_device, mesh=mesh, in_specs=placed, out_specs=P(("row", "col"), "depth"), check_vma=False
    )
```

time: 394 us -> 225 us (0.57)
  waiting for transfers between devices: 352 us -> 54.5 us
  starting transfers between devices: 0.21 us -> 66.1 us
  blocking collectives: 0 us -> 55.3 us
  Pallas kernels: 0 us -> 24 us
  matrix products: 23.4 us -> 0 us
  local copies, waits for them, and re-layouts: 0.01 us -> 5.6 us
    all_gather x4 -> x2, waiting for transfers between devices: 192 us -> 0.01 us  [the longest x1 0.01 us: on_device(): gate = lax.all_gather(gate_weight, 'row', axis=0, tiled=True)]
    psum x1 -> x0, waiting for transfers between devices: 95.3 us -> none  [on_device(): total = lax.psum(both, 'depth')]
    reduce_scatter x1 -> x0, waiting for transfers between devices: 63.1 us -> none  [on_device(): lax.psum_scatter(jnp.dot(hidden, down_block, preferred_element_type=jnp.f...]
    ppermute x0 -> x13, starting transfers between devices: none -> 58.4 us  [the longest x3 21.9 us: gather_ring(): behind = lax.ppermute(behind, axis, ring(size, -1))]
    all_to_all x0 -> x2, blocking collectives: none -> 55.3 us  [the longest x1 31.6 us: on_device(): lax.all_to_all(mine, 'col', 0, 0, axis_index_groups=same_core, tiled=True)]
    ppermute x0 -> x13, waiting for transfers between devices: none -> 38.5 us  [the longest x3 26 us: gather_ring(): ahead = lax.ppermute(ahead, axis, ring(size, 1))]
    pallas_call x0 -> x2, Pallas kernels: none -> 24 us  [the longest x1 14.1 us: first_product(): pl.pallas_call(kernel, out_shape=jax.ShapeDtypeStruct((parts, 2, count //...]
    dot_general x6 -> x0, matrix products: 23.4 us -> none  [the longest x2 9.62 us: add_panel(): return jnp.dot(token_block, piece, preferred_element_type=jnp.float32)]
  transfers between devices with their start and end apart: 6 -> 16, of which waited for: 6 -> 8; matrix products, arithmetic and copies ran while one was open for 5% -> 3% of each run, Pallas kernels for 0% -> 6%
where the time goes in v1:
time: 225 us; the launch traced here: 224 us
  starting transfers between devices  66.1 us (29%)
  blocking collectives  55.3 us (25%)
  waiting for transfers between devices  54.5 us (24%)
  Pallas kernels  24 us (11%)
  between operations  13.8 us (6%)
  local copies, waits for them, and re-layouts  5.6 us (2%)
  other arithmetic  4.68 us (2%)
    all_to_all x1, blocking collectives, on_device(): lax.all_to_all(mine, 'col', 0, 0, axis_index_groups=same_core, tiled=True)  31.6 us
    ppermute x3, waiting for transfers between devices, gather_ring(): ahead = lax.ppermute(ahead, axis, ring(size, 1))  26 us
    all_to_all x1, blocking collectives, on_device(): both = lax.all_to_all(both, 'depth', 0, 0, tiled=True)  23.7 us
    ppermute x3, starting transfers between devices, gather_ring(): behind = lax.ppermute(behind, axis, ring(size, -1))  21.9 us
    all_to_all x1, waiting for transfers between devices, on_device(): lax.all_to_all(spread, 'col', 0, 0, axis_index_groups=same_core, tiled=True)  14.6 us
    pallas_call x1, Pallas kernels, first_product(): pl.pallas_call(kernel, out_shape=jax.ShapeDtypeStruct((parts, 2, count //...  14.1 us
    ppermute x3, starting transfers between devices, gather_ring(): ahead = lax.ppermute(ahead, axis, ring(size, 1))  9.91 us
    pallas_call x1, Pallas kernels, second_product(): pl.pallas_call(second_kernel, out_shape=(half, half), grid_spec=pltpu.Pre...  9.88 us
  transfers between devices with their start and end apart: 16, of which 8 were waited for; matrix products, arithmetic and copies ran while one was open for 3% of the time, Pallas kernels for 6%

profile of v1, /device:TPU:1, one launch (start us, length us, event | category | flops | bytes accessed | tf_op | source)
XLA Modules:
  0.0 224.0 jit_solution(6369202769250002413)
XLA Ops:
  6.5 0.0 all-gather.5.cloned.1.call-start
  6.5 0.7 all-gather.5.cloned.1.call-update
  7.3 0.0 all-gather.3.cloned.1.call-start
  7.3 0.7 all-gather.3.cloned.1.call-update
  8.0 2.1 broadcast_in_dim.2
  10.1 7.7 %all-to-all-start = ((bf16[8,32,2048]{2,1,0:T(8,128)(2,1)}), bf16[8,32,2048]{2,1,0:T(8,128)(2,1)S(1)}, u32[]{:S(2)}, u32[]{:S(2)}) async-start(bf16[8,32,2048]{2,1,0:T(8,128)(2,1)} %broadcast_in_dim.2), calls=%async_computation | async-start | bytes 2097152 | tf_op jit(solution)/shard_map/all_to_all | solution.py:158
  17.8 4.0 %collective-permute-start.1 = (bf16[256,896]{1,0:T(8,128)(2,1)S(1)}, bf16[256,896]{1,0:T(8,128)(2,1)S(1)}, u32[]{:S(2)}, u32[]{:S(2)}) collective-permute-start(bf16[256,896]{1,0:T(8,128)(2,1)S(1)} %copy-done.4), channel_id=1, source_target_pairs={{0,64},{64,128},{128,192},{192,256},{256,320},{320,384},{384,448},... | collective-permute-start | bytes 1376264 | tf_op jit(solution)/shard_map/ppermute | solution.py:22
  21.8 8.6 %collective-permute-start.2 = (bf16[256,896]{1,0:T(8,128)(2,1)S(1)}, bf16[256,896]{1,0:T(8,128)(2,1)S(1)}, u32[]{:S(2)}, u32[]{:S(2)}) collective-permute-start(bf16[256,896]{1,0:T(8,128)(2,1)S(1)} %copy-done.4), channel_id=1, source_target_pairs={{0,448},{64,0},{128,64},{192,128},{256,192},{320,256},{384,320},{4... | collective-permute-start | bytes 1376264 | tf_op jit(solution)/shard_map/ppermute | solution.py:23
  30.4 14.6 %all-to-all-done = bf16[8,32,2048]{2,1,0:T(8,128)(2,1)S(1)} async-done(((bf16[8,32,2048]{2,1,0:T(8,128)(2,1)}), bf16[8,32,2048]{2,1,0:T(8,128)(2,1)S(1)}, u32[]{:S(2)}, u32[]{:S(2)}) %all-to-all-start) | async-done | bytes 1048608 | tf_op jit(solution)/shard_map/all_to_all | solution.py:158
  45.0 4.4 %collective-permute-start = (bf16[256,2048]{1,0:T(8,128)(2,1)S(1)}, bf16[256,2048]{1,0:T(8,128)(2,1)S(1)}, u32[]{:S(2)}, u32[]{:S(2)}) collective-permute-start(bf16[256,2048]{1,0:T(8,128)(2,1)S(1)} %bitcast.28), channel_id=1, source_target_pairs={{0,4},{4,0},{8,12},{12,8},{16,20},{20,16},{24,28},{28,24},{32,36},... | collective-permute-start | bytes 3145736 | tf_op jit(solution)/shard_map/ppermute | solution.py:160
  49.4 0.0 collective-permute-done.1.refs_6_
  49.4 0.0 copy-start.5
  49.4 4.0 %collective-permute-start.3 = (bf16[256,896]{1,0:T(8,128)(2,1)S(1)}, bf16[256,896]{1,0:T(8,128)(2,1)}, u32[]{:S(2)}, u32[]{:S(2)}) collective-permute-start(bf16[256,896]{1,0:T(8,128)(2,1)S(1)} %collective-permute-done.1.refs_6_), channel_id=1, source_target_pairs={{0,64},{64,128},{128,192},{192,256},{256,320},{320,384},{384,448},... | collective-permute-start | bytes 1376264 | tf_op jit(solution)/shard_map/ppermute | solution.py:22
  53.4 0.0 collective-permute-done.2.refs_7_
  53.4 8.6 %collective-permute-start.4 = (bf16[256,896]{1,0:T(8,128)(2,1)S(1)}, bf16[256,896]{1,0:T(8,128)(2,1)S(1)}, u32[]{:S(2)}, u32[]{:S(2)}) collective-permute-start(bf16[256,896]{1,0:T(8,128)(2,1)S(1)} %collective-permute-done.2.refs_7_), channel_id=1, source_target_pairs={{0,448},{64,0},{128,64},{192,128},{256,192},{320,256},{384,320},{4... | collective-permute-start | bytes 1376264 | tf_op jit(solution)/shard_map/ppermute | solution.py:23
  62.0 18.7 %collective-permute-done.3.refs_8_ = bf16[256,896]{1,0:T(8,128)(2,1)} collective-permute-done((bf16[256,896]{1,0:T(8,128)(2,1)S(1)}, bf16[256,896]{1,0:T(8,128)(2,1)}, u32[]{:S(2)}, u32[]{:S(2)}) %collective-permute-start.3) | collective-permute-done | bytes 458784 | tf_op jit(solution)/shard_map/ppermute | solution.py:22
  80.7 1.9 collective-permute-start.5
  82.6 0.0 collective-permute-done.4.refs_9_
  82.6 4.7 %collective-permute-start.6 = (bf16[256,896]{1,0:T(8,128)(2,1)S(1)}, bf16[256,896]{1,0:T(8,128)(2,1)S(1)}, u32[]{:S(2)}, u32[]{:S(2)}) collective-permute-start(bf16[256,896]{1,0:T(8,128)(2,1)S(1)} %collective-permute-done.4.refs_9_), channel_id=1, source_target_pairs={{0,448},{64,0},{128,64},{192,128},{256,192},{320,256},{384,320},{4... | collective-permute-start | bytes 1376264 | tf_op jit(solution)/shard_map/ppermute | solution.py:23
  87.5 0.7 stack.69.refs_0_
  88.2 7.4 %collective-permute-done.5.refs_10_ = bf16[256,896]{1,0:T(8,128)(2,1)S(1)} collective-permute-done((bf16[256,896]{1,0:T(8,128)(2,1)}, bf16[256,896]{1,0:T(8,128)(2,1)S(1)}, u32[]{:S(2)}, u32[]{:S(2)}) %collective-permute-start.5) | collective-permute-done | bytes 458784 | tf_op jit(solution)/shard_map/ppermute | solution.py:22
  95.6 1.9 collective-permute-start.7
  97.5 0.0 collective-permute-done.6.refs_11_
  97.5 4.6 %collective-permute-start.8 = (bf16[128,896]{1,0:T(8,128)(2,1)S(1)}, bf16[128,896]{1,0:T(8,128)(2,1)}, u32[]{:S(2)}, u32[]{:S(2)}) collective-permute-start(bf16[128,896]{1,0:T(8,128)(2,1)S(1)} %slice.17), channel_id=1, source_target_pairs={{0,448},{64,0},{128,64},{192,128},{256,192},{320,256},{384,320},{4... | collective-permute-start | bytes 688136 | tf_op jit(solution)/shard_map/ppermute | solution.py:27
  102.1 0.0 collective-permute-done
  102.1 1.6 pad_maximum_fusion.refs_3_
  103.7 0.6 collective-permute-done.7.refs_12_
  104.4 0.7 copy-done.11
  105.1 3.9 %collective-permute-done.8.refs_13_ = bf16[128,896]{1,0:T(8,128)(2,1)} collective-permute-done((bf16[128,896]{1,0:T(8,128)(2,1)S(1)}, bf16[128,896]{1,0:T(8,128)(2,1)}, u32[]{:S(2)}, u32[]{:S(2)}) %collective-permute-start.8) | collective-permute-done | bytes 229408 | tf_op jit(solution)/shard_map/ppermute | solution.py:27
  109.0 14.1 %first.1 = bf16[4,2,128,896]{3,2,1,0:T(8,128)(2,1)} custom-call(s32[11]{0:T(128)} %stack.69.refs_0_, s32[64,112]{1,0:T(8,128)} %refs_1_.1, s32[64,112]{1,0:T(8,128)} %refs_2_.1, bf16[512,2048]{1,0:T(8,128)(2,1)} %pad_maximum_fusion.refs_3_, bf16[2048,896]{1,0:T(8,128)(2,1)} %all-gather.5.cloned.1.call-done.refs_4_, bf16[256,896]{1,0:T(8,128)(2,1)} %refs_5_.1, ...), custom_call_target="tpu_custom_call" | custom-call | flops 3758096384 | bytes 12582912 | tf_op jit(solution)/shard_map/first/pallas_call | solution.py:69
  123.1 23.7 %all_to_all.15 = bf16[4,2,128,896]{3,2,1,0:T(8,128)(2,1)S(1)} all-to-all(bf16[4,2,128,896]{3,2,1,0:T(8,128)(2,1)} %first.1), channel_id=1, replica_groups=mesh['row'=8,'col'=16,'depth'=4] {'depth'}, dimensions={0} | all-to-all | bytes 3670016 | tf_op jit(solution)/shard_map/all_to_all | solution.py:166
  146.8 0.3 convert_reduce_fusion
  147.1 0.1 fusion.1.refs_0_
  147.2 2.5 %collective-permute-start.10 = (bf16[128,896]{1,0:T(8,128)(2,1)S(1)}, bf16[128,896]{1,0:T(8,128)(2,1)S(1)}, u32[]{:S(2)}, u32[]{:S(2)}) collective-permute-start(bf16[128,896]{1,0:T(8,128)(2,1)S(1)} %fusion.1.refs_0_), channel_id=1, source_target_pairs={{0,2},{1,3},{2,0},{3,1},{4,6},{5,7},{6,4},{7,5},{8,10},{9,11},{10,... | collective-permute-start | bytes 688136 | tf_op jit(solution)/shard_map/ppermute | solution.py:170
  149.7 2.8 %collective-permute-start.11 = (bf16[128,896]{1,0:T(8,128)(2,1)S(1)}, bf16[128,896]{1,0:T(8,128)(2,1)S(1)}, u32[]{:S(2)}, u32[]{:S(2)}) collective-permute-start(bf16[128,896]{1,0:T(8,128)(2,1)S(1)} %fusion.1.refs_0_), channel_id=1, source_target_pairs={{0,1},{1,2},{2,3},{3,0},{4,5},{5,6},{6,7},{7,4},{8,9},{9,10},{10,1... | collective-permute-start | bytes 688136 | tf_op jit(solution)/shard_map/ppermute | solution.py:170
  152.5 3.7 %collective-permute-start.9 = (bf16[128,896]{1,0:T(8,128)(2,1)S(1)}, bf16[128,896]{1,0:T(8,128)(2,1)S(1)}, u32[]{:S(2)}, u32[]{:S(2)}) collective-permute-start(bf16[128,896]{1,0:T(8,128)(2,1)S(1)} %fusion.1.refs_0_), channel_id=1, source_target_pairs={{0,3},{1,0},{2,1},{3,2},{4,7},{5,4},{6,5},{7,6},{8,11},{9,8},{10,9... | collective-permute-start | bytes 688136 | tf_op jit(solution)/shard_map/ppermute | solution.py:170
  156.3 0.7 copy.8.down_keep
  157.0 0.6 stack.59.place
  157.6 0.0 collective-permute-done.10.refs_2_
  157.6 0.3 collective-permute-done.11.refs_3_
  158.0 3.6 %collective-permute-done.9.refs_1_ = bf16[128,896]{1,0:T(8,128)(2,1)S(1)} collective-permute-done((bf16[128,896]{1,0:T(8,128)(2,1)S(1)}, bf16[128,896]{1,0:T(8,128)(2,1)S(1)}, u32[]{:S(2)}, u32[]{:S(2)}) %collective-permute-start.9) | collective-permute-done | bytes 229408 | tf_op jit(solution)/shard_map/ppermute | solution.py:170
  161.6 0.7 copy-done.10
  162.3 9.9 %second.1 = (f32[256,2048]{1,0:T(8,128)}, f32[256,2048]{1,0:T(8,128)}) custom-call(s32[6]{0:T(128)} %stack.59.place, s32[112,64]{1,0:T(8,128)} %copy.8.down_keep, bf16[896,2048]{1,0:T(8,128)(2,1)} %all-gather.3.cloned.1.call-done.down, bf16[128,896]{1,0:T(8,128)(2,1)} %copy-done, bf16[128,896]{1,0:T(8,128)(2,1)} %copy-done.10, bf16[128,896]{1,0:T(8,128)(2,1)} %copy-done.8, ...), custom_call_target="tpu_custom_call" | custom-call | flops 1879048192 | bytes 9437184 | tf_op jit(solution)/shard_map/second/pallas_call | solution.py:125
  172.2 6.7 %collective-permute-start.12 = (f32[256,2048]{1,0:T(8,128)}, f32[256,2048]{1,0:T(8,128)S(1)}, u32[]{:S(2)}, u32[]{:S(2)}) collective-permute-start(f32[256,2048]{1,0:T(8,128)} %get-tuple-element.8), channel_id=1, source_target_pairs={{0,4},{4,0},{8,12},{12,8},{16,20},{20,16},{24,28},{28,24},{32,36},... | collective-permute-start | bytes 6291464 | tf_op jit(solution)/shard_map/ppermute | solution.py:173
  178.9 4.0 %collective-permute-done.12 = f32[256,2048]{1,0:T(8,128)S(1)} collective-permute-done((f32[256,2048]{1,0:T(8,128)}, f32[256,2048]{1,0:T(8,128)S(1)}, u32[]{:S(2)}, u32[]{:S(2)}) %collective-permute-start.12) | collective-permute-done | bytes 2097184 | tf_op jit(solution)/shard_map/ppermute | solution.py:173
  182.9 1.9 add_convert_fusion
  184.8 31.6 %all_to_all.16 = bf16[8,32,2048]{2,1,0:T(8,128)(2,1)S(1)} all-to-all(bf16[8,32,2048]{2,1,0:T(8,128)(2,1)S(1)} %bitcast.27), channel_id=1, replica_groups={{0,8,16,24,32,40,48,56},{4,12,20,28,36,44,52,60},{1,9,17,25,33,41,49,57..., dimensions={0} | all-to-all | bytes 2097152 | tf_op jit(solution)/shard_map/all_to_all | solution.py:175
  216.4 0.8 reduce_sum.22
  (25 shorter events, 0.1 us)
Async XLA Ops:
  6.5 11.2 %copy-start.4 = (bf16[256,896]{1,0:T(8,128)(2,1)S(1)}, bf16[256,896]{1,0:T(8,128)(2,1)}, u32[]{:S(2)}) copy-start(bf16[256,896]{1,0:T(8,128)(2,1)} %refs_5_.1) | copy-start | bytes 1376260
  6.5 102.4 %all-gather.5.cloned.1.call-start = ((), (), s32[]{:S(2)}) async-start(), calls=%async_computation.4 | async-start | bytes 4128768 | tf_op jit(solution)/shard_map/all_gather | solution.py:153
  7.3 150.4 %all-gather.3.cloned.1.call-start = ((), (), s32[]{:S(2)}) async-start(), calls=%async_computation.3 | async-start | bytes 4128768 | tf_op jit(solution)/shard_map/all_gather | solution.py:155
  10.1 34.8 %all-to-all-start = ((bf16[8,32,2048]{2,1,0:T(8,128)(2,1)}), bf16[8,32,2048]{2,1,0:T(8,128)(2,1)S(1)}, u32[]{:S(2)}, u32[]{:S(2)}) async-start(bf16[8,32,2048]{2,1,0:T(8,128)(2,1)} %broadcast_in_dim.2), calls=%async_computation | async-start | bytes 2097152 | tf_op jit(solution)/shard_map/all_to_all | solution.py:158
  17.8 31.6 %collective-permute-start.1 = (bf16[256,896]{1,0:T(8,128)(2,1)S(1)}, bf16[256,896]{1,0:T(8,128)(2,1)S(1)}, u32[]{:S(2)}, u32[]{:S(2)}) collective-permute-start(bf16[256,896]{1,0:T(8,128)(2,1)S(1)} %copy-done.4), channel_id=1, source_target_pairs={{0,64},{64,128},{128,192},{192,256},{256,320},{320,384},{384,448},... | collective-permute-start | bytes 1376264 | tf_op jit(solution)/shard_map/ppermute | solution.py:22
  21.8 31.6 %collective-permute-start.2 = (bf16[256,896]{1,0:T(8,128)(2,1)S(1)}, bf16[256,896]{1,0:T(8,128)(2,1)S(1)}, u32[]{:S(2)}, u32[]{:S(2)}) collective-permute-start(bf16[256,896]{1,0:T(8,128)(2,1)S(1)} %copy-done.4), channel_id=1, source_target_pairs={{0,448},{64,0},{128,64},{192,128},{256,192},{320,256},{384,320},{4... | collective-permute-start | bytes 1376264 | tf_op jit(solution)/shard_map/ppermute | solution.py:23
  45.0 57.2 %collective-permute-start = (bf16[256,2048]{1,0:T(8,128)(2,1)S(1)}, bf16[256,2048]{1,0:T(8,128)(2,1)S(1)}, u32[]{:S(2)}, u32[]{:S(2)}) collective-permute-start(bf16[256,2048]{1,0:T(8,128)(2,1)S(1)} %bitcast.28), channel_id=1, source_target_pairs={{0,4},{4,0},{8,12},{12,8},{16,20},{20,16},{24,28},{28,24},{32,36},... | collective-permute-start | bytes 3145736 | tf_op jit(solution)/shard_map/ppermute | solution.py:160
  49.4 12.6 %copy-start.5 = (bf16[256,896]{1,0:T(8,128)(2,1)}, bf16[256,896]{1,0:T(8,128)(2,1)S(1)}, u32[]{:S(2)}) copy-start(bf16[256,896]{1,0:T(8,128)(2,1)S(1)} %collective-permute-done.1.refs_6_) | copy-start | bytes 1376260
  49.4 31.3 %collective-permute-start.3 = (bf16[256,896]{1,0:T(8,128)(2,1)S(1)}, bf16[256,896]{1,0:T(8,128)(2,1)}, u32[]{:S(2)}, u32[]{:S(2)}) collective-permute-start(bf16[256,896]{1,0:T(8,128)(2,1)S(1)} %collective-permute-done.1.refs_6_), channel_id=1, source_target_pairs={{0,64},{64,128},{128,192},{192,256},{256,320},{320,384},{384,448},... | collective-permute-start | bytes 1376264 | tf_op jit(solution)/shard_map/ppermute | solution.py:22
  53.4 29.2 %copy-start.6 = (bf16[256,896]{1,0:T(8,128)(2,1)}, bf16[256,896]{1,0:T(8,128)(2,1)S(1)}, u32[]{:S(2)}) copy-start(bf16[256,896]{1,0:T(8,128)(2,1)S(1)} %collective-permute-done.2.refs_7_) | copy-start | bytes 1376260
  53.4 29.2 %collective-permute-start.4 = (bf16[256,896]{1,0:T(8,128)(2,1)S(1)}, bf16[256,896]{1,0:T(8,128)(2,1)S(1)}, u32[]{:S(2)}, u32[]{:S(2)}) collective-permute-start(bf16[256,896]{1,0:T(8,128)(2,1)S(1)} %collective-permute-done.2.refs_7_), channel_id=1, source_target_pairs={{0,448},{64,0},{128,64},{192,128},{256,192},{320,256},{384,320},{4... | collective-permute-start | bytes 1376264 | tf_op jit(solution)/shard_map/ppermute | solution.py:23
  80.7 14.8 %collective-permute-start.5 = (bf16[256,896]{1,0:T(8,128)(2,1)}, bf16[256,896]{1,0:T(8,128)(2,1)S(1)}, u32[]{:S(2)}, u32[]{:S(2)}) collective-permute-start(bf16[256,896]{1,0:T(8,128)(2,1)} %collective-permute-done.3.refs_8_), channel_id=1, source_target_pairs={{0,64},{64,128},{128,192},{192,256},{256,320},{320,384},{384,448},... | collective-permute-start | bytes 1376264 | tf_op jit(solution)/shard_map/ppermute | solution.py:22
  82.6 21.1 %copy-start.7 = (bf16[256,896]{1,0:T(8,128)(2,1)}, bf16[256,896]{1,0:T(8,128)(2,1)S(1)}, u32[]{:S(2)}) copy-start(bf16[256,896]{1,0:T(8,128)(2,1)S(1)} %collective-permute-done.4.refs_9_) | copy-start | bytes 1376260
  82.6 14.9 %collective-permute-start.6 = (bf16[256,896]{1,0:T(8,128)(2,1)S(1)}, bf16[256,896]{1,0:T(8,128)(2,1)S(1)}, u32[]{:S(2)}, u32[]{:S(2)}) collective-permute-start(bf16[256,896]{1,0:T(8,128)(2,1)S(1)} %collective-permute-done.4.refs_9_), channel_id=1, source_target_pairs={{0,448},{64,0},{128,64},{192,128},{256,192},{320,256},{384,320},{4... | collective-permute-start | bytes 1376264 | tf_op jit(solution)/shard_map/ppermute | solution.py:23
  95.5 8.2 %copy-start.1 = (bf16[256,896]{1,0:T(8,128)(2,1)}, bf16[256,896]{1,0:T(8,128)(2,1)S(1)}, u32[]{:S(2)}) copy-start(bf16[256,896]{1,0:T(8,128)(2,1)S(1)} %collective-permute-done.5.refs_10_) | copy-start | bytes 1376260
  95.6 8.8 %collective-permute-start.7 = (bf16[128,896]{1,0:T(8,128)(2,1)S(1)}, bf16[128,896]{1,0:T(8,128)(2,1)S(1)}, u32[]{:S(2)}, u32[]{:S(2)}) collective-permute-start(bf16[128,896]{1,0:T(8,128)(2,1)S(1)} %slice.16), channel_id=1, source_target_pairs={{0,64},{64,128},{128,192},{192,256},{256,320},{320,384},{384,448},... | collective-permute-start | bytes 688136 | tf_op jit(solution)/shard_map/ppermute | solution.py:26
  97.5 6.2 %copy-start.2 = (bf16[256,896]{1,0:T(8,128)(2,1)}, bf16[256,896]{1,0:T(8,128)(2,1)S(1)}, u32[]{:S(2)}) copy-start(bf16[256,896]{1,0:T(8,128)(2,1)S(1)} %collective-permute-done.6.refs_11_) | copy-start | bytes 1376260
  97.5 11.4 %collective-permute-start.8 = (bf16[128,896]{1,0:T(8,128)(2,1)S(1)}, bf16[128,896]{1,0:T(8,128)(2,1)}, u32[]{:S(2)}, u32[]{:S(2)}) collective-permute-start(bf16[128,896]{1,0:T(8,128)(2,1)S(1)} %slice.17), channel_id=1, source_target_pairs={{0,448},{64,0},{128,64},{192,128},{256,192},{320,256},{384,320},{4... | collective-permute-start | bytes 688136 | tf_op jit(solution)/shard_map/ppermute | solution.py:27
  104.4 0.7 copy-start.11
  146.8 9.5 %copy-start.3 = (s32[112,64]{0,1:T(8,128)S(1)}, s32[112,64]{0,1:T(8,128)}, u32[]{:S(2)}) copy-start(s32[112,64]{0,1:T(8,128)} %param.13) | copy-start | bytes 86020
  147.2 14.4 %copy-start = (bf16[128,896]{1,0:T(8,128)(2,1)}, bf16[128,896]{1,0:T(8,128)(2,1)S(1)}, u32[]{:S(2)}) copy-start(bf16[128,896]{1,0:T(8,128)(2,1)S(1)} %fusion.1.refs_0_) | copy-start | bytes 688132
  147.2 10.4 %collective-permute-start.10 = (bf16[128,896]{1,0:T(8,128)(2,1)S(1)}, bf16[128,896]{1,0:T(8,128)(2,1)S(1)}, u32[]{:S(2)}, u32[]{:S(2)}) collective-permute-start(bf16[128,896]{1,0:T(8,128)(2,1)S(1)} %fusion.1.refs_0_), channel_id=1, source_target_pairs={{0,2},{1,3},{2,0},{3,1},{4,6},{5,7},{6,4},{7,5},{8,10},{9,11},{10,... | collective-permute-start | bytes 688136 | tf_op jit(solution)/shard_map/ppermute | solution.py:170
  149.7 8.2 %collective-permute-start.11 = (bf16[128,896]{1,0:T(8,128)(2,1)S(1)}, bf16[128,896]{1,0:T(8,128)(2,1)S(1)}, u32[]{:S(2)}, u32[]{:S(2)}) collective-permute-start(bf16[128,896]{1,0:T(8,128)(2,1)S(1)} %fusion.1.refs_0_), channel_id=1, source_target_pairs={{0,1},{1,2},{2,3},{3,0},{4,5},{5,6},{6,7},{7,4},{8,9},{9,10},{10,1... | collective-permute-start | bytes 688136 | tf_op jit(solution)/shard_map/ppermute | solution.py:170
  152.5 9.0 %collective-permute-start.9 = (bf16[128,896]{1,0:T(8,128)(2,1)S(1)}, bf16[128,896]{1,0:T(8,128)(2,1)S(1)}, u32[]{:S(2)}, u32[]{:S(2)}) collective-permute-start(bf16[128,896]{1,0:T(8,128)(2,1)S(1)} %fusion.1.refs_0_), channel_id=1, source_target_pairs={{0,3},{1,0},{2,1},{3,2},{4,7},{5,4},{6,5},{7,6},{8,11},{9,8},{10,9... | collective-permute-start | bytes 688136 | tf_op jit(solution)/shard_map/ppermute | solution.py:170
  157.6 4.0 %copy-start.8 = (bf16[128,896]{1,0:T(8,128)(2,1)}, bf16[128,896]{1,0:T(8,128)(2,1)S(1)}, u32[]{:S(2)}) copy-start(bf16[128,896]{1,0:T(8,128)(2,1)S(1)} %collective-permute-done.10.refs_2_) | copy-start | bytes 688132
  158.0 3.6 %copy-start.9 = (bf16[128,896]{1,0:T(8,128)(2,1)}, bf16[128,896]{1,0:T(8,128)(2,1)S(1)}, u32[]{:S(2)}) copy-start(bf16[128,896]{1,0:T(8,128)(2,1)S(1)} %collective-permute-done.11.refs_3_) | copy-start | bytes 688132
  161.6 0.7 copy-start.10
  172.2 10.7 %collective-permute-start.12 = (f32[256,2048]{1,0:T(8,128)}, f32[256,2048]{1,0:T(8,128)S(1)}, u32[]{:S(2)}, u32[]{:S(2)}) collective-permute-start(f32[256,2048]{1,0:T(8,128)} %get-tuple-element.8), channel_id=1, source_target_pairs={{0,4},{4,0},{8,12},{12,8},{16,20},{20,16},{24,28},{28,24},{32,36},... | collective-permute-start | bytes 6291464 | tf_op jit(solution)/shard_map/ppermute | solution.py:173
Sparse Core Ops, SparseCore 0:
  9.4 74.5 all-gather.4
  86.1 55.7 all-gather.2

commit v2 on v0

v2 whole, which is shorter than its diff:
```python
import functools
import math

import jax
import jax.numpy as jnp
from jax import lax
from jax.experimental import pallas as pl
from jax.experimental.pallas import tpu as pltpu
from jax.sharding import PartitionSpec as P

BLOCK = 128
VMEM = 58 * 1024 * 1024
SECOND_VMEM = 32 * 1024 * 1024
IN_VMEM = pl.BlockSpec(memory_space=pltpu.VMEM)
ANYWHERE = pl.BlockSpec(memory_space=pl.ANY)
IN_SMEM = pl.BlockSpec(memory_space=pltpu.SMEM)


def ring(size, step):
    return [(i, (i + step) % size) for i in range(size)]


def after(value, *others):
    return lax.optimization_barrier((value,) + others)[0]


def mask_kernel(step, place, keep_ref, weight, out):
    for i in range(weight.shape[0] // step):
        block = lax.div(place[0] + i * step, BLOCK)
        for n in range(weight.shape[1] // BLOCK):
            keep = keep_ref[block, place[1] + n].astype(weight.dtype)
            spot = (pl.ds(i * step, step), pl.ds(n * BLOCK, BLOCK))
            out[spot] = weight[spot] * keep


def masked(weight, keep, first_row, first_block_column):
    step = math.gcd(weight.shape[0], BLOCK)
    place = jnp.stack([first_row, first_block_column]).astype(jnp.int32)
    return pl.pallas_call(
        functools.partial(mask_kernel, step),
        out_shape=jax.ShapeDtypeStruct(weight.shape, weight.dtype),
        in_specs=[IN_SMEM, IN_SMEM, IN_VMEM],
        out_specs=IN_VMEM,
        compiler_params=pltpu.CompilerParams(vmem_limit_bytes=VMEM),
        cost_estimate=pl.CostEstimate(flops=weight.size, bytes_accessed=4 * weight.size, transcendentals=0),
        name="mask",
    )(place, keep, weight)


def product_kernel(count, added, place, gate_keep, up_keep, tokens, *refs):
    so_far = refs[0] if added else None
    pieces = refs[1 if added else 0 : -3]
    out, held, sems = refs[-3:]
    units = pieces[0].shape[1]
    copies, row = [], 0
    for k in range(count):
        rows = pieces[k].shape[0]
        for side in range(2):
            spot = (pl.ds(row, rows), pl.ds(side * units, units))
            copy = pltpu.make_async_copy(pieces[side * count + k], held.at[spot], sems.at[2 * k + side])
            copy.start()
            copies.append((row, rows, copy))
        row += rows
    firsts = [place[2 + k] for k in range(count)]
    spots = [pl.ds(pl.multiple_of(firsts[k], BLOCK), copies[2 * k][1]) for k in range(count)]
    for k, (row, rows, copy) in enumerate(copies):
        copy.wait()
        keep, left = ((gate_keep, 0), (up_keep, units))[k % 2]
        block_row = place[0] + lax.div(firsts[k // 2], BLOCK)
        for i in range(rows // BLOCK):
            for n in range(units // BLOCK):
                spot = (pl.ds(row + i * BLOCK, BLOCK), pl.ds(left + n * BLOCK, BLOCK))
                held[spot] = held[spot] * keep[block_row + i, place[1] + n].astype(held.dtype)
    half, width = tokens.shape[0] // 2, 4 * BLOCK
    for start in range(0, 2 * units, width):
        columns = pl.ds(start, min(width, 2 * units - start))
        for t in range(2):
            part = pl.ds(t * half, half)
            left = [tokens[part, spot] for spot in spots]
            left = jnp.concatenate(left, 1) if count > 1 else left[0]
            total = jnp.dot(left, held[:, columns], preferred_element_type=jnp.float32)
            if added:
                total = total + so_far[part, columns]
            out[part, columns] = total.astype(out.dtype)


def product(tokens, gates, ups, gate_keep, up_keep, so_far, dtype, name):
    row, size = lax.axis_index("row"), lax.axis_size("row")
    count, features = tokens.shape
    units = ups[0][2].shape[1]
    rows = sum(a.shape[0] for _, _, a in ups)
    place = [lax.axis_index("depth") * (features // BLOCK), lax.axis_index("col") * (units // BLOCK)]
    place += [lax.rem(row + off + size, size) * (features // size) + start for off, start, _ in ups]
    arrays = [a for _, _, a in gates] + [a for _, _, a in ups]
    added = [] if so_far is None else [so_far]
    return pl.pallas_call(
        functools.partial(product_kernel, len(ups), so_far is not None),
        out_shape=jax.ShapeDtypeStruct((count, 2 * units), dtype),
        in_specs=[IN_SMEM] * 3 + [IN_VMEM] * (1 + len(added)) + [ANYWHERE] * len(arrays),
        out_specs=IN_VMEM,
        scratch_shapes=[
            pltpu.VMEM((rows, 2 * units), jnp.bfloat16),
            pltpu.SemaphoreType.DMA((len(arrays),)),
        ],
        compiler_params=pltpu.CompilerParams(vmem_limit_bytes=VMEM),
        cost_estimate=pl.CostEstimate(
            flops=4 * count * rows * units, bytes_accessed=4 * rows * units, transcendentals=0
        ),
        name=name,
    )(jnp.stack(place).astype(jnp.int32), gate_keep, up_keep, tokens, *added, *arrays)


def second_kernel(share, place, hidden, down, out_own, out_other, held, weight, sems):
    width = down.shape[1] // sems.shape[0]
    copies = []
    for j in range(sems.shape[0]):
        columns = pl.ds(j * width, width)
        copies.append(pltpu.make_async_copy(down.at[:, columns], weight.at[:, columns], sems.at[j]))
        copies[j].start()
    half = out_own.shape[0]
    for y in range(half // share):
        for core in range(2):
            spot = lax.rem(core + place[0], 2) * half + y * share
            held[pl.ds(pl.multiple_of(spot, share), share), :] = hidden[pl.ds((2 * y + core) * share, share), :]
    for j, copy in enumerate(copies):
        copy.wait()
        columns = pl.ds(j * width, width)
        for t, out in enumerate((out_own, out_other)):
            out[:, columns] = jnp.dot(
                held[pl.ds(t * half, half), :], weight[:, columns], preferred_element_type=jnp.float32
            )


def second_product(hidden, down, share):
    count = hidden.shape[0]
    units, features = down.shape
    core = lax.rem(lax.axis_index("col"), 2).reshape((1,)).astype(jnp.int32)
    half = jax.ShapeDtypeStruct((count // 2, features), jnp.float32)
    return pl.pallas_call(
        functools.partial(second_kernel, share),
        out_shape=(half, half),
        in_specs=[IN_SMEM, IN_VMEM, ANYWHERE],
        out_specs=(IN_VMEM, IN_VMEM),
        scratch_shapes=[
            pltpu.VMEM((count, units), jnp.bfloat16),
            pltpu.VMEM((units, features), jnp.bfloat16),
            pltpu.SemaphoreType.DMA((4,)),
        ],
        compiler_params=pltpu.CompilerParams(vmem_limit_bytes=SECOND_VMEM),
        cost_estimate=pl.CostEstimate(
            flops=2 * count * features * units, bytes_accessed=9 * 1024 * 1024, transcendentals=0
        ),
        name="second",
    )(core, hidden, down)


def gather_ring(piece, axis, way):
    size = lax.axis_size(axis)
    found = [(0, 0, piece)]
    ahead = behind = piece
    for step in range(1, size // 2):
        ahead = lax.ppermute(ahead, axis, ring(size, 1))
        behind = lax.ppermute(behind, axis, ring(size, -1))
        found += [(-step, 0, ahead), (step, 0, behind)]
    found.append((size // 2, 0, lax.ppermute(ahead if way > 0 else behind, axis, ring(size, way))))
    return found


def on_device(tokens, gate_weight, up_weight, down_weight, gate_keep, up_keep, down_keep):
    depth = lax.axis_index("depth")
    row = lax.axis_index("row")
    col = lax.axis_index("col")
    depth_size, row_size, col_size = lax.axis_size("depth"), lax.axis_size("row"), lax.axis_size("col")
    same_core = [list(range(c, col_size, 2)) for c in range(2)]
    swap = [(i, i ^ 1) for i in range(col_size)]
    units = gate_weight.shape[1]

    token_block = lax.all_gather(tokens, "col", axis=0, tiled=True)
    gates, ups = gather_ring(gate_weight, "row", 1), gather_ring(up_weight, "row", -1)
    down_row = (col * row_size + row) * down_weight.shape[0]
    down = masked(down_weight, down_keep, down_row, depth * (down_weight.shape[1] // BLOCK))
    down = after(down, *[a for _, _, a in gates[-3:-1] + ups[-3:-1]])
    down = lax.all_gather(down, "row", axis=0, tiled=True)

    so_far = product(token_block, gates[:-1], ups[:-1], gate_keep, up_keep, None, jnp.float32, "most")
    gate, up, so_far = lax.optimization_barrier((gates[-1][2], ups[-1][2], so_far))
    both = product(
        token_block,
        [gates[-1][:2] + (gate,)],
        [ups[-1][:2] + (up,)],
        gate_keep,
        up_keep,
        so_far,
        jnp.bfloat16,
        "last",
    )
    both = both.reshape((depth_size, -1, both.shape[1]))
    both = lax.all_to_all(both, "depth", 0, 0, tiled=True)
    both = jnp.sum(both.astype(jnp.float32), 0)
    hidden = (jax.nn.silu(both[:, :units]) * both[:, units:]).astype(jnp.bfloat16)
    hidden = lax.all_gather(hidden, "depth", axis=0, tiled=True)

    mine, theirs = second_product(hidden, down, tokens.shape[0])
    mine = mine + lax.ppermute(theirs, "col", swap)
    mine = mine.astype(jnp.bfloat16).reshape((col_size // 2,) + tokens.shape)
    mixed = lax.all_to_all(mine, "col", 0, 0, axis_index_groups=same_core, tiled=True)
    return jnp.sum(mixed.astype(jnp.float32), 0).astype(jnp.bfloat16)


def solution(mesh):
    placed = (
        P(("row", "col"), "depth"),
        P(("depth", "row"), "col"),
        P(("depth", "row"), "col"),
        P(("col", "row"), "depth"),
        P(),
        P(),
        P(),
    )
    return jax.shard_map(
        on_device, mesh=mesh, in_specs=placed, out_specs=P(("row", "col"), "depth"), check_vma=False
    )
```

time: 394 us -> 203 us (0.52)
  waiting for transfers between devices: 352 us -> 43 us
  starting transfers between devices: 0.21 us -> 68.4 us
  blocking collectives: 0 us -> 47.1 us
  matrix products: 23.4 us -> 0 us
  Pallas kernels: 0 us -> 22.8 us
  local copies, waits for them, and re-layouts: 0.01 us -> 4.14 us
    all_gather x3 -> x1, waiting for transfers between devices: 149 us -> 0.01 us  [on_device(): down = lax.all_gather(down, 'row', axis=0, tiled=True)]
    psum x1 -> x0, waiting for transfers between devices: 95.3 us -> none  [on_device(): total = lax.psum(both, 'depth')]
    ppermute x0 -> x15, starting transfers between devices: none -> 64.3 us  [the longest x6 32.3 us: gather_ring(): behind = lax.ppermute(behind, axis, ring(size, -1))]
    reduce_scatter x1 -> x0, waiting for transfers between devices: 63.1 us -> none  [on_device(): lax.psum_scatter(jnp.dot(hidden, down_block, preferred_element_type=jnp.f...]
    all_gather x1, waiting for transfers between devices: 43.6 us -> 0.01 us  [on_device(): token_block = lax.all_gather(tokens, 'col', axis=0, tiled=True)]
    all_to_all x0 -> x1, blocking collectives: none -> 34.7 us  [on_device(): lax.all_to_all(mine, 'col', 0, 0, axis_index_groups=same_core, tiled=True)]
    ppermute x0 -> x15, waiting for transfers between devices: none -> 23.8 us  [the longest x6 16.2 us: gather_ring(): behind = lax.ppermute(behind, axis, ring(size, -1))]
    dot_general x6 -> x0, matrix products: 23.4 us -> none  [the longest x2 9.62 us: add_panel(): return jnp.dot(token_block, piece, preferred_element_type=jnp.float32)]
  transfers between devices with their start and end apart: 6 -> 18, of which waited for: 6 -> 7; matrix products, arithmetic and copies ran while one was open for 5% -> 2% of each run, Pallas kernels for 0% -> 9%
where the time goes in v2:
time: 203 us; the launch traced here: 202 us
  starting transfers between devices  68.4 us (34%)
  blocking collectives  47.1 us (23%)
  waiting for transfers between devices  43 us (21%)
  Pallas kernels  22.8 us (11%)
  between operations  13.7 us (7%)
  local copies, waits for them, and re-layouts  4.14 us (2%)
  other arithmetic  2.73 us (1%)
    all_to_all x1, blocking collectives, on_device(): lax.all_to_all(mine, 'col', 0, 0, axis_index_groups=same_core, tiled=True)  34.7 us
    ppermute x6, starting transfers between devices, gather_ring(): behind = lax.ppermute(behind, axis, ring(size, -1))  32.3 us
    all_to_all x1, waiting for transfers between devices, on_device(): both = lax.all_to_all(both, 'depth', 0, 0, tiled=True)  18.5 us
    ppermute x6, waiting for transfers between devices, gather_ring(): behind = lax.ppermute(behind, axis, ring(size, -1))  16.2 us
    pallas_call x2, Pallas kernels, product(): pl.pallas_call(functools.partial(product_kernel, len(ups), so_far is not...  16 us
    ppermute x6, starting transfers between devices, gather_ring(): ahead = lax.ppermute(ahead, axis, ring(size, 1))  14.4 us
    all_gather x1, blocking collectives, on_device(): hidden = lax.all_gather(hidden, 'depth', axis=0, tiled=True)  12.4 us
    ppermute x1, starting transfers between devices, on_device(): mine = mine + lax.ppermute(theirs, 'col', swap)  10.2 us
  transfers between devices with their start and end apart: 18, of which 7 were waited for; matrix products, arithmetic and copies ran while one was open for 2% of the time, Pallas kernels for 9%

profile of v2, /device:TPU:1, one launch (start us, length us, event | category | flops | bytes accessed | tf_op | source)
XLA Modules:
  0.0 201.8 jit_solution(1176263431949982402)
XLA Ops:
  6.5 0.7 all-gather.3.cloned.1.call-update
  7.3 0.0 all-gather.5.cloned.1.call-start
  7.3 4.8 %collective-permute-start = (bf16[256,896]{1,0:T(8,128)(2,1)}, bf16[256,896]{1,0:T(8,128)(2,1)S(1)}, u32[]{:S(2)}, u32[]{:S(2)}) collective-permute-start(bf16[256,896]{1,0:T(8,128)(2,1)} %refs_0_.1), channel_id=1, source_target_pairs={{0,64},{64,128},{128,192},{192,256},{256,320},{320,384},{384,448},... | collective-permute-start | bytes 1376264 | tf_op jit(solution)/shard_map/ppermute | solution.py:162
  12.1 8.6 %collective-permute-start.4 = (bf16[256,896]{1,0:T(8,128)(2,1)}, bf16[256,896]{1,0:T(8,128)(2,1)S(1)}, u32[]{:S(2)}, u32[]{:S(2)}) collective-permute-start(bf16[256,896]{1,0:T(8,128)(2,1)} %refs_7_.1), channel_id=1, source_target_pairs={{0,448},{64,0},{128,64},{192,128},{256,192},{320,256},{384,320},{4... | collective-permute-start | bytes 1376264 | tf_op jit(solution)/shard_map/ppermute | solution.py:163
  20.7 3.4 %collective-permute-start.8 = (bf16[256,896]{1,0:T(8,128)(2,1)}, bf16[256,896]{1,0:T(8,128)(2,1)S(1)}, u32[]{:S(2)}, u32[]{:S(2)}) collective-permute-start(bf16[256,896]{1,0:T(8,128)(2,1)} %refs_0_.1), channel_id=1, source_target_pairs={{0,448},{64,0},{128,64},{192,128},{256,192},{320,256},{384,320},{4... | collective-permute-start | bytes 1376264 | tf_op jit(solution)/shard_map/ppermute | solution.py:163
  24.1 1.9 collective-permute-start.11
  26.0 3.2 %collective-permute-done.refs_1_ = bf16[256,896]{1,0:T(8,128)(2,1)S(1)} collective-permute-done((bf16[256,896]{1,0:T(8,128)(2,1)}, bf16[256,896]{1,0:T(8,128)(2,1)S(1)}, u32[]{:S(2)}, u32[]{:S(2)}) %collective-permute-start) | collective-permute-done | bytes 458784 | tf_op jit(solution)/shard_map/ppermute | solution.py:162
  29.3 1.9 collective-permute-start.1
  31.2 0.0 collective-permute-done.4.refs_9_
  31.2 4.6 %collective-permute-start.5 = (bf16[256,896]{1,0:T(8,128)(2,1)S(1)}, bf16[256,896]{1,0:T(8,128)(2,1)S(1)}, u32[]{:S(2)}, u32[]{:S(2)}) collective-permute-start(bf16[256,896]{1,0:T(8,128)(2,1)S(1)} %collective-permute-done.4.refs_9_), channel_id=1, source_target_pairs={{0,448},{64,0},{128,64},{192,128},{256,192},{320,256},{384,320},{4... | collective-permute-start | bytes 1376264 | tf_op jit(solution)/shard_map/ppermute | solution.py:163
  35.8 4.3 %collective-permute-done.8.refs_2_ = bf16[256,896]{1,0:T(8,128)(2,1)S(1)} collective-permute-done((bf16[256,896]{1,0:T(8,128)(2,1)}, bf16[256,896]{1,0:T(8,128)(2,1)S(1)}, u32[]{:S(2)}, u32[]{:S(2)}) %collective-permute-start.8) | collective-permute-done | bytes 458784 | tf_op jit(solution)/shard_map/ppermute | solution.py:163
  40.1 5.2 %collective-permute-start.9 = (bf16[256,896]{1,0:T(8,128)(2,1)S(1)}, bf16[256,896]{1,0:T(8,128)(2,1)S(1)}, u32[]{:S(2)}, u32[]{:S(2)}) collective-permute-start(bf16[256,896]{1,0:T(8,128)(2,1)S(1)} %collective-permute-done.8.refs_2_), channel_id=1, source_target_pairs={{0,448},{64,0},{128,64},{192,128},{256,192},{320,256},{384,320},{4... | collective-permute-start | bytes 1376264 | tf_op jit(solution)/shard_map/ppermute | solution.py:163
  45.3 0.0 collective-permute-done.11.refs_8_
  45.3 1.9 collective-permute-start.12
  47.2 0.6 collective-permute-done.1.refs_3_
  47.9 1.9 collective-permute-start.2
  49.8 0.0 collective-permute-done.5.refs_11_
  49.8 5.3 %collective-permute-start.6 = (bf16[256,896]{1,0:T(8,128)(2,1)S(1)}, bf16[256,896]{1,0:T(8,128)(2,1)}, u32[]{:S(2)}, u32[]{:S(2)}) collective-permute-start(bf16[256,896]{1,0:T(8,128)(2,1)S(1)} %collective-permute-done.5.refs_11_), channel_id=1, source_target_pairs={{0,448},{64,0},{128,64},{192,128},{256,192},{320,256},{384,320},{4... | collective-permute-start | bytes 1376264 | tf_op jit(solution)/shard_map/ppermute | solution.py:163
  55.1 4.5 %collective-permute-done.9.refs_4_ = bf16[256,896]{1,0:T(8,128)(2,1)S(1)} collective-permute-done((bf16[256,896]{1,0:T(8,128)(2,1)S(1)}, bf16[256,896]{1,0:T(8,128)(2,1)S(1)}, u32[]{:S(2)}, u32[]{:S(2)}) %collective-permute-start.9) | collective-permute-done | bytes 458784 | tf_op jit(solution)/shard_map/ppermute | solution.py:163
  59.6 5.3 %collective-permute-start.10 = (bf16[256,896]{1,0:T(8,128)(2,1)S(1)}, bf16[256,896]{1,0:T(8,128)(2,1)}, u32[]{:S(2)}, u32[]{:S(2)}) collective-permute-start(bf16[256,896]{1,0:T(8,128)(2,1)S(1)} %collective-permute-done.9.refs_4_), channel_id=1, source_target_pairs={{0,448},{64,0},{128,64},{192,128},{256,192},{320,256},{384,320},{4... | collective-permute-start | bytes 1376264 | tf_op jit(solution)/shard_map/ppermute | solution.py:163
  64.9 0.0 collective-permute-done.12.refs_10_
  64.9 1.9 collective-permute-start.13
  66.9 1.5 copy.8.keep_ref
  68.4 0.6 pad_add_fusion.1.place
  69.0 2.9 %mask.1 = bf16[112,2048]{1,0:T(8,128)(2,1)} custom-call(s32[2]{0:T(128)} %pad_add_fusion.1.place, s32[112,64]{1,0:T(8,128)} %copy.8.keep_ref, bf16[112,2048]{1,0:T(8,128)(2,1)} %weight.1), custom_call_target="tpu_custom_call" | custom-call | flops 229376 | bytes 917504 | tf_op jit(solution)/shard_map/mask/pallas_call | solution.py:39
  71.9 0.0 collective-permute-done.2.refs_5_
  71.9 0.0 collective-permute-done.6.refs_13_
  71.9 7.4 %collective-permute-done.10.refs_6_ = bf16[256,896]{1,0:T(8,128)(2,1)} collective-permute-done((bf16[256,896]{1,0:T(8,128)(2,1)S(1)}, bf16[256,896]{1,0:T(8,128)(2,1)}, u32[]{:S(2)}, u32[]{:S(2)}) %collective-permute-start.10) | collective-permute-done | bytes 458784 | tf_op jit(solution)/shard_map/ppermute | solution.py:163
  79.3 0.0 collective-permute-done.13.refs_12_
  79.3 0.0 all-gather.5.cloned.1.call-update
  79.3 1.9 collective-permute-start.3
  81.2 5.4 %collective-permute-start.7 = (bf16[256,896]{1,0:T(8,128)(2,1)}, bf16[256,896]{1,0:T(8,128)(2,1)}, u32[]{:S(2)}, u32[]{:S(2)}) collective-permute-start(bf16[256,896]{1,0:T(8,128)(2,1)} %collective-permute-done.6.refs_13_), channel_id=1, source_target_pairs={{0,448},{64,0},{128,64},{192,128},{256,192},{320,256},{384,320},{4... | collective-permute-start | bytes 1376264 | tf_op jit(solution)/shard_map/ppermute | solution.py:165
  86.7 0.6 stack.56.place
  87.3 0.6 pad_add_fusion.place
  87.9 10.2 %most.1.refs_0_ = f32[512,1792]{1,0:T(8,128)} custom-call(s32[9]{0:T(128)} %stack.56.place, s32[64,112]{1,0:T(8,128)} %gate_keep.3, s32[64,112]{1,0:T(8,128)} %up_keep.3, bf16[512,2048]{1,0:T(8,128)(2,1)} %all-gather.3.cloned.1.call-done.tokens, bf16[256,896]{1,0:T(8,128)(2,1)} %refs_0_.1, bf16[256,896]{1,0:T(8,128)(2,1)} %copy-done.1, ...), custom_call_target="tpu_custom_call" | custom-call | flops 3288334336 | bytes 6422528 | tf_op jit(solution)/shard_map/most/pallas_call | solution.py:96
  98.2 5.8 %last.1 = bf16[512,1792]{1,0:T(8,128)(2,1)} custom-call(s32[3]{0:T(128)} %pad_add_fusion.place, s32[64,112]{1,0:T(8,128)} %gate_keep.3, s32[64,112]{1,0:T(8,128)} %up_keep.3, bf16[512,2048]{1,0:T(8,128)(2,1)} %all-gather.3.cloned.1.call-done.tokens, f32[512,1792]{1,0:T(8,128)} %most.1.refs_0_, bf16[256,896]{1,0:T(8,128)(2,1)} %collective-permute-done.3.refs_1_, ...), custom_call_target="tpu_custom_call" | custom-call | flops 469762048 | bytes 917504 | tf_op jit(solution)/shard_map/last/pallas_call | solution.py:96
  103.9 4.0 %all-to-all-start = ((bf16[4,128,1792]{2,1,0:T(8,128)(2,1)}), bf16[4,128,1792]{2,1,0:T(8,128)(2,1)S(1)}, u32[]{:S(2)}, u32[]{:S(2)}) async-start(bf16[4,128,1792]{2,1,0:T(8,128)(2,1)} %bitcast.14), calls=%async_computation | async-start | bytes 3670016 | tf_op jit(solution)/shard_map/all_to_all | solution.py:198
  108.0 18.5 %all-to-all-done = bf16[4,128,1792]{2,1,0:T(8,128)(2,1)S(1)} async-done(((bf16[4,128,1792]{2,1,0:T(8,128)(2,1)}), bf16[4,128,1792]{2,1,0:T(8,128)(2,1)S(1)}, u32[]{:S(2)}, u32[]{:S(2)}) %all-to-all-start) | async-done | bytes 1835040 | tf_op jit(solution)/shard_map/all_to_all | solution.py:198
  126.4 0.3 convert_reduce_fusion
  126.7 0.1 fusion
  126.8 12.4 %all_gather.10.hidden = bf16[512,896]{1,0:T(8,128)(2,1)S(1)} all-gather(bf16[128,896]{1,0:T(8,128)(2,1)S(1)} %fusion), channel_id=1, replica_groups=mesh['row'=8,'col'=16,'depth'=4] {'depth'}, dimensions={0}, use_global_device_ids=true | all-gather | bytes 1146880 | tf_op jit(solution)/shard_map/all_gather | solution.py:201
  139.2 2.0 %copy-done = bf16[896,2048]{1,0:T(8,128)(2,1)S(1)} copy-done((bf16[896,2048]{1,0:T(8,128)(2,1)S(1)}, bf16[896,2048]{1,0:T(8,128)(2,1)}, u32[]{:S(2)}) %copy-start) | copy-done | bytes 3670040
  141.2 3.9 %second.1 = (f32[256,2048]{1,0:T(8,128)S(1)}, f32[256,2048]{1,0:T(8,128)S(1)}) custom-call(s32[1]{0:T(128)} %bitcast.place, bf16[512,896]{1,0:T(8,128)(2,1)S(1)} %all_gather.10.hidden, bf16[896,2048]{1,0:T(8,128)(2,1)S(1)} %copy-done), custom_call_target="tpu_custom_call" | custom-call | flops 1879048192 | bytes 9437184 | tf_op jit(solution)/shard_map/second/pallas_call | solution.py:139
  145.1 10.2 %collective-permute-start.14 = (f32[256,2048]{1,0:T(8,128)S(1)}, f32[256,2048]{1,0:T(8,128)S(1)}, u32[]{:S(2)}, u32[]{:S(2)}) collective-permute-start(f32[256,2048]{1,0:T(8,128)S(1)} %get-tuple-element.16), channel_id=1, source_target_pairs={{0,4},{4,0},{8,12},{12,8},{16,20},{20,16},{24,28},{28,24},{32,36},... | collective-permute-start | bytes 6291464 | tf_op jit(solution)/shard_map/ppermute | solution.py:204
  155.3 3.8 %collective-permute-done.14 = f32[256,2048]{1,0:T(8,128)S(1)} collective-permute-done((f32[256,2048]{1,0:T(8,128)S(1)}, f32[256,2048]{1,0:T(8,128)S(1)}, u32[]{:S(2)}, u32[]{:S(2)}) %collective-permute-start.14) | collective-permute-done | bytes 2097184 | tf_op jit(solution)/shard_map/ppermute | solution.py:204
  159.1 0.3 add_convert_fusion
  159.4 34.7 %all_to_all.10 = bf16[8,32,2048]{2,1,0:T(8,128)(2,1)S(1)} all-to-all(bf16[8,32,2048]{2,1,0:T(8,128)(2,1)S(1)} %bitcast.15), channel_id=1, replica_groups={{0,8,16,24,32,40,48,56},{4,12,20,28,36,44,52,60},{1,9,17,25,33,41,49,57..., dimensions={0} | all-to-all | bytes 2097152 | tf_op jit(solution)/shard_map/all_to_all | solution.py:206
  194.1 0.8 reduce_sum.22
  (20 shorter events, 0.0 us)
Async XLA Ops:
  6.5 81.3 %all-gather.3.cloned.1.call-start = ((), (), s32[]{:S(2)}) async-start(), calls=%async_computation.2 | async-start | bytes 2228224 | tf_op jit(solution)/shard_map/all_gather | solution.py:178
  7.3 131.9 %all-gather.5.cloned.1.call-start = ((), (), s32[]{:S(2)}) async-start(), calls=%async_computation.3 | async-start | bytes 4128768 | tf_op jit(solution)/shard_map/all_gather | solution.py:183
  7.3 21.9 %collective-permute-start = (bf16[256,896]{1,0:T(8,128)(2,1)}, bf16[256,896]{1,0:T(8,128)(2,1)S(1)}, u32[]{:S(2)}, u32[]{:S(2)}) collective-permute-start(bf16[256,896]{1,0:T(8,128)(2,1)} %refs_0_.1), channel_id=1, source_target_pairs={{0,64},{64,128},{128,192},{192,256},{256,320},{320,384},{384,448},... | collective-permute-start | bytes 1376264 | tf_op jit(solution)/shard_map/ppermute | solution.py:162
  12.1 19.0 %collective-permute-start.4 = (bf16[256,896]{1,0:T(8,128)(2,1)}, bf16[256,896]{1,0:T(8,128)(2,1)S(1)}, u32[]{:S(2)}, u32[]{:S(2)}) collective-permute-start(bf16[256,896]{1,0:T(8,128)(2,1)} %refs_7_.1), channel_id=1, source_target_pairs={{0,448},{64,0},{128,64},{192,128},{256,192},{320,256},{384,320},{4... | collective-permute-start | bytes 1376264 | tf_op jit(solution)/shard_map/ppermute | solution.py:163
  20.7 19.3 %collective-permute-start.8 = (bf16[256,896]{1,0:T(8,128)(2,1)}, bf16[256,896]{1,0:T(8,128)(2,1)S(1)}, u32[]{:S(2)}, u32[]{:S(2)}) collective-permute-start(bf16[256,896]{1,0:T(8,128)(2,1)} %refs_0_.1), channel_id=1, source_target_pairs={{0,448},{64,0},{128,64},{192,128},{256,192},{320,256},{384,320},{4... | collective-permute-start | bytes 1376264 | tf_op jit(solution)/shard_map/ppermute | solution.py:163
  24.1 21.2 %collective-permute-start.11 = (bf16[256,896]{1,0:T(8,128)(2,1)}, bf16[256,896]{1,0:T(8,128)(2,1)S(1)}, u32[]{:S(2)}, u32[]{:S(2)}) collective-permute-start(bf16[256,896]{1,0:T(8,128)(2,1)} %refs_7_.1), channel_id=1, source_target_pairs={{0,64},{64,128},{128,192},{192,256},{256,320},{320,384},{384,448},... | collective-permute-start | bytes 1376264 | tf_op jit(solution)/shard_map/ppermute | solution.py:162
  29.2 58.6 %copy-start.1 = (bf16[256,896]{1,0:T(8,128)(2,1)}, bf16[256,896]{1,0:T(8,128)(2,1)S(1)}, u32[]{:S(2)}) copy-start(bf16[256,896]{1,0:T(8,128)(2,1)S(1)} %collective-permute-done.refs_1_) | copy-start | bytes 1376260
  29.3 18.6 %collective-permute-start.1 = (bf16[256,896]{1,0:T(8,128)(2,1)S(1)}, bf16[256,896]{1,0:T(8,128)(2,1)S(1)}, u32[]{:S(2)}, u32[]{:S(2)}) collective-permute-start(bf16[256,896]{1,0:T(8,128)(2,1)S(1)} %collective-permute-done.refs_1_), channel_id=1, source_target_pairs={{0,64},{64,128},{128,192},{192,256},{256,320},{320,384},{384,448},... | collective-permute-start | bytes 1376264 | tf_op jit(solution)/shard_map/ppermute | solution.py:162
  31.2 56.7 %copy-start.2 = (bf16[256,896]{1,0:T(8,128)(2,1)}, bf16[256,896]{1,0:T(8,128)(2,1)S(1)}, u32[]{:S(2)}) copy-start(bf16[256,896]{1,0:T(8,128)(2,1)S(1)} %collective-permute-done.4.refs_9_) | copy-start | bytes 1376260
  31.2 18.6 %collective-permute-start.5 = (bf16[256,896]{1,0:T(8,128)(2,1)S(1)}, bf16[256,896]{1,0:T(8,128)(2,1)S(1)}, u32[]{:S(2)}, u32[]{:S(2)}) collective-permute-start(bf16[256,896]{1,0:T(8,128)(2,1)S(1)} %collective-permute-done.4.refs_9_), channel_id=1, source_target_pairs={{0,448},{64,0},{128,64},{192,128},{256,192},{320,256},{384,320},{4... | collective-permute-start | bytes 1376264 | tf_op jit(solution)/shard_map/ppermute | solution.py:163
  40.1 47.8 %copy-start.3 = (bf16[256,896]{1,0:T(8,128)(2,1)}, bf16[256,896]{1,0:T(8,128)(2,1)S(1)}, u32[]{:S(2)}) copy-start(bf16[256,896]{1,0:T(8,128)(2,1)S(1)} %collective-permute-done.8.refs_2_) | copy-start | bytes 1376260
  40.1 19.6 %collective-permute-start.9 = (bf16[256,896]{1,0:T(8,128)(2,1)S(1)}, bf16[256,896]{1,0:T(8,128)(2,1)S(1)}, u32[]{:S(2)}, u32[]{:S(2)}) collective-permute-start(bf16[256,896]{1,0:T(8,128)(2,1)S(1)} %collective-permute-done.8.refs_2_), channel_id=1, source_target_pairs={{0,448},{64,0},{128,64},{192,128},{256,192},{320,256},{384,320},{4... | collective-permute-start | bytes 1376264 | tf_op jit(solution)/shard_map/ppermute | solution.py:163
  45.3 42.6 %copy-start.4 = (bf16[256,896]{1,0:T(8,128)(2,1)}, bf16[256,896]{1,0:T(8,128)(2,1)S(1)}, u32[]{:S(2)}) copy-start(bf16[256,896]{1,0:T(8,128)(2,1)S(1)} %collective-permute-done.11.refs_8_) | copy-start | bytes 1376260
  45.3 19.6 %collective-permute-start.12 = (bf16[256,896]{1,0:T(8,128)(2,1)S(1)}, bf16[256,896]{1,0:T(8,128)(2,1)}, u32[]{:S(2)}, u32[]{:S(2)}) collective-permute-start(bf16[256,896]{1,0:T(8,128)(2,1)S(1)} %collective-permute-done.11.refs_8_), channel_id=1, source_target_pairs={{0,64},{64,128},{128,192},{192,256},{256,320},{320,384},{384,448},... | collective-permute-start | bytes 1376264 | tf_op jit(solution)/shard_map/ppermute | solution.py:162
  47.9 40.0 %copy-start.5 = (bf16[256,896]{1,0:T(8,128)(2,1)}, bf16[256,896]{1,0:T(8,128)(2,1)S(1)}, u32[]{:S(2)}) copy-start(bf16[256,896]{1,0:T(8,128)(2,1)S(1)} %collective-permute-done.1.refs_3_) | copy-start | bytes 1376260
  47.9 24.0 %collective-permute-start.2 = (bf16[256,896]{1,0:T(8,128)(2,1)S(1)}, bf16[256,896]{1,0:T(8,128)(2,1)}, u32[]{:S(2)}, u32[]{:S(2)}) collective-permute-start(bf16[256,896]{1,0:T(8,128)(2,1)S(1)} %collective-permute-done.1.refs_3_), channel_id=1, source_target_pairs={{0,64},{64,128},{128,192},{192,256},{256,320},{320,384},{384,448},... | collective-permute-start | bytes 1376264 | tf_op jit(solution)/shard_map/ppermute | solution.py:162
  49.8 38.1 %copy-start.6 = (bf16[256,896]{1,0:T(8,128)(2,1)}, bf16[256,896]{1,0:T(8,128)(2,1)S(1)}, u32[]{:S(2)}) copy-start(bf16[256,896]{1,0:T(8,128)(2,1)S(1)} %collective-permute-done.5.refs_11_) | copy-start | bytes 1376260
  49.8 22.1 %collective-permute-start.6 = (bf16[256,896]{1,0:T(8,128)(2,1)S(1)}, bf16[256,896]{1,0:T(8,128)(2,1)}, u32[]{:S(2)}, u32[]{:S(2)}) collective-permute-start(bf16[256,896]{1,0:T(8,128)(2,1)S(1)} %collective-permute-done.5.refs_11_), channel_id=1, source_target_pairs={{0,448},{64,0},{128,64},{192,128},{256,192},{320,256},{384,320},{4... | collective-permute-start | bytes 1376264 | tf_op jit(solution)/shard_map/ppermute | solution.py:163
  59.6 28.3 %copy-start.7 = (bf16[256,896]{1,0:T(8,128)(2,1)}, bf16[256,896]{1,0:T(8,128)(2,1)S(1)}, u32[]{:S(2)}) copy-start(bf16[256,896]{1,0:T(8,128)(2,1)S(1)} %collective-permute-done.9.refs_4_) | copy-start | bytes 1376260
  59.6 19.7 %collective-permute-start.10 = (bf16[256,896]{1,0:T(8,128)(2,1)S(1)}, bf16[256,896]{1,0:T(8,128)(2,1)}, u32[]{:S(2)}, u32[]{:S(2)}) collective-permute-start(bf16[256,896]{1,0:T(8,128)(2,1)S(1)} %collective-permute-done.9.refs_4_), channel_id=1, source_target_pairs={{0,448},{64,0},{128,64},{192,128},{256,192},{320,256},{384,320},{4... | collective-permute-start | bytes 1376264 | tf_op jit(solution)/shard_map/ppermute | solution.py:163
  64.9 14.3 %collective-permute-start.13 = (bf16[256,896]{1,0:T(8,128)(2,1)}, bf16[256,896]{1,0:T(8,128)(2,1)}, u32[]{:S(2)}, u32[]{:S(2)}) collective-permute-start(bf16[256,896]{1,0:T(8,128)(2,1)} %collective-permute-done.12.refs_10_), channel_id=1, source_target_pairs={{0,64},{64,128},{128,192},{192,256},{256,320},{320,384},{384,448},... | collective-permute-start | bytes 1376264 | tf_op jit(solution)/shard_map/ppermute | solution.py:162
  79.3 18.9 %collective-permute-start.3 = (bf16[256,896]{1,0:T(8,128)(2,1)}, bf16[256,896]{1,0:T(8,128)(2,1)}, u32[]{:S(2)}, u32[]{:S(2)}) collective-permute-start(bf16[256,896]{1,0:T(8,128)(2,1)} %collective-permute-done.2.refs_5_), channel_id=1, source_target_pairs={{0,64},{64,128},{128,192},{192,256},{256,320},{320,384},{384,448},... | collective-permute-start | bytes 1376264 | tf_op jit(solution)/shard_map/ppermute | solution.py:165
  81.2 16.9 %collective-permute-start.7 = (bf16[256,896]{1,0:T(8,128)(2,1)}, bf16[256,896]{1,0:T(8,128)(2,1)}, u32[]{:S(2)}, u32[]{:S(2)}) collective-permute-start(bf16[256,896]{1,0:T(8,128)(2,1)} %collective-permute-done.6.refs_13_), channel_id=1, source_target_pairs={{0,448},{64,0},{128,64},{192,128},{256,192},{320,256},{384,320},{4... | collective-permute-start | bytes 1376264 | tf_op jit(solution)/shard_map/ppermute | solution.py:165
  103.9 22.5 %all-to-all-start = ((bf16[4,128,1792]{2,1,0:T(8,128)(2,1)}), bf16[4,128,1792]{2,1,0:T(8,128)(2,1)S(1)}, u32[]{:S(2)}, u32[]{:S(2)}) async-start(bf16[4,128,1792]{2,1,0:T(8,128)(2,1)} %bitcast.14), calls=%async_computation | async-start | bytes 3670016 | tf_op jit(solution)/shard_map/all_to_all | solution.py:198
  139.2 2.0 %copy-start = (bf16[896,2048]{1,0:T(8,128)(2,1)S(1)}, bf16[896,2048]{1,0:T(8,128)(2,1)}, u32[]{:S(2)}) copy-start(bf16[896,2048]{1,0:T(8,128)(2,1)} %all-gather.5.cloned.1.call-done.down) | copy-start | bytes 11010052
  145.1 14.0 %collective-permute-start.14 = (f32[256,2048]{1,0:T(8,128)S(1)}, f32[256,2048]{1,0:T(8,128)S(1)}, u32[]{:S(2)}, u32[]{:S(2)}) collective-permute-start(f32[256,2048]{1,0:T(8,128)S(1)} %get-tuple-element.16), channel_id=1, source_target_pairs={{0,4},{4,0},{8,12},{12,8},{16,20},{20,16},{24,28},{28,24},{32,36},... | collective-permute-start | bytes 6291464 | tf_op jit(solution)/shard_map/ppermute | solution.py:204
Sparse Core Ops, SparseCore 0:
  9.5 47.7 all-gather.2
  79.4 53.8 all-gather.4

commit v3 on v2

--- a/solution.py
+++ b/solution.py
@@ -47,67 +47,57 @@
     )(place, keep, weight)
 
 
-def product_kernel(count, added, place, gate_keep, up_keep, tokens, *refs):
-    so_far = refs[0] if added else None
-    pieces = refs[1 if added else 0 : -3]
+def product_kernel(place, keep_ref, tokens, *refs):
+    pieces = refs[:-3]
     out, held, sems = refs[-3:]
-    units = pieces[0].shape[1]
+    units = held.shape[1]
     copies, row = [], 0
-    for k in range(count):
-        rows = pieces[k].shape[0]
-        for side in range(2):
-            spot = (pl.ds(row, rows), pl.ds(side * units, units))
-            copy = pltpu.make_async_copy(pieces[side * count + k], held.at[spot], sems.at[2 * k + side])
-            copy.start()
-            copies.append((row, rows, copy))
-        row += rows
-    firsts = [place[2 + k] for k in range(count)]
-    spots = [pl.ds(pl.multiple_of(firsts[k], BLOCK), copies[2 * k][1]) for k in range(count)]
-    for k, (row, rows, copy) in enumerate(copies):
+    for k, ref in enumerate(pieces):
+        copy = pltpu.make_async_copy(ref, held.at[pl.ds(row, ref.shape[0]), :], sems.at[k])
+        copy.start()
+        copies.append((row, ref.shape[0], copy))
+        row += ref.shape[0]
+    firsts = [place[2 + k] for k in range(len(pieces))]
+    spots = [pl.ds(pl.multiple_of(first, BLOCK), rows) for first, (_, rows, _) in zip(firsts, copies)]
+    for first, (row, rows, copy) in zip(firsts, copies):
         copy.wait()
-        keep, left = ((gate_keep, 0), (up_keep, units))[k % 2]
-        block_row = place[0] + lax.div(firsts[k // 2], BLOCK)
+        block_row = place[0] + lax.div(first, BLOCK)
         for i in range(rows // BLOCK):
             for n in range(units // BLOCK):
-                spot = (pl.ds(row + i * BLOCK, BLOCK), pl.ds(left + n * BLOCK, BLOCK))
-                held[spot] = held[spot] * keep[block_row + i, place[1] + n].astype(held.dtype)
+                spot = (pl.ds(row + i * BLOCK, BLOCK), pl.ds(n * BLOCK, BLOCK))
+                held[spot] = held[spot] * keep_ref[block_row + i, place[1] + n].astype(held.dtype)
     half, width = tokens.shape[0] // 2, 4 * BLOCK
-    for start in range(0, 2 * units, width):
-        columns = pl.ds(start, min(width, 2 * units - start))
+    for start in range(0, units, width):
+        columns = pl.ds(start, min(width, units - start))
         for t in range(2):
             part = pl.ds(t * half, half)
-            left = [tokens[part, spot] for spot in spots]
-            left = jnp.concatenate(left, 1) if count > 1 else left[0]
+            left = jnp.concatenate([tokens[part, spot] for spot in spots], 1)
             total = jnp.dot(left, held[:, columns], preferred_element_type=jnp.float32)
-            if added:
-                total = total + so_far[part, columns]
             out[part, columns] = total.astype(out.dtype)
 
 
-def product(tokens, gates, ups, gate_keep, up_keep, so_far, dtype, name):
+def product(tokens, pieces, keep, name):
     row, size = lax.axis_index("row"), lax.axis_size("row")
     count, features = tokens.shape
-    units = ups[0][2].shape[1]
-    rows = sum(a.shape[0] for _, _, a in ups)
+    units = pieces[0][1].shape[1]
     place = [lax.axis_index("depth") * (features // BLOCK), lax.axis_index("col") * (units // BLOCK)]
-    place += [lax.rem(row + off + size, size) * (features // size) + start for off, start, _ in ups]
-    arrays = [a for _, _, a in gates] + [a for _, _, a in ups]
-    added = [] if so_far is None else [so_far]
+    place += [lax.rem(row + off + size, size) * (features // size) for off, _ in pieces]
+    arrays = [a for _, a in pieces]
     return pl.pallas_call(
-        functools.partial(product_kernel, len(ups), so_far is not None),
-        out_shape=jax.ShapeDtypeStruct((count, 2 * units), dtype),
-        in_specs=[IN_SMEM] * 3 + [IN_VMEM] * (1 + len(added)) + [ANYWHERE] * len(arrays),
+        product_kernel,
+        out_shape=jax.ShapeDtypeStruct((count, units), jnp.bfloat16),
+        in_specs=[IN_SMEM] * 2 + [IN_VMEM] + [ANYWHERE] * len(arrays),
         out_specs=IN_VMEM,
         scratch_shapes=[
-            pltpu.VMEM((rows, 2 * units), jnp.bfloat16),
+            pltpu.VMEM((features, units), jnp.bfloat16),
             pltpu.SemaphoreType.DMA((len(arrays),)),
         ],
         compiler_params=pltpu.CompilerParams(vmem_limit_bytes=VMEM),
         cost_estimate=pl.CostEstimate(
-            flops=4 * count * rows * units, bytes_accessed=4 * rows * units, transcendentals=0
+            flops=2 * count * features * units, bytes_accessed=2 * features * units, transcendentals=0
         ),
         name=name,
-    )(jnp.stack(place).astype(jnp.int32), gate_keep, up_keep, tokens, *added, *arrays)
+    )(jnp.stack(place).astype(jnp.int32), keep, tokens, *arrays)
 
 
 def second_kernel(share, place, hidden, down, out_own, out_other, held, weight, sems):
@@ -156,13 +146,13 @@
 
 def gather_ring(piece, axis, way):
     size = lax.axis_size(axis)
-    found = [(0, 0, piece)]
+    found = [(0, piece)]
     ahead = behind = piece
     for step in range(1, size // 2):
         ahead = lax.ppermute(ahead, axis, ring(size, 1))
         behind = lax.ppermute(behind, axis, ring(size, -1))
-        found += [(-step, 0, ahead), (step, 0, behind)]
-    found.append((size // 2, 0, lax.ppermute(ahead if way > 0 else behind, axis, ring(size, way))))
+        found += [(-step, ahead), (step, behind)]
+    found.append((size // 2, lax.ppermute(ahead if way > 0 else behind, axis, ring(size, way))))
     return found
 
 
@@ -179,25 +169,20 @@
     gates, ups = gather_ring(gate_weight, "row", 1), gather_ring(up_weight, "row", -1)
     down_row = (col * row_size + row) * down_weight.shape[0]
     down = masked(down_weight, down_keep, down_row, depth * (down_weight.shape[1] // BLOCK))
-    down = after(down, *[a for _, _, a in gates[-3:-1] + ups[-3:-1]])
+    down = after(down, *[a for _, a in gates[-3:] + ups[-3:-1]])
     down = lax.all_gather(down, "row", axis=0, tiled=True)
 
-    so_far = product(token_block, gates[:-1], ups[:-1], gate_keep, up_keep, None, jnp.float32, "most")
-    gate, up, so_far = lax.optimization_barrier((gates[-1][2], ups[-1][2], so_far))
-    both = product(
-        token_block,
-        [gates[-1][:2] + (gate,)],
-        [ups[-1][:2] + (up,)],
-        gate_keep,
-        up_keep,
-        so_far,
-        jnp.bfloat16,
-        "last",
-    )
-    both = both.reshape((depth_size, -1, both.shape[1]))
-    both = lax.all_to_all(both, "depth", 0, 0, tiled=True)
-    both = jnp.sum(both.astype(jnp.float32), 0)
-    hidden = (jax.nn.silu(both[:, :units]) * both[:, units:]).astype(jnp.bfloat16)
+    def exchange(share):
+        return lax.all_to_all(share.reshape((depth_size, -1, units)), "depth", 0, 0, tiled=True)
+
+    gate = product(token_block, gates, gate_keep, "gate")
+    last, gate = lax.optimization_barrier((ups[-1][1], gate))
+    gate = exchange(gate)
+    up = product(token_block, ups[:-1] + [(ups[-1][0], last)], up_keep, "up")
+    up, gate = lax.optimization_barrier((up, gate))
+    up = exchange(up)
+    gate, up = [jnp.sum(share.astype(jnp.float32), 0) for share in (gate, up)]
+    hidden = (jax.nn.silu(gate) * up).astype(jnp.bfloat16)
     hidden = lax.all_gather(hidden, "depth", axis=0, tiled=True)
 
     mine, theirs = second_product(hidden, down, tokens.shape[0])

time: 203 us -> 201 us (level)
  waiting for transfers between devices: 43 us -> 46.9 us
  starting transfers between devices: 68.4 us -> 64.6 us
  Pallas kernels: 22.8 us -> 20.7 us
    ppermute x2, waiting for transfers between devices: 0.01 us -> 7.76 us  [gather_ring(): lax.ppermute(ahead if way > 0 else behind, axis, ring(size, way))]
    all_to_all x1 -> x2, waiting for transfers between devices: 18.5 us -> 11 us  [exchange(): lax.all_to_all(share.reshape((depth_size, -1, units)), 'depth', 0, 0, til...]
    all_gather x1, waiting for transfers between devices: 0.01 us -> 5.55 us  [on_device(): down = lax.all_gather(down, 'row', axis=0, tiled=True)]
    ppermute x1, starting transfers between devices: 10.2 us -> 5.46 us  [on_device(): mine = mine + lax.ppermute(theirs, 'col', swap)]
    all_to_all x1 -> x2, starting transfers between devices: 4.02 us -> 7.54 us  [exchange(): lax.all_to_all(share.reshape((depth_size, -1, units)), 'depth', 0, 0, til...]
    ppermute x2, starting transfers between devices: 7.35 us -> 4.66 us  [gather_ring(): lax.ppermute(ahead if way > 0 else behind, axis, ring(size, way))]
    ppermute x6, waiting for transfers between devices: 16.2 us -> 13.7 us  [gather_ring(): behind = lax.ppermute(behind, axis, ring(size, -1))]
    pallas_call x2, Pallas kernels: 16 us -> 13.9 us  [product(): pl.pallas_call(product_kernel, out_shape=jax.ShapeDtypeStruct((count, uni...]
  transfers between devices with their start and end apart: 18 -> 19, of which waited for: 7 -> 11; matrix products, arithmetic and copies ran while one was open for 2% -> 2% of each run, Pallas kernels for 9% -> 8%
where the time goes in v3:
time: 201 us; the launch traced here: 200 us
  starting transfers between devices  64.6 us (32%)
  blocking collectives  47.6 us (24%)
  waiting for transfers between devices  46.9 us (23%)
  Pallas kernels  20.7 us (10%)
  between operations  13.7 us (7%)
  local copies, waits for them, and re-layouts  4.13 us (2%)
  other arithmetic  2.06 us (1%)
    all_to_all x1, blocking collectives, on_device(): lax.all_to_all(mine, 'col', 0, 0, axis_index_groups=same_core, tiled=True)  34.5 us
    ppermute x6, starting transfers between devices, gather_ring(): behind = lax.ppermute(behind, axis, ring(size, -1))  32.4 us
    ppermute x6, starting transfers between devices, gather_ring(): ahead = lax.ppermute(ahead, axis, ring(size, 1))  14.4 us
    pallas_call x2, Pallas kernels, product(): pl.pallas_call(product_kernel, out_shape=jax.ShapeDtypeStruct((count, uni...  13.9 us
    ppermute x6, waiting for transfers between devices, gather_ring(): behind = lax.ppermute(behind, axis, ring(size, -1))  13.7 us
    all_gather x1, blocking collectives, on_device(): hidden = lax.all_gather(hidden, 'depth', axis=0, tiled=True)  13 us
    all_to_all x2, waiting for transfers between devices, exchange(): lax.all_to_all(share.reshape((depth_size, -1, units)), 'depth', 0, 0, til...  11 us
    ppermute x2, waiting for transfers between devices, gather_ring(): lax.ppermute(ahead if way > 0 else behind, axis, ring(size, way))  7.76 us
  transfers between devices with their start and end apart: 19, of which 11 were waited for; matrix products, arithmetic and copies ran while one was open for 2% of the time, Pallas kernels for 8%

profile of v3, /device:TPU:1, one launch (start us, length us, event | category | flops | bytes accessed | tf_op | source)
XLA Modules:
  0.0 199.6 jit_solution(13283179836535207154)
XLA Ops:
  6.5 0.7 all-gather.3.cloned.1.call-update
  7.3 0.0 all-gather.5.cloned.1.call-start
  7.3 4.8 %collective-permute-start.7 = (bf16[256,896]{1,0:T(8,128)(2,1)}, bf16[256,896]{1,0:T(8,128)(2,1)S(1)}, u32[]{:S(2)}, u32[]{:S(2)}) collective-permute-start(bf16[256,896]{1,0:T(8,128)(2,1)} %refs_0_.2), channel_id=1, source_target_pairs={{0,64},{64,128},{128,192},{192,256},{256,320},{320,384},{384,448},... | collective-permute-start | bytes 1376264 | tf_op jit(solution)/shard_map/ppermute | solution.py:152
  12.1 8.6 %collective-permute-start.8 = (bf16[256,896]{1,0:T(8,128)(2,1)}, bf16[256,896]{1,0:T(8,128)(2,1)S(1)}, u32[]{:S(2)}, u32[]{:S(2)}) collective-permute-start(bf16[256,896]{1,0:T(8,128)(2,1)} %refs_0_.2), channel_id=1, source_target_pairs={{0,448},{64,0},{128,64},{192,128},{256,192},{320,256},{384,320},{4... | collective-permute-start | bytes 1376264 | tf_op jit(solution)/shard_map/ppermute | solution.py:153
  20.7 3.4 %collective-permute-start.1 = (bf16[256,896]{1,0:T(8,128)(2,1)}, bf16[256,896]{1,0:T(8,128)(2,1)S(1)}, u32[]{:S(2)}, u32[]{:S(2)}) collective-permute-start(bf16[256,896]{1,0:T(8,128)(2,1)} %refs_0_.3), channel_id=1, source_target_pairs={{0,448},{64,0},{128,64},{192,128},{256,192},{320,256},{384,320},{4... | collective-permute-start | bytes 1376264 | tf_op jit(solution)/shard_map/ppermute | solution.py:153
  24.1 1.9 collective-permute-start
  26.0 3.2 %collective-permute-done.7.refs_1_ = bf16[256,896]{1,0:T(8,128)(2,1)S(1)} collective-permute-done((bf16[256,896]{1,0:T(8,128)(2,1)}, bf16[256,896]{1,0:T(8,128)(2,1)S(1)}, u32[]{:S(2)}, u32[]{:S(2)}) %collective-permute-start.7) | collective-permute-done | bytes 458784 | tf_op jit(solution)/shard_map/ppermute | solution.py:152
  29.3 1.9 collective-permute-start.9
  31.2 0.0 collective-permute-done.8.refs_2_
  31.2 4.6 %collective-permute-start.10 = (bf16[256,896]{1,0:T(8,128)(2,1)S(1)}, bf16[256,896]{1,0:T(8,128)(2,1)}, u32[]{:S(2)}, u32[]{:S(2)}) collective-permute-start(bf16[256,896]{1,0:T(8,128)(2,1)S(1)} %collective-permute-done.8.refs_2_), channel_id=1, source_target_pairs={{0,448},{64,0},{128,64},{192,128},{256,192},{320,256},{384,320},{4... | collective-permute-start | bytes 1376264 | tf_op jit(solution)/shard_map/ppermute | solution.py:153
  35.8 4.3 %collective-permute-done.1.refs_2_ = bf16[256,896]{1,0:T(8,128)(2,1)S(1)} collective-permute-done((bf16[256,896]{1,0:T(8,128)(2,1)}, bf16[256,896]{1,0:T(8,128)(2,1)S(1)}, u32[]{:S(2)}, u32[]{:S(2)}) %collective-permute-start.1) | collective-permute-done | bytes 458784 | tf_op jit(solution)/shard_map/ppermute | solution.py:153
  40.1 5.2 %collective-permute-start.3 = (bf16[256,896]{1,0:T(8,128)(2,1)S(1)}, bf16[256,896]{1,0:T(8,128)(2,1)S(1)}, u32[]{:S(2)}, u32[]{:S(2)}) collective-permute-start(bf16[256,896]{1,0:T(8,128)(2,1)S(1)} %collective-permute-done.1.refs_2_), channel_id=1, source_target_pairs={{0,448},{64,0},{128,64},{192,128},{256,192},{320,256},{384,320},{4... | collective-permute-start | bytes 1376264 | tf_op jit(solution)/shard_map/ppermute | solution.py:153
  45.3 0.0 collective-permute-done.refs_1_
  45.3 1.9 collective-permute-start.2
  47.2 0.6 collective-permute-done.9.refs_3_
  47.9 1.9 collective-permute-start.11
  49.8 5.4 %collective-permute-start.12 = (bf16[256,896]{1,0:T(8,128)(2,1)}, bf16[256,896]{1,0:T(8,128)(2,1)}, u32[]{:S(2)}, u32[]{:S(2)}) collective-permute-start(bf16[256,896]{1,0:T(8,128)(2,1)} %collective-permute-done.10.refs_4_), channel_id=1, source_target_pairs={{0,448},{64,0},{128,64},{192,128},{256,192},{320,256},{384,320},{4... | collective-permute-start | bytes 1376264 | tf_op jit(solution)/shard_map/ppermute | solution.py:153
  55.2 4.4 %collective-permute-done.3.refs_4_ = bf16[256,896]{1,0:T(8,128)(2,1)S(1)} collective-permute-done((bf16[256,896]{1,0:T(8,128)(2,1)S(1)}, bf16[256,896]{1,0:T(8,128)(2,1)S(1)}, u32[]{:S(2)}, u32[]{:S(2)}) %collective-permute-start.3) | collective-permute-done | bytes 458784 | tf_op jit(solution)/shard_map/ppermute | solution.py:153
  59.6 5.3 %collective-permute-start.5 = (bf16[256,896]{1,0:T(8,128)(2,1)S(1)}, bf16[256,896]{1,0:T(8,128)(2,1)}, u32[]{:S(2)}, u32[]{:S(2)}) collective-permute-start(bf16[256,896]{1,0:T(8,128)(2,1)S(1)} %collective-permute-done.3.refs_4_), channel_id=1, source_target_pairs={{0,448},{64,0},{128,64},{192,128},{256,192},{320,256},{384,320},{4... | collective-permute-start | bytes 1376264 | tf_op jit(solution)/shard_map/ppermute | solution.py:153
  64.9 1.9 collective-permute-start.4
  66.9 0.5 collective-permute-done.11.refs_5_
  67.4 1.9 collective-permute-start.13
  69.3 1.5 copy.8.keep_ref
  70.8 0.6 pad_add_fusion.place
  71.3 2.9 %mask.1 = bf16[112,2048]{1,0:T(8,128)(2,1)} custom-call(s32[2]{0:T(128)} %pad_add_fusion.place, s32[112,64]{1,0:T(8,128)} %copy.8.keep_ref, bf16[112,2048]{1,0:T(8,128)(2,1)} %weight.1), custom_call_target="tpu_custom_call" | custom-call | flops 229376 | bytes 917504 | tf_op jit(solution)/shard_map/mask/pallas_call | solution.py:39
  74.3 5.0 %collective-permute-done.5.refs_6_ = bf16[256,896]{1,0:T(8,128)(2,1)} collective-permute-done((bf16[256,896]{1,0:T(8,128)(2,1)S(1)}, bf16[256,896]{1,0:T(8,128)(2,1)}, u32[]{:S(2)}, u32[]{:S(2)}) %collective-permute-start.5) | collective-permute-done | bytes 458784 | tf_op jit(solution)/shard_map/ppermute | solution.py:153
  79.3 7.8 %collective-permute-done.13.refs_7_ = bf16[256,896]{1,0:T(8,128)(2,1)} collective-permute-done((bf16[256,896]{1,0:T(8,128)(2,1)}, bf16[256,896]{1,0:T(8,128)(2,1)}, u32[]{:S(2)}, u32[]{:S(2)}) %collective-permute-start.13) | collective-permute-done | bytes 458784 | tf_op jit(solution)/shard_map/ppermute | solution.py:155
  87.0 0.0 all-gather.5.cloned.1.call-update
  87.1 2.8 %collective-permute-start.6 = (bf16[256,896]{1,0:T(8,128)(2,1)}, bf16[256,896]{1,0:T(8,128)(2,1)}, u32[]{:S(2)}, u32[]{:S(2)}) collective-permute-start(bf16[256,896]{1,0:T(8,128)(2,1)} %collective-permute-done.5.refs_6_), channel_id=1, source_target_pairs={{0,448},{64,0},{128,64},{192,128},{256,192},{320,256},{384,320},{4... | collective-permute-start | bytes 1376264 | tf_op jit(solution)/shard_map/ppermute | solution.py:155
  89.8 0.6 stack.61.place
  90.4 7.0 %gate.1 = bf16[512,896]{1,0:T(8,128)(2,1)} custom-call(s32[10]{0:T(128)} %stack.61.place, s32[64,112]{1,0:T(8,128)} %keep_ref.3, bf16[512,2048]{1,0:T(8,128)(2,1)} %all-gather.3.cloned.1.call-done.tokens, bf16[256,896]{1,0:T(8,128)(2,1)} %refs_0_.2, bf16[256,896]{1,0:T(8,128)(2,1)} %copy-done.3, bf16[256,896]{1,0:T(8,128)(2,1)} %copy-done.4, ...), custom_call_target="tpu_custom_call" | custom-call | flops 1879048192 | bytes 3670016 | tf_op jit(solution)/shard_map/gate/pallas_call | solution.py:86
  97.5 4.0 %all-to-all-start = ((bf16[4,128,896]{2,1,0:T(8,128)(2,1)}), bf16[4,128,896]{2,1,0:T(8,128)(2,1)S(1)}, u32[]{:S(2)}, u32[]{:S(2)}) async-start(bf16[4,128,896]{2,1,0:T(8,128)(2,1)} %bitcast.17), calls=%async_computation | async-start | bytes 1835008 | tf_op jit(solution)/shard_map/all_to_all | solution.py:176
  101.5 7.0 %up.1 = bf16[512,896]{1,0:T(8,128)(2,1)} custom-call(s32[10]{0:T(128)} %stack.61.place, s32[64,112]{1,0:T(8,128)} %keep_ref.4, bf16[512,2048]{1,0:T(8,128)(2,1)} %all-gather.3.cloned.1.call-done.tokens, bf16[256,896]{1,0:T(8,128)(2,1)} %refs_0_.3, bf16[256,896]{1,0:T(8,128)(2,1)} %copy-done.2, bf16[256,896]{1,0:T(8,128)(2,1)} %copy-done.1, ...), custom_call_target="tpu_custom_call" | custom-call | flops 1879048192 | bytes 3670016 | tf_op jit(solution)/shard_map/up/pallas_call | solution.py:86
  108.5 2.1 %all-to-all-done = bf16[4,128,896]{2,1,0:T(8,128)(2,1)S(1)} async-done(((bf16[4,128,896]{2,1,0:T(8,128)(2,1)}), bf16[4,128,896]{2,1,0:T(8,128)(2,1)S(1)}, u32[]{:S(2)}, u32[]{:S(2)}) %all-to-all-start) | async-done | bytes 917536 | tf_op jit(solution)/shard_map/all_to_all | solution.py:176
  110.6 3.5 %all-to-all-start.1 = ((bf16[4,128,896]{2,1,0:T(8,128)(2,1)}), bf16[4,128,896]{2,1,0:T(8,128)(2,1)S(1)}, u32[]{:S(2)}, u32[]{:S(2)}) async-start(bf16[4,128,896]{2,1,0:T(8,128)(2,1)} %bitcast.16), calls=%async_computation.1 | async-start | bytes 1835008 | tf_op jit(solution)/shard_map/all_to_all | solution.py:176
  114.1 0.1 convert_reduce_fusion.1
  114.2 8.9 %all-to-all-done.1 = bf16[4,128,896]{2,1,0:T(8,128)(2,1)S(1)} async-done(((bf16[4,128,896]{2,1,0:T(8,128)(2,1)}), bf16[4,128,896]{2,1,0:T(8,128)(2,1)S(1)}, u32[]{:S(2)}, u32[]{:S(2)}) %all-to-all-start.1) | async-done | bytes 917536 | tf_op jit(solution)/shard_map/all_to_all | solution.py:176
  123.1 0.1 convert_reduce_fusion
  123.3 0.1 multiply_convert_fusion
  123.4 13.0 %all_gather.10.hidden = bf16[512,896]{1,0:T(8,128)(2,1)S(1)} all-gather(bf16[128,896]{1,0:T(8,128)(2,1)S(1)} %multiply_convert_fusion), channel_id=1, replica_groups=mesh['row'=8,'col'=16,'depth'=4] {'depth'}, dimensions={0}, use_global_device_ids=true | all-gather | bytes 1146880 | tf_op jit(solution)/shard_map/all_gather | solution.py:186
  136.4 5.5 %all-gather.5.cloned.1.call-done.down = bf16[896,2048]{1,0:T(8,128)(2,1)} async-done(((bf16[112,2048]{1,0:T(8,128)(2,1)}), bf16[896,2048]{1,0:T(8,128)(2,1)}) %all-gather.5.cloned.1.call-update) | async-done | bytes 3670032 | tf_op jit(solution)/shard_map/all_gather | solution.py:173
  142.0 2.0 %copy-done = bf16[896,2048]{1,0:T(8,128)(2,1)S(1)} copy-done((bf16[896,2048]{1,0:T(8,128)(2,1)S(1)}, bf16[896,2048]{1,0:T(8,128)(2,1)}, u32[]{:S(2)}) %copy-start) | copy-done | bytes 3670040
  144.0 3.9 %second.1 = (f32[256,2048]{1,0:T(8,128)S(1)}, f32[256,2048]{1,0:T(8,128)S(1)}) custom-call(s32[1]{0:T(128)} %bitcast.place, bf16[512,896]{1,0:T(8,128)(2,1)S(1)} %all_gather.10.hidden, bf16[896,2048]{1,0:T(8,128)(2,1)S(1)} %copy-done), custom_call_target="tpu_custom_call" | custom-call | flops 1879048192 | bytes 9437184 | tf_op jit(solution)/shard_map/second/pallas_call | solution.py:129
  147.9 5.5 %collective-permute-start.14 = (f32[256,2048]{1,0:T(8,128)S(1)}, f32[256,2048]{1,0:T(8,128)S(1)}, u32[]{:S(2)}, u32[]{:S(2)}) collective-permute-start(f32[256,2048]{1,0:T(8,128)S(1)} %get-tuple-element.18), channel_id=1, source_target_pairs={{0,4},{4,0},{8,12},{12,8},{16,20},{20,16},{24,28},{28,24},{32,36},... | collective-permute-start | bytes 6291464 | tf_op jit(solution)/shard_map/ppermute | solution.py:189
  153.4 3.8 %collective-permute-done.14 = f32[256,2048]{1,0:T(8,128)S(1)} collective-permute-done((f32[256,2048]{1,0:T(8,128)S(1)}, f32[256,2048]{1,0:T(8,128)S(1)}, u32[]{:S(2)}, u32[]{:S(2)}) %collective-permute-start.14) | collective-permute-done | bytes 2097184 | tf_op jit(solution)/shard_map/ppermute | solution.py:189
  157.1 0.3 add_convert_fusion
  157.4 34.5 %all_to_all.15 = bf16[8,32,2048]{2,1,0:T(8,128)(2,1)S(1)} all-to-all(bf16[8,32,2048]{2,1,0:T(8,128)(2,1)S(1)} %bitcast.15), channel_id=1, replica_groups={{0,8,16,24,32,40,48,56},{4,12,20,28,36,44,52,60},{1,9,17,25,33,41,49,57..., dimensions={0} | all-to-all | bytes 2097152 | tf_op jit(solution)/shard_map/all_to_all | solution.py:191
  192.0 0.8 reduce_sum.32
  (22 shorter events, 0.0 us)
Async XLA Ops:
  6.5 83.9 %all-gather.3.cloned.1.call-start = ((), (), s32[]{:S(2)}) async-start(), calls=%async_computation.3 | async-start | bytes 2228224 | tf_op jit(solution)/shard_map/all_gather | solution.py:168
  7.3 134.7 %all-gather.5.cloned.1.call-start = ((), (), s32[]{:S(2)}) async-start(), calls=%async_computation.4 | async-start | bytes 4128768 | tf_op jit(solution)/shard_map/all_gather | solution.py:173
  7.3 21.9 %collective-permute-start.7 = (bf16[256,896]{1,0:T(8,128)(2,1)}, bf16[256,896]{1,0:T(8,128)(2,1)S(1)}, u32[]{:S(2)}, u32[]{:S(2)}) collective-permute-start(bf16[256,896]{1,0:T(8,128)(2,1)} %refs_0_.2), channel_id=1, source_target_pairs={{0,64},{64,128},{128,192},{192,256},{256,320},{320,384},{384,448},... | collective-permute-start | bytes 1376264 | tf_op jit(solution)/shard_map/ppermute | solution.py:152
  12.1 19.0 %collective-permute-start.8 = (bf16[256,896]{1,0:T(8,128)(2,1)}, bf16[256,896]{1,0:T(8,128)(2,1)S(1)}, u32[]{:S(2)}, u32[]{:S(2)}) collective-permute-start(bf16[256,896]{1,0:T(8,128)(2,1)} %refs_0_.2), channel_id=1, source_target_pairs={{0,448},{64,0},{128,64},{192,128},{256,192},{320,256},{384,320},{4... | collective-permute-start | bytes 1376264 | tf_op jit(solution)/shard_map/ppermute | solution.py:153
  20.7 19.3 %collective-permute-start.1 = (bf16[256,896]{1,0:T(8,128)(2,1)}, bf16[256,896]{1,0:T(8,128)(2,1)S(1)}, u32[]{:S(2)}, u32[]{:S(2)}) collective-permute-start(bf16[256,896]{1,0:T(8,128)(2,1)} %refs_0_.3), channel_id=1, source_target_pairs={{0,448},{64,0},{128,64},{192,128},{256,192},{320,256},{384,320},{4... | collective-permute-start | bytes 1376264 | tf_op jit(solution)/shard_map/ppermute | solution.py:153
  24.1 21.2 %collective-permute-start = (bf16[256,896]{1,0:T(8,128)(2,1)}, bf16[256,896]{1,0:T(8,128)(2,1)S(1)}, u32[]{:S(2)}, u32[]{:S(2)}) collective-permute-start(bf16[256,896]{1,0:T(8,128)(2,1)} %refs_0_.3), channel_id=1, source_target_pairs={{0,64},{64,128},{128,192},{192,256},{256,320},{320,384},{384,448},... | collective-permute-start | bytes 1376264 | tf_op jit(solution)/shard_map/ppermute | solution.py:152
  29.2 61.2 %copy-start.3 = (bf16[256,896]{1,0:T(8,128)(2,1)}, bf16[256,896]{1,0:T(8,128)(2,1)S(1)}, u32[]{:S(2)}) copy-start(bf16[256,896]{1,0:T(8,128)(2,1)S(1)} %collective-permute-done.7.refs_1_) | copy-start | bytes 1376260
  29.3 18.6 %collective-permute-start.9 = (bf16[256,896]{1,0:T(8,128)(2,1)S(1)}, bf16[256,896]{1,0:T(8,128)(2,1)S(1)}, u32[]{:S(2)}, u32[]{:S(2)}) collective-permute-start(bf16[256,896]{1,0:T(8,128)(2,1)S(1)} %collective-permute-done.7.refs_1_), channel_id=1, source_target_pairs={{0,64},{64,128},{128,192},{192,256},{256,320},{320,384},{384,448},... | collective-permute-start | bytes 1376264 | tf_op jit(solution)/shard_map/ppermute | solution.py:152
  31.2 59.2 %copy-start.4 = (bf16[256,896]{1,0:T(8,128)(2,1)}, bf16[256,896]{1,0:T(8,128)(2,1)S(1)}, u32[]{:S(2)}) copy-start(bf16[256,896]{1,0:T(8,128)(2,1)S(1)} %collective-permute-done.8.refs_2_) | copy-start | bytes 1376260
  31.2 18.6 %collective-permute-start.10 = (bf16[256,896]{1,0:T(8,128)(2,1)S(1)}, bf16[256,896]{1,0:T(8,128)(2,1)}, u32[]{:S(2)}, u32[]{:S(2)}) collective-permute-start(bf16[256,896]{1,0:T(8,128)(2,1)S(1)} %collective-permute-done.8.refs_2_), channel_id=1, source_target_pairs={{0,448},{64,0},{128,64},{192,128},{256,192},{320,256},{384,320},{4... | collective-permute-start | bytes 1376264 | tf_op jit(solution)/shard_map/ppermute | solution.py:153
  40.1 57.4 %copy-start.1 = (bf16[256,896]{1,0:T(8,128)(2,1)}, bf16[256,896]{1,0:T(8,128)(2,1)S(1)}, u32[]{:S(2)}) copy-start(bf16[256,896]{1,0:T(8,128)(2,1)S(1)} %collective-permute-done.1.refs_2_) | copy-start | bytes 1376260
  40.1 19.6 %collective-permute-start.3 = (bf16[256,896]{1,0:T(8,128)(2,1)S(1)}, bf16[256,896]{1,0:T(8,128)(2,1)S(1)}, u32[]{:S(2)}, u32[]{:S(2)}) collective-permute-start(bf16[256,896]{1,0:T(8,128)(2,1)S(1)} %collective-permute-done.1.refs_2_), channel_id=1, source_target_pairs={{0,448},{64,0},{128,64},{192,128},{256,192},{320,256},{384,320},{4... | collective-permute-start | bytes 1376264 | tf_op jit(solution)/shard_map/ppermute | solution.py:153
  45.3 52.1 %copy-start.2 = (bf16[256,896]{1,0:T(8,128)(2,1)}, bf16[256,896]{1,0:T(8,128)(2,1)S(1)}, u32[]{:S(2)}) copy-start(bf16[256,896]{1,0:T(8,128)(2,1)S(1)} %collective-permute-done.refs_1_) | copy-start | bytes 1376260
  45.3 19.6 %collective-permute-start.2 = (bf16[256,896]{1,0:T(8,128)(2,1)S(1)}, bf16[256,896]{1,0:T(8,128)(2,1)S(1)}, u32[]{:S(2)}, u32[]{:S(2)}) collective-permute-start(bf16[256,896]{1,0:T(8,128)(2,1)S(1)} %collective-permute-done.refs_1_), channel_id=1, source_target_pairs={{0,64},{64,128},{128,192},{192,256},{256,320},{320,384},{384,448},... | collective-permute-start | bytes 1376264 | tf_op jit(solution)/shard_map/ppermute | solution.py:152
  47.9 42.6 %copy-start.6 = (bf16[256,896]{1,0:T(8,128)(2,1)}, bf16[256,896]{1,0:T(8,128)(2,1)S(1)}, u32[]{:S(2)}) copy-start(bf16[256,896]{1,0:T(8,128)(2,1)S(1)} %collective-permute-done.9.refs_3_) | copy-start | bytes 1376260
  47.9 19.5 %collective-permute-start.11 = (bf16[256,896]{1,0:T(8,128)(2,1)S(1)}, bf16[256,896]{1,0:T(8,128)(2,1)}, u32[]{:S(2)}, u32[]{:S(2)}) collective-permute-start(bf16[256,896]{1,0:T(8,128)(2,1)S(1)} %collective-permute-done.9.refs_3_), channel_id=1, source_target_pairs={{0,64},{64,128},{128,192},{192,256},{256,320},{320,384},{384,448},... | collective-permute-start | bytes 1376264 | tf_op jit(solution)/shard_map/ppermute | solution.py:152
  49.8 24.5 %collective-permute-start.12 = (bf16[256,896]{1,0:T(8,128)(2,1)}, bf16[256,896]{1,0:T(8,128)(2,1)}, u32[]{:S(2)}, u32[]{:S(2)}) collective-permute-start(bf16[256,896]{1,0:T(8,128)(2,1)} %collective-permute-done.10.refs_4_), channel_id=1, source_target_pairs={{0,448},{64,0},{128,64},{192,128},{256,192},{320,256},{384,320},{4... | collective-permute-start | bytes 1376264 | tf_op jit(solution)/shard_map/ppermute | solution.py:153
  59.6 37.8 %copy-start.5 = (bf16[256,896]{1,0:T(8,128)(2,1)}, bf16[256,896]{1,0:T(8,128)(2,1)S(1)}, u32[]{:S(2)}) copy-start(bf16[256,896]{1,0:T(8,128)(2,1)S(1)} %collective-permute-done.3.refs_4_) | copy-start | bytes 1376260
  59.6 19.7 %collective-permute-start.5 = (bf16[256,896]{1,0:T(8,128)(2,1)S(1)}, bf16[256,896]{1,0:T(8,128)(2,1)}, u32[]{:S(2)}, u32[]{:S(2)}) collective-permute-start(bf16[256,896]{1,0:T(8,128)(2,1)S(1)} %collective-permute-done.3.refs_4_), channel_id=1, source_target_pairs={{0,448},{64,0},{128,64},{192,128},{256,192},{320,256},{384,320},{4... | collective-permute-start | bytes 1376264 | tf_op jit(solution)/shard_map/ppermute | solution.py:153
  64.9 32.5 %copy-start.7 = (bf16[256,896]{1,0:T(8,128)(2,1)}, bf16[256,896]{1,0:T(8,128)(2,1)S(1)}, u32[]{:S(2)}) copy-start(bf16[256,896]{1,0:T(8,128)(2,1)S(1)} %collective-permute-done.2.refs_3_) | copy-start | bytes 1376260
  64.9 14.3 %collective-permute-start.4 = (bf16[256,896]{1,0:T(8,128)(2,1)S(1)}, bf16[256,896]{1,0:T(8,128)(2,1)}, u32[]{:S(2)}, u32[]{:S(2)}) collective-permute-start(bf16[256,896]{1,0:T(8,128)(2,1)S(1)} %collective-permute-done.2.refs_3_), channel_id=1, source_target_pairs={{0,64},{64,128},{128,192},{192,256},{256,320},{320,384},{384,448},... | collective-permute-start | bytes 1376264 | tf_op jit(solution)/shard_map/ppermute | solution.py:152
  67.4 19.7 %collective-permute-start.13 = (bf16[256,896]{1,0:T(8,128)(2,1)}, bf16[256,896]{1,0:T(8,128)(2,1)}, u32[]{:S(2)}, u32[]{:S(2)}) collective-permute-start(bf16[256,896]{1,0:T(8,128)(2,1)} %collective-permute-done.11.refs_5_), channel_id=1, source_target_pairs={{0,64},{64,128},{128,192},{192,256},{256,320},{320,384},{384,448},... | collective-permute-start | bytes 1376264 | tf_op jit(solution)/shard_map/ppermute | solution.py:155
  87.1 10.4 %collective-permute-start.6 = (bf16[256,896]{1,0:T(8,128)(2,1)}, bf16[256,896]{1,0:T(8,128)(2,1)}, u32[]{:S(2)}, u32[]{:S(2)}) collective-permute-start(bf16[256,896]{1,0:T(8,128)(2,1)} %collective-permute-done.5.refs_6_), channel_id=1, source_target_pairs={{0,448},{64,0},{128,64},{192,128},{256,192},{320,256},{384,320},{4... | collective-permute-start | bytes 1376264 | tf_op jit(solution)/shard_map/ppermute | solution.py:155
  97.5 13.1 %all-to-all-start = ((bf16[4,128,896]{2,1,0:T(8,128)(2,1)}), bf16[4,128,896]{2,1,0:T(8,128)(2,1)S(1)}, u32[]{:S(2)}, u32[]{:S(2)}) async-start(bf16[4,128,896]{2,1,0:T(8,128)(2,1)} %bitcast.17), calls=%async_computation | async-start | bytes 1835008 | tf_op jit(solution)/shard_map/all_to_all | solution.py:176
  110.6 12.6 %all-to-all-start.1 = ((bf16[4,128,896]{2,1,0:T(8,128)(2,1)}), bf16[4,128,896]{2,1,0:T(8,128)(2,1)S(1)}, u32[]{:S(2)}, u32[]{:S(2)}) async-start(bf16[4,128,896]{2,1,0:T(8,128)(2,1)} %bitcast.16), calls=%async_computation.1 | async-start | bytes 1835008 | tf_op jit(solution)/shard_map/all_to_all | solution.py:176
  142.0 2.0 %copy-start = (bf16[896,2048]{1,0:T(8,128)(2,1)S(1)}, bf16[896,2048]{1,0:T(8,128)(2,1)}, u32[]{:S(2)}) copy-start(bf16[896,2048]{1,0:T(8,128)(2,1)} %all-gather.5.cloned.1.call-done.down) | copy-start | bytes 11010052
  147.9 9.2 %collective-permute-start.14 = (f32[256,2048]{1,0:T(8,128)S(1)}, f32[256,2048]{1,0:T(8,128)S(1)}, u32[]{:S(2)}, u32[]{:S(2)}) collective-permute-start(f32[256,2048]{1,0:T(8,128)S(1)} %get-tuple-element.18), channel_id=1, source_target_pairs={{0,4},{4,0},{8,12},{12,8},{16,20},{20,16},{24,28},{28,24},{32,36},... | collective-permute-start | bytes 6291464 | tf_op jit(solution)/shard_map/ppermute | solution.py:189
Sparse Core Ops, SparseCore 0:
  9.5 47.9 all-gather.2
  87.2 54.7 all-gather.4

commit v4 on v3

--- a/solution.py
+++ b/solution.py
@@ -100,45 +100,40 @@
     )(jnp.stack(place).astype(jnp.int32), keep, tokens, *arrays)
 
 
-def second_kernel(share, place, hidden, down, out_own, out_other, held, weight, sems):
+def second_kernel(share, side, place, hidden, down, out, held, weight, sems):
     width = down.shape[1] // sems.shape[0]
     copies = []
     for j in range(sems.shape[0]):
         columns = pl.ds(j * width, width)
         copies.append(pltpu.make_async_copy(down.at[:, columns], weight.at[:, columns], sems.at[j]))
         copies[j].start()
-    half = out_own.shape[0]
-    for y in range(half // share):
-        for core in range(2):
-            spot = lax.rem(core + place[0], 2) * half + y * share
-            held[pl.ds(pl.multiple_of(spot, share), share), :] = hidden[pl.ds((2 * y + core) * share, share), :]
+    core = lax.rem(place[0] + side, 2)
+    for y in range(out.shape[0] // share):
+        spot = pl.multiple_of((2 * y + core) * share, share)
+        held[pl.ds(y * share, share), :] = hidden[pl.ds(spot, share), :]
     for j, copy in enumerate(copies):
         copy.wait()
         columns = pl.ds(j * width, width)
-        for t, out in enumerate((out_own, out_other)):
-            out[:, columns] = jnp.dot(
-                held[pl.ds(t * half, half), :], weight[:, columns], preferred_element_type=jnp.float32
-            )
-
-
-def second_product(hidden, down, share):
+        out[:, columns] = jnp.dot(held[...], weight[:, columns], preferred_element_type=jnp.float32)
+
+
+def second_product(hidden, down, share, side):
     count = hidden.shape[0]
     units, features = down.shape
     core = lax.rem(lax.axis_index("col"), 2).reshape((1,)).astype(jnp.int32)
-    half = jax.ShapeDtypeStruct((count // 2, features), jnp.float32)
     return pl.pallas_call(
-        functools.partial(second_kernel, share),
-        out_shape=(half, half),
+        functools.partial(second_kernel, share, side),
+        out_shape=jax.ShapeDtypeStruct((count // 2, features), jnp.float32),
         in_specs=[IN_SMEM, IN_VMEM, ANYWHERE],
-        out_specs=(IN_VMEM, IN_VMEM),
+        out_specs=IN_VMEM,
         scratch_shapes=[
-            pltpu.VMEM((count, units), jnp.bfloat16),
+            pltpu.VMEM((count // 2, units), jnp.bfloat16),
             pltpu.VMEM((units, features), jnp.bfloat16),
             pltpu.SemaphoreType.DMA((4,)),
         ],
         compiler_params=pltpu.CompilerParams(vmem_limit_bytes=SECOND_VMEM),
         cost_estimate=pl.CostEstimate(
-            flops=2 * count * features * units, bytes_accessed=9 * 1024 * 1024, transcendentals=0
+            flops=count * features * units, bytes_accessed=6 * 1024 * 1024, transcendentals=0
         ),
         name="second",
     )(core, hidden, down)
@@ -185,8 +180,8 @@
     hidden = (jax.nn.silu(gate) * up).astype(jnp.bfloat16)
     hidden = lax.all_gather(hidden, "depth", axis=0, tiled=True)
 
-    mine, theirs = second_product(hidden, down, tokens.shape[0])
-    mine = mine + lax.ppermute(theirs, "col", swap)
+    theirs = lax.ppermute(second_product(hidden, down, tokens.shape[0], 1), "col", swap)
+    mine = second_product(hidden, down, tokens.shape[0], 0) + theirs
     mine = mine.astype(jnp.bfloat16).reshape((col_size // 2,) + tokens.shape)
     mixed = lax.all_to_all(mine, "col", 0, 0, axis_index_groups=same_core, tiled=True)
     return jnp.sum(mixed.astype(jnp.float32), 0).astype(jnp.bfloat16)

time: 201 us -> 199 us (0.990)
  waiting for transfers between devices: 46.9 us -> 43.9 us
    ppermute x1, waiting for transfers between devices: 3.76 us -> 1.02 us  [on_device(): lax.ppermute(second_product(hidden, down, tokens.shape[0], 1), 'col', swap)]
    pallas_call x1 -> x2, Pallas kernels: 3.86 us -> 5.48 us  [second_product(): pl.pallas_call(functools.partial(second_kernel, share, side), out_shape=j...]
  transfers between devices with their start and end apart: 19 -> 19, of which waited for: 11 -> 11; matrix products, arithmetic and copies ran while one was open for 2% -> 2% of each run, Pallas kernels for 8% -> 10%
where the time goes in v4:
time: 199 us
  starting transfers between devices  64.5 us (32%)
  blocking collectives  47.6 us (24%)
  waiting for transfers between devices  43.9 us (22%)
  Pallas kernels  22.4 us (11%)
  between operations  13.7 us (7%)
  local copies, waits for them, and re-layouts  4.22 us (2%)
  other arithmetic  2.16 us (1%)
    all_to_all x1, blocking collectives, on_device(): lax.all_to_all(mine, 'col', 0, 0, axis_index_groups=same_core, tiled=True)  34.5 us
    ppermute x6, starting transfers between devices, gather_ring(): behind = lax.ppermute(behind, axis, ring(size, -1))  32.4 us
    ppermute x6, starting transfers between devices, gather_ring(): ahead = lax.ppermute(ahead, axis, ring(size, 1))  14.4 us
    pallas_call x2, Pallas kernels, product(): pl.pallas_call(product_kernel, out_shape=jax.ShapeDtypeStruct((count, uni...  14 us
    ppermute x6, waiting for transfers between devices, gather_ring(): behind = lax.ppermute(behind, axis, ring(size, -1))  13.6 us
    all_gather x1, blocking collectives, on_device(): hidden = lax.all_gather(hidden, 'depth', axis=0, tiled=True)  13 us
    all_to_all x2, waiting for transfers between devices, exchange(): lax.all_to_all(share.reshape((depth_size, -1, units)), 'depth', 0, 0, til...  11 us
    ppermute x2, waiting for transfers between devices, gather_ring(): lax.ppermute(ahead if way > 0 else behind, axis, ring(size, way))  7.76 us
  transfers between devices with their start and end apart: 19, of which 11 were waited for; matrix products, arithmetic and copies ran while one was open for 2% of the time, Pallas kernels for 10%

profile of v4, /device:TPU:1, one launch (start us, length us, event | category | flops | bytes accessed | tf_op | source)
XLA Modules:
  0.0 198.5 jit_solution(15229652428432570135)
XLA Ops:
  6.5 0.7 all-gather.3.cloned.1.call-update
  7.3 0.0 all-gather.5.cloned.1.call-start
  7.3 4.8 %collective-permute-start.7 = (bf16[256,896]{1,0:T(8,128)(2,1)}, bf16[256,896]{1,0:T(8,128)(2,1)S(1)}, u32[]{:S(2)}, u32[]{:S(2)}) collective-permute-start(bf16[256,896]{1,0:T(8,128)(2,1)} %refs_0_.2), channel_id=1, source_target_pairs={{0,64},{64,128},{128,192},{192,256},{256,320},{320,384},{384,448},... | collective-permute-start | bytes 1376264 | tf_op jit(solution)/shard_map/ppermute | solution.py:147
  12.1 8.6 %collective-permute-start.8 = (bf16[256,896]{1,0:T(8,128)(2,1)}, bf16[256,896]{1,0:T(8,128)(2,1)S(1)}, u32[]{:S(2)}, u32[]{:S(2)}) collective-permute-start(bf16[256,896]{1,0:T(8,128)(2,1)} %refs_0_.2), channel_id=1, source_target_pairs={{0,448},{64,0},{128,64},{192,128},{256,192},{320,256},{384,320},{4... | collective-permute-start | bytes 1376264 | tf_op jit(solution)/shard_map/ppermute | solution.py:148
  20.7 3.4 %collective-permute-start.1 = (bf16[256,896]{1,0:T(8,128)(2,1)}, bf16[256,896]{1,0:T(8,128)(2,1)S(1)}, u32[]{:S(2)}, u32[]{:S(2)}) collective-permute-start(bf16[256,896]{1,0:T(8,128)(2,1)} %refs_0_.3), channel_id=1, source_target_pairs={{0,448},{64,0},{128,64},{192,128},{256,192},{320,256},{384,320},{4... | collective-permute-start | bytes 1376264 | tf_op jit(solution)/shard_map/ppermute | solution.py:148
  24.1 1.9 collective-permute-start
  26.0 3.2 %collective-permute-done.7.refs_1_ = bf16[256,896]{1,0:T(8,128)(2,1)S(1)} collective-permute-done((bf16[256,896]{1,0:T(8,128)(2,1)}, bf16[256,896]{1,0:T(8,128)(2,1)S(1)}, u32[]{:S(2)}, u32[]{:S(2)}) %collective-permute-start.7) | collective-permute-done | bytes 458784 | tf_op jit(solution)/shard_map/ppermute | solution.py:147
  29.3 1.9 collective-permute-start.9
  31.2 0.0 collective-permute-done.8.refs_2_
  31.2 4.6 %collective-permute-start.10 = (bf16[256,896]{1,0:T(8,128)(2,1)S(1)}, bf16[256,896]{1,0:T(8,128)(2,1)}, u32[]{:S(2)}, u32[]{:S(2)}) collective-permute-start(bf16[256,896]{1,0:T(8,128)(2,1)S(1)} %collective-permute-done.8.refs_2_), channel_id=1, source_target_pairs={{0,448},{64,0},{128,64},{192,128},{256,192},{320,256},{384,320},{4... | collective-permute-start | bytes 1376264 | tf_op jit(solution)/shard_map/ppermute | solution.py:148
  35.8 4.3 %collective-permute-done.1.refs_2_ = bf16[256,896]{1,0:T(8,128)(2,1)S(1)} collective-permute-done((bf16[256,896]{1,0:T(8,128)(2,1)}, bf16[256,896]{1,0:T(8,128)(2,1)S(1)}, u32[]{:S(2)}, u32[]{:S(2)}) %collective-permute-start.1) | collective-permute-done | bytes 458784 | tf_op jit(solution)/shard_map/ppermute | solution.py:148
  40.1 5.2 %collective-permute-start.3 = (bf16[256,896]{1,0:T(8,128)(2,1)S(1)}, bf16[256,896]{1,0:T(8,128)(2,1)S(1)}, u32[]{:S(2)}, u32[]{:S(2)}) collective-permute-start(bf16[256,896]{1,0:T(8,128)(2,1)S(1)} %collective-permute-done.1.refs_2_), channel_id=1, source_target_pairs={{0,448},{64,0},{128,64},{192,128},{256,192},{320,256},{384,320},{4... | collective-permute-start | bytes 1376264 | tf_op jit(solution)/shard_map/ppermute | solution.py:148
  45.3 1.9 collective-permute-start.2
  47.2 0.6 collective-permute-done.9.refs_3_
  47.9 1.9 collective-permute-start.11
  49.8 5.4 %collective-permute-start.12 = (bf16[256,896]{1,0:T(8,128)(2,1)}, bf16[256,896]{1,0:T(8,128)(2,1)}, u32[]{:S(2)}, u32[]{:S(2)}) collective-permute-start(bf16[256,896]{1,0:T(8,128)(2,1)} %collective-permute-done.10.refs_4_), channel_id=1, source_target_pairs={{0,448},{64,0},{128,64},{192,128},{256,192},{320,256},{384,320},{4... | collective-permute-start | bytes 1376264 | tf_op jit(solution)/shard_map/ppermute | solution.py:148
  55.2 4.4 %collective-permute-done.3.refs_4_ = bf16[256,896]{1,0:T(8,128)(2,1)S(1)} collective-permute-done((bf16[256,896]{1,0:T(8,128)(2,1)S(1)}, bf16[256,896]{1,0:T(8,128)(2,1)S(1)}, u32[]{:S(2)}, u32[]{:S(2)}) %collective-permute-start.3) | collective-permute-done | bytes 458784 | tf_op jit(solution)/shard_map/ppermute | solution.py:148
  59.6 5.3 %collective-permute-start.5 = (bf16[256,896]{1,0:T(8,128)(2,1)S(1)}, bf16[256,896]{1,0:T(8,128)(2,1)}, u32[]{:S(2)}, u32[]{:S(2)}) collective-permute-start(bf16[256,896]{1,0:T(8,128)(2,1)S(1)} %collective-permute-done.3.refs_4_), channel_id=1, source_target_pairs={{0,448},{64,0},{128,64},{192,128},{256,192},{320,256},{384,320},{4... | collective-permute-start | bytes 1376264 | tf_op jit(solution)/shard_map/ppermute | solution.py:148
  64.9 1.9 collective-permute-start.4
  66.9 0.5 collective-permute-done.11.refs_5_
  67.4 1.9 collective-permute-start.13
  69.3 1.5 copy.8.keep_ref
  70.8 0.7 pad_add_fusion.place
  71.4 2.9 %mask.1 = bf16[112,2048]{1,0:T(8,128)(2,1)} custom-call(s32[2]{0:T(128)} %pad_add_fusion.place, s32[112,64]{1,0:T(8,128)} %copy.8.keep_ref, bf16[112,2048]{1,0:T(8,128)(2,1)} %weight.1), custom_call_target="tpu_custom_call" | custom-call | flops 229376 | bytes 917504 | tf_op jit(solution)/shard_map/mask/pallas_call | solution.py:39
  74.4 4.9 %collective-permute-done.5.refs_6_ = bf16[256,896]{1,0:T(8,128)(2,1)} collective-permute-done((bf16[256,896]{1,0:T(8,128)(2,1)S(1)}, bf16[256,896]{1,0:T(8,128)(2,1)}, u32[]{:S(2)}, u32[]{:S(2)}) %collective-permute-start.5) | collective-permute-done | bytes 458784 | tf_op jit(solution)/shard_map/ppermute | solution.py:148
  79.3 7.8 %collective-permute-done.13.refs_7_ = bf16[256,896]{1,0:T(8,128)(2,1)} collective-permute-done((bf16[256,896]{1,0:T(8,128)(2,1)}, bf16[256,896]{1,0:T(8,128)(2,1)}, u32[]{:S(2)}, u32[]{:S(2)}) %collective-permute-start.13) | collective-permute-done | bytes 458784 | tf_op jit(solution)/shard_map/ppermute | solution.py:150
  87.0 0.0 all-gather.5.cloned.1.call-update
  87.1 2.8 %collective-permute-start.6 = (bf16[256,896]{1,0:T(8,128)(2,1)}, bf16[256,896]{1,0:T(8,128)(2,1)}, u32[]{:S(2)}, u32[]{:S(2)}) collective-permute-start(bf16[256,896]{1,0:T(8,128)(2,1)} %collective-permute-done.5.refs_6_), channel_id=1, source_target_pairs={{0,448},{64,0},{128,64},{192,128},{256,192},{320,256},{384,320},{4... | collective-permute-start | bytes 1376264 | tf_op jit(solution)/shard_map/ppermute | solution.py:150
  89.8 0.7 stack.61.place
  90.5 7.0 %gate.1 = bf16[512,896]{1,0:T(8,128)(2,1)} custom-call(s32[10]{0:T(128)} %stack.61.place, s32[64,112]{1,0:T(8,128)} %keep_ref.3, bf16[512,2048]{1,0:T(8,128)(2,1)} %all-gather.3.cloned.1.call-done.tokens, bf16[256,896]{1,0:T(8,128)(2,1)} %refs_0_.2, bf16[256,896]{1,0:T(8,128)(2,1)} %copy-done.3, bf16[256,896]{1,0:T(8,128)(2,1)} %copy-done.4, ...), custom_call_target="tpu_custom_call" | custom-call | flops 1879048192 | bytes 3670016 | tf_op jit(solution)/shard_map/gate/pallas_call | solution.py:86
  97.6 4.0 %all-to-all-start = ((bf16[4,128,896]{2,1,0:T(8,128)(2,1)}), bf16[4,128,896]{2,1,0:T(8,128)(2,1)S(1)}, u32[]{:S(2)}, u32[]{:S(2)}) async-start(bf16[4,128,896]{2,1,0:T(8,128)(2,1)} %bitcast.17), calls=%async_computation | async-start | bytes 1835008 | tf_op jit(solution)/shard_map/all_to_all | solution.py:171
  101.6 7.0 %up.1 = bf16[512,896]{1,0:T(8,128)(2,1)} custom-call(s32[10]{0:T(128)} %stack.61.place, s32[64,112]{1,0:T(8,128)} %keep_ref.4, bf16[512,2048]{1,0:T(8,128)(2,1)} %all-gather.3.cloned.1.call-done.tokens, bf16[256,896]{1,0:T(8,128)(2,1)} %refs_0_.3, bf16[256,896]{1,0:T(8,128)(2,1)} %copy-done.2, bf16[256,896]{1,0:T(8,128)(2,1)} %copy-done.1, ...), custom_call_target="tpu_custom_call" | custom-call | flops 1879048192 | bytes 3670016 | tf_op jit(solution)/shard_map/up/pallas_call | solution.py:86
  108.6 2.1 %all-to-all-done = bf16[4,128,896]{2,1,0:T(8,128)(2,1)S(1)} async-done(((bf16[4,128,896]{2,1,0:T(8,128)(2,1)}), bf16[4,128,896]{2,1,0:T(8,128)(2,1)S(1)}, u32[]{:S(2)}, u32[]{:S(2)}) %all-to-all-start) | async-done | bytes 917536 | tf_op jit(solution)/shard_map/all_to_all | solution.py:171
  110.7 3.5 %all-to-all-start.1 = ((bf16[4,128,896]{2,1,0:T(8,128)(2,1)}), bf16[4,128,896]{2,1,0:T(8,128)(2,1)S(1)}, u32[]{:S(2)}, u32[]{:S(2)}) async-start(bf16[4,128,896]{2,1,0:T(8,128)(2,1)} %bitcast.16), calls=%async_computation.1 | async-start | bytes 1835008 | tf_op jit(solution)/shard_map/all_to_all | solution.py:171
  114.2 0.1 convert_reduce_fusion.1
  114.3 8.9 %all-to-all-done.1 = bf16[4,128,896]{2,1,0:T(8,128)(2,1)S(1)} async-done(((bf16[4,128,896]{2,1,0:T(8,128)(2,1)}), bf16[4,128,896]{2,1,0:T(8,128)(2,1)S(1)}, u32[]{:S(2)}, u32[]{:S(2)}) %all-to-all-start.1) | async-done | bytes 917536 | tf_op jit(solution)/shard_map/all_to_all | solution.py:171
  123.2 0.1 convert_reduce_fusion
  123.4 0.1 multiply_convert_fusion
  123.5 13.0 %all_gather.10.hidden = bf16[512,896]{1,0:T(8,128)(2,1)S(1)} all-gather(bf16[128,896]{1,0:T(8,128)(2,1)S(1)} %multiply_convert_fusion), channel_id=1, replica_groups=mesh['row'=8,'col'=16,'depth'=4] {'depth'}, dimensions={0}, use_global_device_ids=true | all-gather | bytes 1146880 | tf_op jit(solution)/shard_map/all_gather | solution.py:181
  136.5 5.5 %all-gather.5.cloned.1.call-done.down = bf16[896,2048]{1,0:T(8,128)(2,1)} async-done(((bf16[112,2048]{1,0:T(8,128)(2,1)}), bf16[896,2048]{1,0:T(8,128)(2,1)}) %all-gather.5.cloned.1.call-update) | async-done | bytes 3670032 | tf_op jit(solution)/shard_map/all_gather | solution.py:168
  142.0 2.0 %copy-done = bf16[896,2048]{1,0:T(8,128)(2,1)S(1)} copy-done((bf16[896,2048]{1,0:T(8,128)(2,1)S(1)}, bf16[896,2048]{1,0:T(8,128)(2,1)}, u32[]{:S(2)}) %copy-start) | copy-done | bytes 3670040
  144.0 2.7 %second.3 = f32[256,2048]{1,0:T(8,128)S(1)} custom-call(s32[1]{0:T(128)} %bitcast.place, bf16[512,896]{1,0:T(8,128)(2,1)S(1)} %all_gather.10.hidden, bf16[896,2048]{1,0:T(8,128)(2,1)S(1)} %copy-done), custom_call_target="tpu_custom_call" | custom-call | flops 939524096 | bytes 6291456 | tf_op jit(solution)/shard_map/second/pallas_call | solution.py:124
  146.8 5.4 %collective-permute-start.14 = (f32[256,2048]{1,0:T(8,128)S(1)}, f32[256,2048]{1,0:T(8,128)S(1)}, u32[]{:S(2)}, u32[]{:S(2)}) collective-permute-start(f32[256,2048]{1,0:T(8,128)S(1)} %second.3), channel_id=1, source_target_pairs={{0,4},{4,0},{8,12},{12,8},{16,20},{20,16},{24,28},{28,24},{32,36},... | collective-permute-start | bytes 6291464 | tf_op jit(solution)/shard_map/ppermute | solution.py:183
  152.2 2.7 %second.2 = f32[256,2048]{1,0:T(8,128)S(1)} custom-call(s32[1]{0:T(128)} %bitcast.place, bf16[512,896]{1,0:T(8,128)(2,1)S(1)} %all_gather.10.hidden, bf16[896,2048]{1,0:T(8,128)(2,1)S(1)} %copy-done), custom_call_target="tpu_custom_call" | custom-call | flops 939524096 | bytes 6291456 | tf_op jit(solution)/shard_map/second/pallas_call | solution.py:124
  155.0 1.0 collective-permute-done.14
  156.0 0.3 add_convert_fusion
  156.3 34.5 %all_to_all.15 = bf16[8,32,2048]{2,1,0:T(8,128)(2,1)S(1)} all-to-all(bf16[8,32,2048]{2,1,0:T(8,128)(2,1)S(1)} %bitcast.15), channel_id=1, replica_groups={{0,8,16,24,32,40,48,56},{4,12,20,28,36,44,52,60},{1,9,17,25,33,41,49,57..., dimensions={0} | all-to-all | bytes 2097152 | tf_op jit(solution)/shard_map/all_to_all | solution.py:186
  190.9 0.8 reduce_sum.32
  (23 shorter events, 0.0 us)
Async XLA Ops:
  6.5 84.0 %all-gather.3.cloned.1.call-start = ((), (), s32[]{:S(2)}) async-start(), calls=%async_computation.3 | async-start | bytes 2228224 | tf_op jit(solution)/shard_map/all_gather | solution.py:163
  7.3 134.7 %all-gather.5.cloned.1.call-start = ((), (), s32[]{:S(2)}) async-start(), calls=%async_computation.4 | async-start | bytes 4128768 | tf_op jit(solution)/shard_map/all_gather | solution.py:168
  7.3 21.9 %collective-permute-start.7 = (bf16[256,896]{1,0:T(8,128)(2,1)}, bf16[256,896]{1,0:T(8,128)(2,1)S(1)}, u32[]{:S(2)}, u32[]{:S(2)}) collective-permute-start(bf16[256,896]{1,0:T(8,128)(2,1)} %refs_0_.2), channel_id=1, source_target_pairs={{0,64},{64,128},{128,192},{192,256},{256,320},{320,384},{384,448},... | collective-permute-start | bytes 1376264 | tf_op jit(solution)/shard_map/ppermute | solution.py:147
  12.1 19.0 %collective-permute-start.8 = (bf16[256,896]{1,0:T(8,128)(2,1)}, bf16[256,896]{1,0:T(8,128)(2,1)S(1)}, u32[]{:S(2)}, u32[]{:S(2)}) collective-permute-start(bf16[256,896]{1,0:T(8,128)(2,1)} %refs_0_.2), channel_id=1, source_target_pairs={{0,448},{64,0},{128,64},{192,128},{256,192},{320,256},{384,320},{4... | collective-permute-start | bytes 1376264 | tf_op jit(solution)/shard_map/ppermute | solution.py:148
  20.7 19.3 %collective-permute-start.1 = (bf16[256,896]{1,0:T(8,128)(2,1)}, bf16[256,896]{1,0:T(8,128)(2,1)S(1)}, u32[]{:S(2)}, u32[]{:S(2)}) collective-permute-start(bf16[256,896]{1,0:T(8,128)(2,1)} %refs_0_.3), channel_id=1, source_target_pairs={{0,448},{64,0},{128,64},{192,128},{256,192},{320,256},{384,320},{4... | collective-permute-start | bytes 1376264 | tf_op jit(solution)/shard_map/ppermute | solution.py:148
  24.1 21.2 %collective-permute-start = (bf16[256,896]{1,0:T(8,128)(2,1)}, bf16[256,896]{1,0:T(8,128)(2,1)S(1)}, u32[]{:S(2)}, u32[]{:S(2)}) collective-permute-start(bf16[256,896]{1,0:T(8,128)(2,1)} %refs_0_.3), channel_id=1, source_target_pairs={{0,64},{64,128},{128,192},{192,256},{256,320},{320,384},{384,448},... | collective-permute-start | bytes 1376264 | tf_op jit(solution)/shard_map/ppermute | solution.py:147
  29.2 61.3 %copy-start.3 = (bf16[256,896]{1,0:T(8,128)(2,1)}, bf16[256,896]{1,0:T(8,128)(2,1)S(1)}, u32[]{:S(2)}) copy-start(bf16[256,896]{1,0:T(8,128)(2,1)S(1)} %collective-permute-done.7.refs_1_) | copy-start | bytes 1376260
  29.3 18.6 %collective-permute-start.9 = (bf16[256,896]{1,0:T(8,128)(2,1)S(1)}, bf16[256,896]{1,0:T(8,128)(2,1)S(1)}, u32[]{:S(2)}, u32[]{:S(2)}) collective-permute-start(bf16[256,896]{1,0:T(8,128)(2,1)S(1)} %collective-permute-done.7.refs_1_), channel_id=1, source_target_pairs={{0,64},{64,128},{128,192},{192,256},{256,320},{320,384},{384,448},... | collective-permute-start | bytes 1376264 | tf_op jit(solution)/shard_map/ppermute | solution.py:147
  31.2 59.3 %copy-start.4 = (bf16[256,896]{1,0:T(8,128)(2,1)}, bf16[256,896]{1,0:T(8,128)(2,1)S(1)}, u32[]{:S(2)}) copy-start(bf16[256,896]{1,0:T(8,128)(2,1)S(1)} %collective-permute-done.8.refs_2_) | copy-start | bytes 1376260
  31.2 18.6 %collective-permute-start.10 = (bf16[256,896]{1,0:T(8,128)(2,1)S(1)}, bf16[256,896]{1,0:T(8,128)(2,1)}, u32[]{:S(2)}, u32[]{:S(2)}) collective-permute-start(bf16[256,896]{1,0:T(8,128)(2,1)S(1)} %collective-permute-done.8.refs_2_), channel_id=1, source_target_pairs={{0,448},{64,0},{128,64},{192,128},{256,192},{320,256},{384,320},{4... | collective-permute-start | bytes 1376264 | tf_op jit(solution)/shard_map/ppermute | solution.py:148
  40.1 57.5 %copy-start.1 = (bf16[256,896]{1,0:T(8,128)(2,1)}, bf16[256,896]{1,0:T(8,128)(2,1)S(1)}, u32[]{:S(2)}) copy-start(bf16[256,896]{1,0:T(8,128)(2,1)S(1)} %collective-permute-done.1.refs_2_) | copy-start | bytes 1376260
  40.1 19.6 %collective-permute-start.3 = (bf16[256,896]{1,0:T(8,128)(2,1)S(1)}, bf16[256,896]{1,0:T(8,128)(2,1)S(1)}, u32[]{:S(2)}, u32[]{:S(2)}) collective-permute-start(bf16[256,896]{1,0:T(8,128)(2,1)S(1)} %collective-permute-done.1.refs_2_), channel_id=1, source_target_pairs={{0,448},{64,0},{128,64},{192,128},{256,192},{320,256},{384,320},{4... | collective-permute-start | bytes 1376264 | tf_op jit(solution)/shard_map/ppermute | solution.py:148
  45.3 52.2 %copy-start.2 = (bf16[256,896]{1,0:T(8,128)(2,1)}, bf16[256,896]{1,0:T(8,128)(2,1)S(1)}, u32[]{:S(2)}) copy-start(bf16[256,896]{1,0:T(8,128)(2,1)S(1)} %collective-permute-done.refs_1_) | copy-start | bytes 1376260
  45.3 19.6 %collective-permute-start.2 = (bf16[256,896]{1,0:T(8,128)(2,1)S(1)}, bf16[256,896]{1,0:T(8,128)(2,1)S(1)}, u32[]{:S(2)}, u32[]{:S(2)}) collective-permute-start(bf16[256,896]{1,0:T(8,128)(2,1)S(1)} %collective-permute-done.refs_1_), channel_id=1, source_target_pairs={{0,64},{64,128},{128,192},{192,256},{256,320},{320,384},{384,448},... | collective-permute-start | bytes 1376264 | tf_op jit(solution)/shard_map/ppermute | solution.py:147
  47.9 42.7 %copy-start.6 = (bf16[256,896]{1,0:T(8,128)(2,1)}, bf16[256,896]{1,0:T(8,128)(2,1)S(1)}, u32[]{:S(2)}) copy-start(bf16[256,896]{1,0:T(8,128)(2,1)S(1)} %collective-permute-done.9.refs_3_) | copy-start | bytes 1376260
  47.9 19.5 %collective-permute-start.11 = (bf16[256,896]{1,0:T(8,128)(2,1)S(1)}, bf16[256,896]{1,0:T(8,128)(2,1)}, u32[]{:S(2)}, u32[]{:S(2)}) collective-permute-start(bf16[256,896]{1,0:T(8,128)(2,1)S(1)} %collective-permute-done.9.refs_3_), channel_id=1, source_target_pairs={{0,64},{64,128},{128,192},{192,256},{256,320},{320,384},{384,448},... | collective-permute-start | bytes 1376264 | tf_op jit(solution)/shard_map/ppermute | solution.py:147
  49.8 24.6 %collective-permute-start.12 = (bf16[256,896]{1,0:T(8,128)(2,1)}, bf16[256,896]{1,0:T(8,128)(2,1)}, u32[]{:S(2)}, u32[]{:S(2)}) collective-permute-start(bf16[256,896]{1,0:T(8,128)(2,1)} %collective-permute-done.10.refs_4_), channel_id=1, source_target_pairs={{0,448},{64,0},{128,64},{192,128},{256,192},{320,256},{384,320},{4... | collective-permute-start | bytes 1376264 | tf_op jit(solution)/shard_map/ppermute | solution.py:148
  59.6 37.9 %copy-start.5 = (bf16[256,896]{1,0:T(8,128)(2,1)}, bf16[256,896]{1,0:T(8,128)(2,1)S(1)}, u32[]{:S(2)}) copy-start(bf16[256,896]{1,0:T(8,128)(2,1)S(1)} %collective-permute-done.3.refs_4_) | copy-start | bytes 1376260
  59.6 19.7 %collective-permute-start.5 = (bf16[256,896]{1,0:T(8,128)(2,1)S(1)}, bf16[256,896]{1,0:T(8,128)(2,1)}, u32[]{:S(2)}, u32[]{:S(2)}) collective-permute-start(bf16[256,896]{1,0:T(8,128)(2,1)S(1)} %collective-permute-done.3.refs_4_), channel_id=1, source_target_pairs={{0,448},{64,0},{128,64},{192,128},{256,192},{320,256},{384,320},{4... | collective-permute-start | bytes 1376264 | tf_op jit(solution)/shard_map/ppermute | solution.py:148
  64.9 32.6 %copy-start.7 = (bf16[256,896]{1,0:T(8,128)(2,1)}, bf16[256,896]{1,0:T(8,128)(2,1)S(1)}, u32[]{:S(2)}) copy-start(bf16[256,896]{1,0:T(8,128)(2,1)S(1)} %collective-permute-done.2.refs_3_) | copy-start | bytes 1376260
  64.9 14.3 %collective-permute-start.4 = (bf16[256,896]{1,0:T(8,128)(2,1)S(1)}, bf16[256,896]{1,0:T(8,128)(2,1)}, u32[]{:S(2)}, u32[]{:S(2)}) collective-permute-start(bf16[256,896]{1,0:T(8,128)(2,1)S(1)} %collective-permute-done.2.refs_3_), channel_id=1, source_target_pairs={{0,64},{64,128},{128,192},{192,256},{256,320},{320,384},{384,448},... | collective-permute-start | bytes 1376264 | tf_op jit(solution)/shard_map/ppermute | solution.py:147
  67.4 19.7 %collective-permute-start.13 = (bf16[256,896]{1,0:T(8,128)(2,1)}, bf16[256,896]{1,0:T(8,128)(2,1)}, u32[]{:S(2)}, u32[]{:S(2)}) collective-permute-start(bf16[256,896]{1,0:T(8,128)(2,1)} %collective-permute-done.11.refs_5_), channel_id=1, source_target_pairs={{0,64},{64,128},{128,192},{192,256},{256,320},{320,384},{384,448},... | collective-permute-start | bytes 1376264 | tf_op jit(solution)/shard_map/ppermute | solution.py:150
  87.1 10.5 %collective-permute-start.6 = (bf16[256,896]{1,0:T(8,128)(2,1)}, bf16[256,896]{1,0:T(8,128)(2,1)}, u32[]{:S(2)}, u32[]{:S(2)}) collective-permute-start(bf16[256,896]{1,0:T(8,128)(2,1)} %collective-permute-done.5.refs_6_), channel_id=1, source_target_pairs={{0,448},{64,0},{128,64},{192,128},{256,192},{320,256},{384,320},{4... | collective-permute-start | bytes 1376264 | tf_op jit(solution)/shard_map/ppermute | solution.py:150
  97.6 13.1 %all-to-all-start = ((bf16[4,128,896]{2,1,0:T(8,128)(2,1)}), bf16[4,128,896]{2,1,0:T(8,128)(2,1)S(1)}, u32[]{:S(2)}, u32[]{:S(2)}) async-start(bf16[4,128,896]{2,1,0:T(8,128)(2,1)} %bitcast.17), calls=%async_computation | async-start | bytes 1835008 | tf_op jit(solution)/shard_map/all_to_all | solution.py:171
  110.7 12.6 %all-to-all-start.1 = ((bf16[4,128,896]{2,1,0:T(8,128)(2,1)}), bf16[4,128,896]{2,1,0:T(8,128)(2,1)S(1)}, u32[]{:S(2)}, u32[]{:S(2)}) async-start(bf16[4,128,896]{2,1,0:T(8,128)(2,1)} %bitcast.16), calls=%async_computation.1 | async-start | bytes 1835008 | tf_op jit(solution)/shard_map/all_to_all | solution.py:171
  142.0 2.0 %copy-start = (bf16[896,2048]{1,0:T(8,128)(2,1)S(1)}, bf16[896,2048]{1,0:T(8,128)(2,1)}, u32[]{:S(2)}) copy-start(bf16[896,2048]{1,0:T(8,128)(2,1)} %all-gather.5.cloned.1.call-done.down) | copy-start | bytes 11010052
  146.8 9.2 %collective-permute-start.14 = (f32[256,2048]{1,0:T(8,128)S(1)}, f32[256,2048]{1,0:T(8,128)S(1)}, u32[]{:S(2)}, u32[]{:S(2)}) collective-permute-start(f32[256,2048]{1,0:T(8,128)S(1)} %second.3), channel_id=1, source_target_pairs={{0,4},{4,0},{8,12},{12,8},{16,20},{20,16},{24,28},{28,24},{32,36},... | collective-permute-start | bytes 6291464 | tf_op jit(solution)/shard_map/ppermute | solution.py:183
Sparse Core Ops, SparseCore 0:
  9.5 47.9 all-gather.2
  87.2 54.7 all-gather.4

commit v5 on v4

--- a/solution.py
+++ b/solution.py
@@ -100,21 +100,15 @@
     )(jnp.stack(place).astype(jnp.int32), keep, tokens, *arrays)
 
 
-def second_kernel(share, side, place, hidden, down, out, held, weight, sems):
-    width = down.shape[1] // sems.shape[0]
-    copies = []
-    for j in range(sems.shape[0]):
-        columns = pl.ds(j * width, width)
-        copies.append(pltpu.make_async_copy(down.at[:, columns], weight.at[:, columns], sems.at[j]))
-        copies[j].start()
+def second_kernel(share, side, place, hidden, down, out, held):
+    width = 4 * BLOCK
     core = lax.rem(place[0] + side, 2)
     for y in range(out.shape[0] // share):
         spot = pl.multiple_of((2 * y + core) * share, share)
         held[pl.ds(y * share, share), :] = hidden[pl.ds(spot, share), :]
-    for j, copy in enumerate(copies):
-        copy.wait()
-        columns = pl.ds(j * width, width)
-        out[:, columns] = jnp.dot(held[...], weight[:, columns], preferred_element_type=jnp.float32)
+    for start in range(0, down.shape[1], width):
+        columns = pl.ds(start, width)
+        out[:, columns] = jnp.dot(held[...], down[:, columns], preferred_element_type=jnp.float32)
 
 
 def second_product(hidden, down, share, side):
@@ -124,12 +118,10 @@
     return pl.pallas_call(
         functools.partial(second_kernel, share, side),
         out_shape=jax.ShapeDtypeStruct((count // 2, features), jnp.float32),
-        in_specs=[IN_SMEM, IN_VMEM, ANYWHERE],
+        in_specs=[IN_SMEM, IN_VMEM, IN_VMEM],
         out_specs=IN_VMEM,
         scratch_shapes=[
             pltpu.VMEM((count // 2, units), jnp.bfloat16),
-            pltpu.VMEM((units, features), jnp.bfloat16),
-            pltpu.SemaphoreType.DMA((4,)),
         ],
         compiler_params=pltpu.CompilerParams(vmem_limit_bytes=SECOND_VMEM),
         cost_estimate=pl.CostEstimate(

time: 199 us -> 198 us (level)
  Pallas kernels: 22.4 us -> 19.4 us
    pallas_call x2, Pallas kernels: 5.48 us -> 2.5 us  [second_product(): pl.pallas_call(functools.partial(second_kernel, share, side), out_shape=j...]
  transfers between devices with their start and end apart: 19 -> 19, of which waited for: 11 -> 11; matrix products, arithmetic and copies ran while one was open for 2% -> 2% of each run, Pallas kernels for 10% -> 9%
where the time goes in v5:
time: 198 us; the launch traced here: 197 us
  starting transfers between devices  64.6 us (33%)
  blocking collectives  47.6 us (24%)
  waiting for transfers between devices  45.4 us (23%)
  Pallas kernels  19.4 us (10%)
  between operations  13.7 us (7%)
  local copies, waits for them, and re-layouts  4.22 us (2%)
  other arithmetic  2.16 us (1%)
    all_to_all x1, blocking collectives, on_device(): lax.all_to_all(mine, 'col', 0, 0, axis_index_groups=same_core, tiled=True)  34.5 us
    ppermute x6, starting transfers between devices, gather_ring(): behind = lax.ppermute(behind, axis, ring(size, -1))  32.4 us
    ppermute x6, starting transfers between devices, gather_ring(): ahead = lax.ppermute(ahead, axis, ring(size, 1))  14.4 us
    pallas_call x2, Pallas kernels, product(): pl.pallas_call(product_kernel, out_shape=jax.ShapeDtypeStruct((count, uni...  14 us
    ppermute x6, waiting for transfers between devices, gather_ring(): behind = lax.ppermute(behind, axis, ring(size, -1))  13.6 us
    all_gather x1, blocking collectives, on_device(): hidden = lax.all_gather(hidden, 'depth', axis=0, tiled=True)  13 us
    all_to_all x2, waiting for transfers between devices, exchange(): lax.all_to_all(share.reshape((depth_size, -1, units)), 'depth', 0, 0, til...  11 us
    ppermute x2, waiting for transfers between devices, gather_ring(): lax.ppermute(ahead if way > 0 else behind, axis, ring(size, way))  7.76 us
  transfers between devices with their start and end apart: 19, of which 11 were waited for; matrix products, arithmetic and copies ran while one was open for 2% of the time, Pallas kernels for 9%

profile of v5, /device:TPU:1, one launch (start us, length us, event | category | flops | bytes accessed | tf_op | source)
XLA Modules:
  0.0 197.0 jit_solution(15541878905594374038)
XLA Ops:
  6.5 0.7 all-gather.3.cloned.1.call-update
  7.3 0.0 all-gather.5.cloned.1.call-start
  7.3 4.8 %collective-permute-start.7 = (bf16[256,896]{1,0:T(8,128)(2,1)}, bf16[256,896]{1,0:T(8,128)(2,1)S(1)}, u32[]{:S(2)}, u32[]{:S(2)}) collective-permute-start(bf16[256,896]{1,0:T(8,128)(2,1)} %refs_0_.2), channel_id=1, source_target_pairs={{0,64},{64,128},{128,192},{192,256},{256,320},{320,384},{384,448},... | collective-permute-start | bytes 1376264 | tf_op jit(solution)/shard_map/ppermute | solution.py:139
  12.1 8.6 %collective-permute-start.8 = (bf16[256,896]{1,0:T(8,128)(2,1)}, bf16[256,896]{1,0:T(8,128)(2,1)S(1)}, u32[]{:S(2)}, u32[]{:S(2)}) collective-permute-start(bf16[256,896]{1,0:T(8,128)(2,1)} %refs_0_.2), channel_id=1, source_target_pairs={{0,448},{64,0},{128,64},{192,128},{256,192},{320,256},{384,320},{4... | collective-permute-start | bytes 1376264 | tf_op jit(solution)/shard_map/ppermute | solution.py:140
  20.7 3.4 %collective-permute-start.1 = (bf16[256,896]{1,0:T(8,128)(2,1)}, bf16[256,896]{1,0:T(8,128)(2,1)S(1)}, u32[]{:S(2)}, u32[]{:S(2)}) collective-permute-start(bf16[256,896]{1,0:T(8,128)(2,1)} %refs_0_.3), channel_id=1, source_target_pairs={{0,448},{64,0},{128,64},{192,128},{256,192},{320,256},{384,320},{4... | collective-permute-start | bytes 1376264 | tf_op jit(solution)/shard_map/ppermute | solution.py:140
  24.1 1.9 collective-permute-start
  26.0 3.2 %collective-permute-done.7.refs_1_ = bf16[256,896]{1,0:T(8,128)(2,1)S(1)} collective-permute-done((bf16[256,896]{1,0:T(8,128)(2,1)}, bf16[256,896]{1,0:T(8,128)(2,1)S(1)}, u32[]{:S(2)}, u32[]{:S(2)}) %collective-permute-start.7) | collective-permute-done | bytes 458784 | tf_op jit(solution)/shard_map/ppermute | solution.py:139
  29.3 1.9 collective-permute-start.9
  31.2 4.6 %collective-permute-start.10 = (bf16[256,896]{1,0:T(8,128)(2,1)S(1)}, bf16[256,896]{1,0:T(8,128)(2,1)}, u32[]{:S(2)}, u32[]{:S(2)}) collective-permute-start(bf16[256,896]{1,0:T(8,128)(2,1)S(1)} %collective-permute-done.8.refs_2_), channel_id=1, source_target_pairs={{0,448},{64,0},{128,64},{192,128},{256,192},{320,256},{384,320},{4... | collective-permute-start | bytes 1376264 | tf_op jit(solution)/shard_map/ppermute | solution.py:140
  35.8 4.3 %collective-permute-done.1.refs_2_ = bf16[256,896]{1,0:T(8,128)(2,1)S(1)} collective-permute-done((bf16[256,896]{1,0:T(8,128)(2,1)}, bf16[256,896]{1,0:T(8,128)(2,1)S(1)}, u32[]{:S(2)}, u32[]{:S(2)}) %collective-permute-start.1) | collective-permute-done | bytes 458784 | tf_op jit(solution)/shard_map/ppermute | solution.py:140
  40.1 5.2 %collective-permute-start.3 = (bf16[256,896]{1,0:T(8,128)(2,1)S(1)}, bf16[256,896]{1,0:T(8,128)(2,1)S(1)}, u32[]{:S(2)}, u32[]{:S(2)}) collective-permute-start(bf16[256,896]{1,0:T(8,128)(2,1)S(1)} %collective-permute-done.1.refs_2_), channel_id=1, source_target_pairs={{0,448},{64,0},{128,64},{192,128},{256,192},{320,256},{384,320},{4... | collective-permute-start | bytes 1376264 | tf_op jit(solution)/shard_map/ppermute | solution.py:140
  45.3 1.9 collective-permute-start.2
  47.2 0.6 collective-permute-done.9.refs_3_
  47.9 1.9 collective-permute-start.11
  49.8 5.4 %collective-permute-start.12 = (bf16[256,896]{1,0:T(8,128)(2,1)}, bf16[256,896]{1,0:T(8,128)(2,1)}, u32[]{:S(2)}, u32[]{:S(2)}) collective-permute-start(bf16[256,896]{1,0:T(8,128)(2,1)} %collective-permute-done.10.refs_4_), channel_id=1, source_target_pairs={{0,448},{64,0},{128,64},{192,128},{256,192},{320,256},{384,320},{4... | collective-permute-start | bytes 1376264 | tf_op jit(solution)/shard_map/ppermute | solution.py:140
  55.2 4.4 %collective-permute-done.3.refs_4_ = bf16[256,896]{1,0:T(8,128)(2,1)S(1)} collective-permute-done((bf16[256,896]{1,0:T(8,128)(2,1)S(1)}, bf16[256,896]{1,0:T(8,128)(2,1)S(1)}, u32[]{:S(2)}, u32[]{:S(2)}) %collective-permute-start.3) | collective-permute-done | bytes 458784 | tf_op jit(solution)/shard_map/ppermute | solution.py:140
  59.6 5.3 %collective-permute-start.5 = (bf16[256,896]{1,0:T(8,128)(2,1)S(1)}, bf16[256,896]{1,0:T(8,128)(2,1)}, u32[]{:S(2)}, u32[]{:S(2)}) collective-permute-start(bf16[256,896]{1,0:T(8,128)(2,1)S(1)} %collective-permute-done.3.refs_4_), channel_id=1, source_target_pairs={{0,448},{64,0},{128,64},{192,128},{256,192},{320,256},{384,320},{4... | collective-permute-start | bytes 1376264 | tf_op jit(solution)/shard_map/ppermute | solution.py:140
  64.9 1.9 collective-permute-start.4
  66.9 0.5 collective-permute-done.11.refs_5_
  67.4 1.9 collective-permute-start.13
  69.3 1.5 copy.8.keep_ref
  70.8 0.7 pad_add_fusion.place
  71.4 2.9 %mask.1 = bf16[112,2048]{1,0:T(8,128)(2,1)} custom-call(s32[2]{0:T(128)} %pad_add_fusion.place, s32[112,64]{1,0:T(8,128)} %copy.8.keep_ref, bf16[112,2048]{1,0:T(8,128)(2,1)} %weight.1), custom_call_target="tpu_custom_call" | custom-call | flops 229376 | bytes 917504 | tf_op jit(solution)/shard_map/mask/pallas_call | solution.py:39
  74.4 0.0 collective-permute-done.12.refs_6_
  74.4 4.9 %collective-permute-done.5.refs_6_ = bf16[256,896]{1,0:T(8,128)(2,1)} collective-permute-done((bf16[256,896]{1,0:T(8,128)(2,1)S(1)}, bf16[256,896]{1,0:T(8,128)(2,1)}, u32[]{:S(2)}, u32[]{:S(2)}) %collective-permute-start.5) | collective-permute-done | bytes 458784 | tf_op jit(solution)/shard_map/ppermute | solution.py:140
  79.3 7.8 %collective-permute-done.13.refs_7_ = bf16[256,896]{1,0:T(8,128)(2,1)} collective-permute-done((bf16[256,896]{1,0:T(8,128)(2,1)}, bf16[256,896]{1,0:T(8,128)(2,1)}, u32[]{:S(2)}, u32[]{:S(2)}) %collective-permute-start.13) | collective-permute-done | bytes 458784 | tf_op jit(solution)/shard_map/ppermute | solution.py:142
  87.0 0.0 all-gather.5.cloned.1.call-update
  87.1 2.8 %collective-permute-start.6 = (bf16[256,896]{1,0:T(8,128)(2,1)}, bf16[256,896]{1,0:T(8,128)(2,1)}, u32[]{:S(2)}, u32[]{:S(2)}) collective-permute-start(bf16[256,896]{1,0:T(8,128)(2,1)} %collective-permute-done.5.refs_6_), channel_id=1, source_target_pairs={{0,448},{64,0},{128,64},{192,128},{256,192},{320,256},{384,320},{4... | collective-permute-start | bytes 1376264 | tf_op jit(solution)/shard_map/ppermute | solution.py:142
  89.8 0.7 stack.61.place
  90.5 7.0 %gate.1 = bf16[512,896]{1,0:T(8,128)(2,1)} custom-call(s32[10]{0:T(128)} %stack.61.place, s32[64,112]{1,0:T(8,128)} %keep_ref.3, bf16[512,2048]{1,0:T(8,128)(2,1)} %all-gather.3.cloned.1.call-done.tokens, bf16[256,896]{1,0:T(8,128)(2,1)} %refs_0_.2, bf16[256,896]{1,0:T(8,128)(2,1)} %copy-done.3, bf16[256,896]{1,0:T(8,128)(2,1)} %copy-done.4, ...), custom_call_target="tpu_custom_call" | custom-call | flops 1879048192 | bytes 3670016 | tf_op jit(solution)/shard_map/gate/pallas_call | solution.py:86
  97.6 4.0 %all-to-all-start = ((bf16[4,128,896]{2,1,0:T(8,128)(2,1)}), bf16[4,128,896]{2,1,0:T(8,128)(2,1)S(1)}, u32[]{:S(2)}, u32[]{:S(2)}) async-start(bf16[4,128,896]{2,1,0:T(8,128)(2,1)} %bitcast.17), calls=%async_computation | async-start | bytes 1835008 | tf_op jit(solution)/shard_map/all_to_all | solution.py:163
  101.6 7.0 %up.1 = bf16[512,896]{1,0:T(8,128)(2,1)} custom-call(s32[10]{0:T(128)} %stack.61.place, s32[64,112]{1,0:T(8,128)} %keep_ref.4, bf16[512,2048]{1,0:T(8,128)(2,1)} %all-gather.3.cloned.1.call-done.tokens, bf16[256,896]{1,0:T(8,128)(2,1)} %refs_0_.3, bf16[256,896]{1,0:T(8,128)(2,1)} %copy-done.2, bf16[256,896]{1,0:T(8,128)(2,1)} %copy-done.1, ...), custom_call_target="tpu_custom_call" | custom-call | flops 1879048192 | bytes 3670016 | tf_op jit(solution)/shard_map/up/pallas_call | solution.py:86
  108.6 2.1 %all-to-all-done = bf16[4,128,896]{2,1,0:T(8,128)(2,1)S(1)} async-done(((bf16[4,128,896]{2,1,0:T(8,128)(2,1)}), bf16[4,128,896]{2,1,0:T(8,128)(2,1)S(1)}, u32[]{:S(2)}, u32[]{:S(2)}) %all-to-all-start) | async-done | bytes 917536 | tf_op jit(solution)/shard_map/all_to_all | solution.py:163
  110.7 3.5 %all-to-all-start.1 = ((bf16[4,128,896]{2,1,0:T(8,128)(2,1)}), bf16[4,128,896]{2,1,0:T(8,128)(2,1)S(1)}, u32[]{:S(2)}, u32[]{:S(2)}) async-start(bf16[4,128,896]{2,1,0:T(8,128)(2,1)} %bitcast.16), calls=%async_computation.1 | async-start | bytes 1835008 | tf_op jit(solution)/shard_map/all_to_all | solution.py:163
  114.2 0.1 convert_reduce_fusion.1
  114.3 8.9 %all-to-all-done.1 = bf16[4,128,896]{2,1,0:T(8,128)(2,1)S(1)} async-done(((bf16[4,128,896]{2,1,0:T(8,128)(2,1)}), bf16[4,128,896]{2,1,0:T(8,128)(2,1)S(1)}, u32[]{:S(2)}, u32[]{:S(2)}) %all-to-all-start.1) | async-done | bytes 917536 | tf_op jit(solution)/shard_map/all_to_all | solution.py:163
  123.2 0.1 convert_reduce_fusion
  123.4 0.1 multiply_convert_fusion
  123.5 13.0 %all_gather.10.hidden = bf16[512,896]{1,0:T(8,128)(2,1)S(1)} all-gather(bf16[128,896]{1,0:T(8,128)(2,1)S(1)} %multiply_convert_fusion), channel_id=1, replica_groups=mesh['row'=8,'col'=16,'depth'=4] {'depth'}, dimensions={0}, use_global_device_ids=true | all-gather | bytes 1146880 | tf_op jit(solution)/shard_map/all_gather | solution.py:173
  136.5 5.5 %all-gather.5.cloned.1.call-done.down = bf16[896,2048]{1,0:T(8,128)(2,1)} async-done(((bf16[112,2048]{1,0:T(8,128)(2,1)}), bf16[896,2048]{1,0:T(8,128)(2,1)}) %all-gather.5.cloned.1.call-update) | async-done | bytes 3670032 | tf_op jit(solution)/shard_map/all_gather | solution.py:160
  142.0 2.0 %copy-done = bf16[896,2048]{1,0:T(8,128)(2,1)S(1)} copy-done((bf16[896,2048]{1,0:T(8,128)(2,1)S(1)}, bf16[896,2048]{1,0:T(8,128)(2,1)}, u32[]{:S(2)}) %copy-start) | copy-done | bytes 3670040
  144.0 1.2 second.3
  145.3 5.5 %collective-permute-start.14 = (f32[256,2048]{1,0:T(8,128)S(1)}, f32[256,2048]{1,0:T(8,128)S(1)}, u32[]{:S(2)}, u32[]{:S(2)}) collective-permute-start(f32[256,2048]{1,0:T(8,128)S(1)} %second.3), channel_id=1, source_target_pairs={{0,4},{4,0},{8,12},{12,8},{16,20},{20,16},{24,28},{28,24},{32,36},... | collective-permute-start | bytes 6291464 | tf_op jit(solution)/shard_map/ppermute | solution.py:175
  150.7 1.3 second.2
  152.0 2.5 %collective-permute-done.14 = f32[256,2048]{1,0:T(8,128)S(1)} collective-permute-done((f32[256,2048]{1,0:T(8,128)S(1)}, f32[256,2048]{1,0:T(8,128)S(1)}, u32[]{:S(2)}, u32[]{:S(2)}) %collective-permute-start.14) | collective-permute-done | bytes 2097184 | tf_op jit(solution)/shard_map/ppermute | solution.py:175
  154.5 0.3 add_convert_fusion
  154.8 34.5 %all_to_all.15 = bf16[8,32,2048]{2,1,0:T(8,128)(2,1)S(1)} all-to-all(bf16[8,32,2048]{2,1,0:T(8,128)(2,1)S(1)} %bitcast.15), channel_id=1, replica_groups={{0,8,16,24,32,40,48,56},{4,12,20,28,36,44,52,60},{1,9,17,25,33,41,49,57..., dimensions={0} | all-to-all | bytes 2097152 | tf_op jit(solution)/shard_map/all_to_all | solution.py:178
  189.4 0.8 reduce_sum.32
  (23 shorter events, 0.0 us)
Async XLA Ops:
  6.5 84.0 %all-gather.3.cloned.1.call-start = ((), (), s32[]{:S(2)}) async-start(), calls=%async_computation.3 | async-start | bytes 2228224 | tf_op jit(solution)/shard_map/all_gather | solution.py:155
  7.3 134.7 %all-gather.5.cloned.1.call-start = ((), (), s32[]{:S(2)}) async-start(), calls=%async_computation.4 | async-start | bytes 4128768 | tf_op jit(solution)/shard_map/all_gather | solution.py:160
  7.3 21.9 %collective-permute-start.7 = (bf16[256,896]{1,0:T(8,128)(2,1)}, bf16[256,896]{1,0:T(8,128)(2,1)S(1)}, u32[]{:S(2)}, u32[]{:S(2)}) collective-permute-start(bf16[256,896]{1,0:T(8,128)(2,1)} %refs_0_.2), channel_id=1, source_target_pairs={{0,64},{64,128},{128,192},{192,256},{256,320},{320,384},{384,448},... | collective-permute-start | bytes 1376264 | tf_op jit(solution)/shard_map/ppermute | solution.py:139
  12.1 19.0 %collective-permute-start.8 = (bf16[256,896]{1,0:T(8,128)(2,1)}, bf16[256,896]{1,0:T(8,128)(2,1)S(1)}, u32[]{:S(2)}, u32[]{:S(2)}) collective-permute-start(bf16[256,896]{1,0:T(8,128)(2,1)} %refs_0_.2), channel_id=1, source_target_pairs={{0,448},{64,0},{128,64},{192,128},{256,192},{320,256},{384,320},{4... | collective-permute-start | bytes 1376264 | tf_op jit(solution)/shard_map/ppermute | solution.py:140
  20.7 19.3 %collective-permute-start.1 = (bf16[256,896]{1,0:T(8,128)(2,1)}, bf16[256,896]{1,0:T(8,128)(2,1)S(1)}, u32[]{:S(2)}, u32[]{:S(2)}) collective-permute-start(bf16[256,896]{1,0:T(8,128)(2,1)} %refs_0_.3), channel_id=1, source_target_pairs={{0,448},{64,0},{128,64},{192,128},{256,192},{320,256},{384,320},{4... | collective-permute-start | bytes 1376264 | tf_op jit(solution)/shard_map/ppermute | solution.py:140
  24.1 21.2 %collective-permute-start = (bf16[256,896]{1,0:T(8,128)(2,1)}, bf16[256,896]{1,0:T(8,128)(2,1)S(1)}, u32[]{:S(2)}, u32[]{:S(2)}) collective-permute-start(bf16[256,896]{1,0:T(8,128)(2,1)} %refs_0_.3), channel_id=1, source_target_pairs={{0,64},{64,128},{128,192},{192,256},{256,320},{320,384},{384,448},... | collective-permute-start | bytes 1376264 | tf_op jit(solution)/shard_map/ppermute | solution.py:139
  29.2 61.3 %copy-start.3 = (bf16[256,896]{1,0:T(8,128)(2,1)}, bf16[256,896]{1,0:T(8,128)(2,1)S(1)}, u32[]{:S(2)}) copy-start(bf16[256,896]{1,0:T(8,128)(2,1)S(1)} %collective-permute-done.7.refs_1_) | copy-start | bytes 1376260
  29.3 18.6 %collective-permute-start.9 = (bf16[256,896]{1,0:T(8,128)(2,1)S(1)}, bf16[256,896]{1,0:T(8,128)(2,1)S(1)}, u32[]{:S(2)}, u32[]{:S(2)}) collective-permute-start(bf16[256,896]{1,0:T(8,128)(2,1)S(1)} %collective-permute-done.7.refs_1_), channel_id=1, source_target_pairs={{0,64},{64,128},{128,192},{192,256},{256,320},{320,384},{384,448},... | collective-permute-start | bytes 1376264 | tf_op jit(solution)/shard_map/ppermute | solution.py:139
  31.2 59.3 %copy-start.4 = (bf16[256,896]{1,0:T(8,128)(2,1)}, bf16[256,896]{1,0:T(8,128)(2,1)S(1)}, u32[]{:S(2)}) copy-start(bf16[256,896]{1,0:T(8,128)(2,1)S(1)} %collective-permute-done.8.refs_2_) | copy-start | bytes 1376260
  31.2 18.6 %collective-permute-start.10 = (bf16[256,896]{1,0:T(8,128)(2,1)S(1)}, bf16[256,896]{1,0:T(8,128)(2,1)}, u32[]{:S(2)}, u32[]{:S(2)}) collective-permute-start(bf16[256,896]{1,0:T(8,128)(2,1)S(1)} %collective-permute-done.8.refs_2_), channel_id=1, source_target_pairs={{0,448},{64,0},{128,64},{192,128},{256,192},{320,256},{384,320},{4... | collective-permute-start | bytes 1376264 | tf_op jit(solution)/shard_map/ppermute | solution.py:140
  40.1 57.5 %copy-start.1 = (bf16[256,896]{1,0:T(8,128)(2,1)}, bf16[256,896]{1,0:T(8,128)(2,1)S(1)}, u32[]{:S(2)}) copy-start(bf16[256,896]{1,0:T(8,128)(2,1)S(1)} %collective-permute-done.1.refs_2_) | copy-start | bytes 1376260
  40.1 19.6 %collective-permute-start.3 = (bf16[256,896]{1,0:T(8,128)(2,1)S(1)}, bf16[256,896]{1,0:T(8,128)(2,1)S(1)}, u32[]{:S(2)}, u32[]{:S(2)}) collective-permute-start(bf16[256,896]{1,0:T(8,128)(2,1)S(1)} %collective-permute-done.1.refs_2_), channel_id=1, source_target_pairs={{0,448},{64,0},{128,64},{192,128},{256,192},{320,256},{384,320},{4... | collective-permute-start | bytes 1376264 | tf_op jit(solution)/shard_map/ppermute | solution.py:140
  45.3 52.2 %copy-start.2 = (bf16[256,896]{1,0:T(8,128)(2,1)}, bf16[256,896]{1,0:T(8,128)(2,1)S(1)}, u32[]{:S(2)}) copy-start(bf16[256,896]{1,0:T(8,128)(2,1)S(1)} %collective-permute-done.refs_1_) | copy-start | bytes 1376260
  45.3 19.6 %collective-permute-start.2 = (bf16[256,896]{1,0:T(8,128)(2,1)S(1)}, bf16[256,896]{1,0:T(8,128)(2,1)S(1)}, u32[]{:S(2)}, u32[]{:S(2)}) collective-permute-start(bf16[256,896]{1,0:T(8,128)(2,1)S(1)} %collective-permute-done.refs_1_), channel_id=1, source_target_pairs={{0,64},{64,128},{128,192},{192,256},{256,320},{320,384},{384,448},... | collective-permute-start | bytes 1376264 | tf_op jit(solution)/shard_map/ppermute | solution.py:139
  47.9 42.7 %copy-start.6 = (bf16[256,896]{1,0:T(8,128)(2,1)}, bf16[256,896]{1,0:T(8,128)(2,1)S(1)}, u32[]{:S(2)}) copy-start(bf16[256,896]{1,0:T(8,128)(2,1)S(1)} %collective-permute-done.9.refs_3_) | copy-start | bytes 1376260
  47.9 19.5 %collective-permute-start.11 = (bf16[256,896]{1,0:T(8,128)(2,1)S(1)}, bf16[256,896]{1,0:T(8,128)(2,1)}, u32[]{:S(2)}, u32[]{:S(2)}) collective-permute-start(bf16[256,896]{1,0:T(8,128)(2,1)S(1)} %collective-permute-done.9.refs_3_), channel_id=1, source_target_pairs={{0,64},{64,128},{128,192},{192,256},{256,320},{320,384},{384,448},... | collective-permute-start | bytes 1376264 | tf_op jit(solution)/shard_map/ppermute | solution.py:139
  49.8 24.6 %collective-permute-start.12 = (bf16[256,896]{1,0:T(8,128)(2,1)}, bf16[256,896]{1,0:T(8,128)(2,1)}, u32[]{:S(2)}, u32[]{:S(2)}) collective-permute-start(bf16[256,896]{1,0:T(8,128)(2,1)} %collective-permute-done.10.refs_4_), channel_id=1, source_target_pairs={{0,448},{64,0},{128,64},{192,128},{256,192},{320,256},{384,320},{4... | collective-permute-start | bytes 1376264 | tf_op jit(solution)/shard_map/ppermute | solution.py:140
  59.6 37.9 %copy-start.5 = (bf16[256,896]{1,0:T(8,128)(2,1)}, bf16[256,896]{1,0:T(8,128)(2,1)S(1)}, u32[]{:S(2)}) copy-start(bf16[256,896]{1,0:T(8,128)(2,1)S(1)} %collective-permute-done.3.refs_4_) | copy-start | bytes 1376260
  59.6 19.7 %collective-permute-start.5 = (bf16[256,896]{1,0:T(8,128)(2,1)S(1)}, bf16[256,896]{1,0:T(8,128)(2,1)}, u32[]{:S(2)}, u32[]{:S(2)}) collective-permute-start(bf16[256,896]{1,0:T(8,128)(2,1)S(1)} %collective-permute-done.3.refs_4_), channel_id=1, source_target_pairs={{0,448},{64,0},{128,64},{192,128},{256,192},{320,256},{384,320},{4... | collective-permute-start | bytes 1376264 | tf_op jit(solution)/shard_map/ppermute | solution.py:140
  64.9 32.6 %copy-start.7 = (bf16[256,896]{1,0:T(8,128)(2,1)}, bf16[256,896]{1,0:T(8,128)(2,1)S(1)}, u32[]{:S(2)}) copy-start(bf16[256,896]{1,0:T(8,128)(2,1)S(1)} %collective-permute-done.2.refs_3_) | copy-start | bytes 1376260
  64.9 14.3 %collective-permute-start.4 = (bf16[256,896]{1,0:T(8,128)(2,1)S(1)}, bf16[256,896]{1,0:T(8,128)(2,1)}, u32[]{:S(2)}, u32[]{:S(2)}) collective-permute-start(bf16[256,896]{1,0:T(8,128)(2,1)S(1)} %collective-permute-done.2.refs_3_), channel_id=1, source_target_pairs={{0,64},{64,128},{128,192},{192,256},{256,320},{320,384},{384,448},... | collective-permute-start | bytes 1376264 | tf_op jit(solution)/shard_map/ppermute | solution.py:139
  67.4 19.7 %collective-permute-start.13 = (bf16[256,896]{1,0:T(8,128)(2,1)}, bf16[256,896]{1,0:T(8,128)(2,1)}, u32[]{:S(2)}, u32[]{:S(2)}) collective-permute-start(bf16[256,896]{1,0:T(8,128)(2,1)} %collective-permute-done.11.refs_5_), channel_id=1, source_target_pairs={{0,64},{64,128},{128,192},{192,256},{256,320},{320,384},{384,448},... | collective-permute-start | bytes 1376264 | tf_op jit(solution)/shard_map/ppermute | solution.py:142
  87.1 10.5 %collective-permute-start.6 = (bf16[256,896]{1,0:T(8,128)(2,1)}, bf16[256,896]{1,0:T(8,128)(2,1)}, u32[]{:S(2)}, u32[]{:S(2)}) collective-permute-start(bf16[256,896]{1,0:T(8,128)(2,1)} %collective-permute-done.5.refs_6_), channel_id=1, source_target_pairs={{0,448},{64,0},{128,64},{192,128},{256,192},{320,256},{384,320},{4... | collective-permute-start | bytes 1376264 | tf_op jit(solution)/shard_map/ppermute | solution.py:142
  97.6 13.1 %all-to-all-start = ((bf16[4,128,896]{2,1,0:T(8,128)(2,1)}), bf16[4,128,896]{2,1,0:T(8,128)(2,1)S(1)}, u32[]{:S(2)}, u32[]{:S(2)}) async-start(bf16[4,128,896]{2,1,0:T(8,128)(2,1)} %bitcast.17), calls=%async_computation | async-start | bytes 1835008 | tf_op jit(solution)/shard_map/all_to_all | solution.py:163
  110.7 12.6 %all-to-all-start.1 = ((bf16[4,128,896]{2,1,0:T(8,128)(2,1)}), bf16[4,128,896]{2,1,0:T(8,128)(2,1)S(1)}, u32[]{:S(2)}, u32[]{:S(2)}) async-start(bf16[4,128,896]{2,1,0:T(8,128)(2,1)} %bitcast.16), calls=%async_computation.1 | async-start | bytes 1835008 | tf_op jit(solution)/shard_map/all_to_all | solution.py:163
  142.0 2.0 %copy-start = (bf16[896,2048]{1,0:T(8,128)(2,1)S(1)}, bf16[896,2048]{1,0:T(8,128)(2,1)}, u32[]{:S(2)}) copy-start(bf16[896,2048]{1,0:T(8,128)(2,1)} %all-gather.5.cloned.1.call-done.down) | copy-start | bytes 11010052
  145.3 9.2 %collective-permute-start.14 = (f32[256,2048]{1,0:T(8,128)S(1)}, f32[256,2048]{1,0:T(8,128)S(1)}, u32[]{:S(2)}, u32[]{:S(2)}) collective-permute-start(f32[256,2048]{1,0:T(8,128)S(1)} %second.3), channel_id=1, source_target_pairs={{0,4},{4,0},{8,12},{12,8},{16,20},{20,16},{24,28},{28,24},{32,36},... | collective-permute-start | bytes 6291464 | tf_op jit(solution)/shard_map/ppermute | solution.py:175
Sparse Core Ops, SparseCore 0:
  9.5 47.9 all-gather.2
  87.2 54.7 all-gather.4
